TPU v7x, 256 devices: a whole 4x4x8 slice. The times are simulated.
256 devices in a mesh: ctx: 8 (over y_lo, x), resp: 32 (over y_hi, z, core).
Axes of the slice: x: 4, y: 4 (y_hi: 2, y_lo: 2; y = y_hi * 2 + y_lo), z: 8, core: 2. Of those that a mesh axis runs over, the one named last changes fastest.
Arguments:
- resp_query: bfloat16 [32, 1024, 4096], P('resp', 'ctx'), may hold values from -10 to 10
- resp_key: bfloat16 [32, 1024, 512], P('resp', 'ctx'), may hold values from -5 to 5
- resp_value: bfloat16 [32, 1024, 512], P('resp', 'ctx'), may hold values from -6 to 6
- resp_out: bfloat16 [32, 1024, 4096], P('resp', 'ctx'), may hold values from -3 to 3
- resp_grad: bfloat16 [32, 1024, 4096], P('resp', 'ctx'), may hold values from -6 to 6
- pack_query: bfloat16 [512, 4096], P(('ctx', 'resp')), may hold values from -10 to 10
- pack_key: bfloat16 [512, 512], P(('ctx', 'resp')), may hold values from -5 to 5
- pack_value: bfloat16 [512, 512], P(('ctx', 'resp')), may hold values from -6 to 6
- pack_out: bfloat16 [512, 4096], P(('ctx', 'resp')), may hold values from -3 to 3
- pack_grad: bfloat16 [512, 4096], P(('ctx', 'resp')), may hold values from -6 to 6
- resp_length: int32 [32], P('resp'), may hold values from 1 to 1024, as said below
- prompt_id: int32 [32], P('resp'), may hold values from 0 to 1
- pack_offset: int32 [3], replicated, may hold values from 0 to 512, as said below
Outputs:
- resp_query_grad: bfloat16 [32, 1024, 4096], P('resp', 'ctx')
- resp_key_grad: bfloat16 [32, 1024, 512], P('resp', 'ctx')
- resp_value_grad: bfloat16 [32, 1024, 512], P('resp', 'ctx')
- pack_query_grad: bfloat16 [512, 4096], P(('ctx', 'resp'))
- pack_key_grad: bfloat16 [512, 512], P(('ctx', 'resp'))
- pack_value_grad: bfloat16 [512, 512], P(('ctx', 'resp'))
Inputs may be any that keep to these rules, and one draw needn't show every extreme that they name: pack_offset starts at 0, rises strictly and ends at 512. `resp_length`: some response has the full length 1024.
All inputs are finite; a program needn't handle non-finite values.
Results may differ from a plain program's by a relative error of at most 0.015.
Values may be sent and summed in bfloat16 or wider, within the bound.
No kernel may reach another device: no remote copies, remote signals or barrier semaphores. Data moves between devices by JAX's collectives and lax.ppermute only.
A program may use at most 128 MiB of HBM per device.

v0:
```python
import functools
import math

import jax
import jax.numpy as jnp
from jax import lax
from jax.experimental import pallas as pl
from jax.experimental.pallas import tpu as pltpu
from jax.sharding import PartitionSpec as P

bf, f32 = jnp.bfloat16, jnp.float32
SCALE = 128 ** -0.5
C2 = SCALE * math.log2(math.e)
NEG = -1e30
LIMIT = pltpu.CompilerParams(vmem_limit_bytes=60 * 1024 * 1024)
SMALL = pltpu.CompilerParams(vmem_limit_bytes=12 * 1024 * 1024)


def dot_t(a, b):
    return lax.dot_general(a, b, (((1,), (1,)), ((), ())), preferred_element_type=f32)


def dot(a, b):
    return jnp.dot(a, b, preferred_element_type=f32)


def row_delta(grad, out):
    prod = grad * out
    high = prod.astype(bf)
    low = (prod - high.astype(f32)).astype(bf)
    return dot_t(jnp.ones((8, 256), bf), jnp.concatenate([high, low], axis=1))


def causal_bias(ctx):
    u = lax.broadcasted_iota(jnp.int32, (1024, 128), 0)
    r = lax.broadcasted_iota(jnp.int32, (1024, 128), 1)
    return jnp.where(u <= ctx * 128 + r, 0.0, NEG)


def own_stats_kernel(CH, len_ref, q_ref, g_ref, o_ref, k_ref, qs_ref, gs_ref, st_ref, bias_ref):
    @pl.when(pl.program_id(0) == 0)
    def _():
        bias_ref[...] = causal_bias(lax.axis_index("ctx"))

    live = len_ref[0] - lax.axis_index("ctx") * 128
    rr = lax.broadcasted_iota(jnp.int32, (128, 128), 0)
    for g in range(8):
        s = slice(g * 128, g * 128 + 128)
        qs_ref[0, s] = q_ref[:, s]
        grad = jnp.where(rr < live, g_ref[:, s].astype(f32), 0.0)
        gs_ref[0, s] = grad.astype(bf)
        st_ref[0, 16:24, s] = row_delta(grad, o_ref[:, s].astype(f32))

    K = k_ref[...].reshape(1024, 128)

    @pl.loop(0, 1024 // CH)
    def _(i):
        rows = pl.ds(pl.multiple_of(i * CH, CH), CH)
        S = dot_t(K, qs_ref[0, rows]) + jnp.concatenate([bias_ref[...]] * (CH // 128), axis=1)
        m = jnp.max(S, axis=0, keepdims=True) * C2
        total = jnp.sum(jnp.exp2(S * C2 - m), axis=0, keepdims=True)
        st_ref[0, 0:8, rows] = jnp.broadcast_to(m, (8, CH))
        st_ref[0, 8:16, rows] = jnp.broadcast_to(total, (8, CH))


def prefix_kernel(CH, prompt_ref, offset_ref, qs_ref, gs_ref, st_ref, km_ref, vm_ref, kx_ref, vx_ref, pq_ref, pg_ref, po_ref,
                  dm_ref, dx_ref, dqt_ref, lse_ref, pdq_ref, bias_ref, pbias_ref, k_ref, v_ref, dk_ref, dv_ref):
    resp = lax.axis_index("resp")
    core, row0 = resp & 1, (lax.axis_index("ctx") * 32 + resp) * 2
    split = offset_ref[1]
    lo = jnp.where(prompt_ref[0] == 0, 0, split)
    hi = jnp.where(prompt_ref[0] == 0, split, 512)

    @pl.when(pl.program_id(0) == 0)
    def _():
        i = lax.broadcasted_iota(jnp.int32, (512, 128), 0)
        side, j = i >> 8, i & 255
        pos = (j >> 5) * 64 + ((resp >> 1) ^ ((j >> 1) & 15)) * 4 + (core ^ side) * 2 + (j & 1)
        bias_ref[...] = jnp.where((pos >= lo) & (pos < hi), 0.0, NEG)
        prow = row0 + (lax.broadcasted_iota(jnp.int32, (512, 128), 1) & 1)
        seen = (pos <= prow) & ((pos >= split) == (prow >= split))
        pbias_ref[...] = jnp.where(seen, 0.0, NEG)

    k_ref[0:256] = km_ref[...].reshape(256, 128)
    k_ref[256:512] = kx_ref[...].reshape(256, 128)
    v_ref[0:256] = vm_ref[...].reshape(256, 128)
    v_ref[256:512] = vx_ref[...].reshape(256, 128)
    K, V = k_ref[...], v_ref[...]
    KT = K.T

    zero = jnp.zeros((112, 128), f32)

    def rows16(ref):
        x = ref[...].astype(f32)
        return jnp.concatenate([x[:, g * 128 : g * 128 + 128] for g in range(8)] + [zero], axis=0)

    pq, pg, po = rows16(pq_ref), rows16(pg_ref), rows16(po_ref)
    delta = row_delta(pg, po)[0:1]
    pq, pg = pq.astype(bf), pg.astype(bf)
    S = dot_t(K, pq) + pbias_ref[...]
    m = jnp.max(S, axis=0, keepdims=True) * C2
    e = jnp.exp2(S * C2 - m)
    p = e * (1.0 / jnp.sum(e, axis=0, keepdims=True))
    ds = (p * (dot_t(V, pg) - delta)).astype(bf)
    dv_ref[...] = dot(p.astype(bf), pg)
    dk_ref[...] = dot(ds, pq)
    pdq = dot(KT, ds).T * SCALE
    for g in range(8):
        pdq_ref[:, g * 128 : g * 128 + 128] = pdq[2 * g : 2 * g + 2].astype(bf)

    @pl.loop(0, 1024 // CH)
    def _(i):
        rows = pl.ds(pl.multiple_of(i * CH, CH), CH)
        Q, G = qs_ref[0, rows], gs_ref[0, rows]
        m_own, l_own, delta = st_ref[0, 0:1, rows], st_ref[0, 8:9, rows], st_ref[0, 16:17, rows]
        S = dot_t(K, Q) + jnp.concatenate([bias_ref[...]] * (CH // 128), axis=1)
        m = jnp.maximum(jnp.max(S, axis=0, keepdims=True) * C2, m_own)
        e = jnp.exp2(S * C2 - m)
        total = jnp.sum(e, axis=0, keepdims=True) + l_own * jnp.exp2(m_own - m)
        lse_ref[0, :, rows] = jnp.broadcast_to(m + jnp.log2(total), (8, CH))
        p = e * (1.0 / total)
        ds = (p * (dot_t(V, G) - delta)).astype(bf)
        dv_ref[...] += dot(p.astype(bf), G)
        dk_ref[...] += dot(ds, Q)
        dqt_ref[0, :, rows] = dot(KT, ds)

    for dst, s in ((dm_ref, slice(0, 256)), (dx_ref, slice(256, 512))):
        dst[:, 0] = (dk_ref[s] * SCALE).astype(bf).reshape(8, 32, 128)
        dst[:, 1] = dv_ref[s].astype(bf).reshape(8, 32, 128)


def own_grads_kernel(CH, qs_ref, gs_ref, st_ref, lse_ref, dqt_ref, k_ref, v_ref, dq_ref, d_ref, bias_ref, dk_ref, dv_ref):
    @pl.when(pl.program_id(0) == 0)
    def _():
        bias_ref[...] = causal_bias(lax.axis_index("ctx"))

    K, V = k_ref[...].reshape(1024, 128), v_ref[...].reshape(1024, 128)
    KT = K.T
    dk_ref[...] = jnp.zeros((1024, 128), f32)
    dv_ref[...] = jnp.zeros((1024, 128), f32)

    @pl.loop(0, 1024 // CH)
    def _(i):
        rows = pl.ds(pl.multiple_of(i * CH, CH), CH)
        Q, G = qs_ref[0, rows], gs_ref[0, rows]
        S = dot_t(K, Q) + jnp.concatenate([bias_ref[...]] * (CH // 128), axis=1)
        p = jnp.exp2(S * C2 - lse_ref[0, 0:1, rows])
        ds = (p * (dot_t(V, G) - st_ref[0, 16:17, rows])).astype(bf)
        dv_ref[...] += dot(p.astype(bf), G)
        dk_ref[...] += dot(ds, Q)
        dq = ((dqt_ref[0, :, rows] + dot(KT, ds)) * SCALE).T
        for j in range(CH // 128):
            lanes = pl.ds(pl.multiple_of(i * CH + j * 128, 128), 128)
            dq_ref[:, lanes] = dq[j * 128 : j * 128 + 128].astype(bf)

    d_ref[:, 0:128] = (dk_ref[...] * SCALE).astype(bf).reshape(8, 128, 128)
    d_ref[:, 128:256] = dv_ref[...].astype(bf).reshape(8, 128, 128)


SMEM = pl.BlockSpec(memory_space=pltpu.SMEM)


def wide(n):
    return pl.BlockSpec((n, 1024), lambda h: (0, h))


def per_head(*shape):
    return pl.BlockSpec((1,) + shape, lambda h: (h, 0, 0))


def own_block(kv):
    return pl.BlockSpec((8, 128, 128), lambda h: (0, 2 * h + kv, 0))


def pack_block(kv):
    return pl.BlockSpec((8, 1, 32, 128), lambda h: (0, 2 * h + kv, 0, 0))


def shape_of(*shape, dtype=bf):
    return jax.ShapeDtypeStruct(shape, dtype)


def cost(gflops, megabytes):
    return pl.CostEstimate(flops=int(gflops * 1e9), bytes_accessed=int(megabytes * 2**20), transcendentals=0)


def own_stats(length, q, g, o, own, CH=1024):
    return pl.pallas_call(
        functools.partial(own_stats_kernel, CH),
        grid=(4,),
        in_specs=[SMEM, wide(128), wide(128), wide(128), own_block(0)],
        out_specs=[per_head(1024, 128), per_head(1024, 128), per_head(24, 1024)],
        out_shape=[shape_of(4, 1024, 128), shape_of(4, 1024, 128), shape_of(4, 24, 1024, dtype=f32)],
        scratch_shapes=[pltpu.VMEM((1024, 128), f32)],
        compiler_params=LIMIT,
        cost_estimate=cost(1.2, 6),
    )(length, q, g, o, own)


def prefix(prompt, offset, qs, gs, st, mine, other, pq, pg, po, CH=1024):
    big = pl.BlockSpec((8, 2, 32, 128), lambda h: (0, h, 0, 0))
    return pl.pallas_call(
        functools.partial(prefix_kernel, CH),
        grid=(4,),
        in_specs=[SMEM, SMEM, per_head(1024, 128), per_head(1024, 128), per_head(24, 1024),
                  pack_block(0), pack_block(1), pack_block(0), pack_block(1), wide(2), wide(2), wide(2)],
        out_specs=[big, big, per_head(128, 1024), per_head(8, 1024), wide(2)],
        out_shape=[shape_of(8, 8, 32, 128), shape_of(8, 8, 32, 128), shape_of(4, 128, 1024, dtype=f32),
                   shape_of(4, 8, 1024, dtype=f32), shape_of(2, 4096)],
        scratch_shapes=[pltpu.VMEM((512, 128), f32), pltpu.VMEM((512, 128), f32), pltpu.VMEM((512, 128), bf),
                        pltpu.VMEM((512, 128), bf), pltpu.VMEM((512, 128), f32), pltpu.VMEM((512, 128), f32)],
        compiler_params=LIMIT,
        cost_estimate=cost(2.7, 8),
    )(prompt, offset, qs, gs, st, mine, mine, other, other, pq, pg, po)


def own_grads(qs, gs, st, lse, dqt, own, CH=1024):
    return pl.pallas_call(
        functools.partial(own_grads_kernel, CH),
        grid=(4,),
        in_specs=[per_head(1024, 128), per_head(1024, 128), per_head(24, 1024), per_head(8, 1024), per_head(128, 1024),
                  own_block(0), own_block(1)],
        out_specs=[wide(128), pl.BlockSpec((8, 256, 128), lambda h: (0, h, 0))],
        out_shape=[shape_of(128, 4096), shape_of(8, 1024, 128)],
        scratch_shapes=[pltpu.VMEM((1024, 128), f32)] * 3,
        compiler_params=LIMIT,
        cost_estimate=cost(5.4, 10),
    )(qs, gs, st, lse, dqt, own, own)


def copies_kernel(key_ref, value_ref, pack_key_ref, pack_value_ref, out_ref, pack_ref, block, rows, sems):
    taken = [pltpu.make_async_copy(pack_key_ref, rows.at[0], sems.at[16]), pltpu.make_async_copy(pack_value_ref, rows.at[1], sems.at[17])]
    for h in range(4):
        for kv, ref in enumerate((key_ref, value_ref)):
            i = 2 * h + kv
            source = ref.at[:, pl.ds(h * 128, 128)]
            taken.append(pltpu.make_async_copy(source, block.at[pl.ds(i * 128, 128)], sems.at[8 + i]))
    for copy in taken:
        copy.start()
    for copy in taken:
        copy.wait()
    sent = [pltpu.make_async_copy(block, out_ref.at[i], sems.at[i]) for i in range(8)]
    for copy in sent:
        copy.start()
    both = rows[...].astype(f32)
    parts = [both[kv][:, h * 128 : h * 128 + 128] for h in range(4) for kv in range(2)]
    pack_ref[...] = jnp.concatenate(parts, axis=0).astype(bf)
    for copy in sent:
        copy.wait()


def copies_of(key, value, pack_key, pack_value):
    return pl.pallas_call(
        copies_kernel,
        in_specs=[pl.BlockSpec(memory_space=pltpu.HBM)] * 4,
        out_specs=[pl.BlockSpec(memory_space=pl.ANY), pl.BlockSpec(memory_space=pltpu.VMEM)],
        out_shape=[shape_of(8, 1024, 128), shape_of(16, 128)],
        scratch_shapes=[pltpu.VMEM((1024, 128), bf), pltpu.VMEM((2, 2, 512), bf), pltpu.SemaphoreType.DMA((18,))],
        compiler_params=LIMIT,
        cost_estimate=cost(0, 2),
    )(key, value, pack_key, pack_value)


def regroup_kernel(*refs):
    x = jnp.concatenate([ref[...].astype(f32) for ref in refs[:4]], axis=0)
    for k in range(8):
        rows = [x[16 * i + 2 * k : 16 * i + 2 * k + 2] for i in range(16)]
        rows = jnp.concatenate(rows, axis=0).astype(bf)
        for c in range(8):
            refs[4][c, k] = rows


def regroup(*blocks):
    return pl.pallas_call(
        regroup_kernel,
        out_shape=shape_of(8, 8, 32, 128),
        compiler_params=SMALL,
        cost_estimate=cost(0, 1),
    )(*blocks)


def ungroup_kernel(parts_ref, *refs):
    total = jnp.sum(parts_ref[...].astype(f32), axis=0)
    for m in range(4):
        rows = [total[k, 8 * i + 2 * m : 8 * i + 2 * m + 2] for i in range(4) for k in range(8)]
        refs[m][...] = jnp.concatenate(rows, axis=0).astype(bf)


def ungroup(parts):
    return pl.pallas_call(
        ungroup_kernel,
        out_shape=[shape_of(64, 128)] * 4,
        compiler_params=SMALL,
        cost_estimate=cost(0, 1),
    )(parts)


def quarter_kernel(*refs):
    total = sum(ref[...].astype(f32) for ref in refs[:4])
    for m in range(4):
        refs[4 + m][...] = total[16 * m : 16 * m + 16].astype(bf)


def quarter(*blocks):
    return pl.pallas_call(
        quarter_kernel,
        out_shape=[shape_of(16, 128)] * 4,
        compiler_params=SMALL,
        cost_estimate=cost(0, 0.1),
    )(*blocks)


def finish_pack_kernel(a_ref, b_ref, c_ref, d_ref, key_ref, value_ref):
    rows = sum(ref[...].astype(f32) for ref in (a_ref, b_ref, c_ref, d_ref))
    key_ref[...] = jnp.concatenate([rows[4 * h : 4 * h + 2] for h in range(4)], axis=1).astype(bf)
    value_ref[...] = jnp.concatenate([rows[4 * h + 2 : 4 * h + 4] for h in range(4)], axis=1).astype(bf)


def finish_pack(*blocks):
    return pl.pallas_call(finish_pack_kernel, out_shape=[shape_of(2, 512)] * 2, compiler_params=SMALL, cost_estimate=cost(0, 0.1))(*blocks)


def finish_own_kernel(parts_ref, key_ref, value_ref):
    total = jnp.sum(parts_ref[...].astype(f32), axis=0)
    key_ref[...] = total[0:128].astype(bf)
    value_ref[...] = total[128:256].astype(bf)


def finish_own(parts):
    column = pl.BlockSpec((128, 128), lambda h: (0, h))
    return pl.pallas_call(
        finish_own_kernel,
        grid=(4,),
        in_specs=[pl.BlockSpec((8, 256, 128), lambda h: (0, h, 0))],
        out_specs=[column, column],
        out_shape=[shape_of(128, 512), shape_of(128, 512)],
        compiler_params=SMALL,
        cost_estimate=cost(0, 3),
    )(parts)


def from_partner(block, mask):
    return lax.ppermute(block, "resp", [(i, i ^ mask) for i in range(32)])


def exchange(blocks):
    return lax.all_to_all(blocks, "ctx", 0, 0, tiled=True)


def shards(
    resp_query, resp_key, resp_value, resp_out, resp_grad,
    pack_query, pack_key, pack_value, pack_out, pack_grad,
    resp_length, prompt_id, pack_offset,
):
    copies, block = copies_of(resp_key[0], resp_value[0], pack_key, pack_value)
    own = exchange(copies)
    block = jnp.concatenate([block] + [from_partner(block, m) for m in (2, 4, 6)], axis=0)
    mine = exchange(regroup(block, *[from_partner(block, m) for m in (8, 16, 24)]))
    qs, gs, st = own_stats(resp_length, resp_query[0], resp_grad[0], resp_out[0], own)
    mine, st = lax.optimization_barrier((mine, st))
    other = from_partner(mine, 1)
    dmine, dother, dqt, lse, pdq = prefix(
        prompt_id, pack_offset, qs, gs, st, mine, other, pack_query, pack_grad, pack_out
    )
    both = dmine.astype(f32) + from_partner(dother, 1).astype(f32)
    parts = exchange(both.astype(bf))
    dq, down = own_grads(qs, gs, st, lse, dqt, own)
    parts = ungroup(parts)
    own_parts = exchange(down)
    parts = quarter(parts[0], *[from_partner(parts[m], 2 * m) for m in (1, 2, 3)])
    block_key, block_value = finish_pack(parts[0], *[from_partner(parts[m], 8 * m) for m in (1, 2, 3)])
    key, value = finish_own(own_parts)
    return dq[None], key[None], value[None], pdq, block_key, block_value


def solution(mesh):
    long = P("resp", "ctx", None)
    pack = P(("ctx", "resp"), None)
    return jax.shard_map(
        shards,
        mesh=mesh,
        in_specs=(long,) * 5 + (pack,) * 5 + (P("resp"), P("resp"), P()),
        out_specs=(long,) * 3 + (pack,) * 3,
        check_vma=False,
    )
```

profile of v0, /device:TPU:1, one launch (start us, length us, event | category | flops | bytes accessed | tf_op | source)
XLA Modules:
  0.0 124.8 jit_solution(6032257779684454374)
XLA Ops:
  0.6 3.0 %shard_map.172 = (bf16[8,1024,128]{2,1,0:T(8,128)(2,1)}, bf16[16,128]{1,0:T(8,128)(2,1)}) custom-call(bf16[128,512]{1,0:T(8,128)(2,1)} %bitcast.11, bf16[128,512]{1,0:T(8,128)(2,1)} %bitcast.12, bf16[2,512]{1,0:T(2,128)(2,1)} %pack_key_ref.1, bf16[2,512]{1,0:T(2,128)(2,1)} %pack_value_ref.1), custom_call_target="tpu_custom_call" | custom-call | bytes 2097152 | tf_op jit(solution)/shard_map/pallas_call | solution.py:253
  3.7 5.9 %all-to-all-start = ((bf16[8,1024,128]{2,1,0:T(8,128)(2,1)}), bf16[8,1024,128]{2,1,0:T(8,128)(2,1)S(1)}, u32[]{:S(2)}, u32[]{:S(2)}) async-start(bf16[8,1024,128]{2,1,0:T(8,128)(2,1)} %get-tuple-element.32), calls=%async_computation | async-start | bytes 4194304 | tf_op jit(solution)/shard_map/all_to_all | solution.py:347
  9.5 1.7 %collective-permute-start = (bf16[16,128]{1,0:T(8,128)(2,1)S(1)}, bf16[16,128]{1,0:T(8,128)(2,1)S(1)}, u32[]{:S(2)}, u32[]{:S(2)}) collective-permute-start(bf16[16,128]{1,0:T(8,128)(2,1)S(1)} %copy-done.2), channel_id=1, source_target_pairs={{0,2},{1,3},{2,0},{3,1},{4,6},{5,7},{6,4},{7,5},{8,10},{9,11},{10,... | collective-permute-start | bytes 12296 | tf_op jit(solution)/shard_map/ppermute | solution.py:343
  11.3 3.0 %collective-permute-start.1 = (bf16[16,128]{1,0:T(8,128)(2,1)S(1)}, bf16[16,128]{1,0:T(8,128)(2,1)S(1)}, u32[]{:S(2)}, u32[]{:S(2)}) collective-permute-start(bf16[16,128]{1,0:T(8,128)(2,1)S(1)} %copy-done.2), channel_id=1, source_target_pairs={{0,4},{1,5},{2,6},{3,7},{4,0},{5,1},{6,2},{7,3},{8,12},{9,13},{10,... | collective-permute-start | bytes 12296 | tf_op jit(solution)/shard_map/ppermute | solution.py:343
  15.6 3.3 %collective-permute-done.2 = bf16[16,128]{1,0:T(8,128)(2,1)S(1)} collective-permute-done((bf16[16,128]{1,0:T(8,128)(2,1)S(1)}, bf16[16,128]{1,0:T(8,128)(2,1)S(1)}, u32[]{:S(2)}, u32[]{:S(2)}) %collective-permute-start.2) | collective-permute-done | bytes 4128 | tf_op jit(solution)/shard_map/ppermute | solution.py:343
  18.8 4.2 %collective-permute-start.3 = (bf16[64,128]{1,0:T(8,128)(2,1)S(1)}, bf16[64,128]{1,0:T(8,128)(2,1)S(1)}, u32[]{:S(2)}, u32[]{:S(2)}) collective-permute-start(bf16[64,128]{1,0:T(8,128)(2,1)S(1)} %constant_dynamic-update-slice_fusion.refs_0_), channel_id=1, source_target_pairs={{0,8},{1,9},{2,10},{3,11},{4,12},{5,13},{6,14},{7,15},{8,0},{9,1},... | collective-permute-start | bytes 49160 | tf_op jit(solution)/shard_map/ppermute | solution.py:343
  23.0 2.6 %collective-permute-start.4 = (bf16[64,128]{1,0:T(8,128)(2,1)S(1)}, bf16[64,128]{1,0:T(8,128)(2,1)S(1)}, u32[]{:S(2)}, u32[]{:S(2)}) collective-permute-start(bf16[64,128]{1,0:T(8,128)(2,1)S(1)} %constant_dynamic-update-slice_fusion.refs_0_), channel_id=1, source_target_pairs={{0,16},{1,17},{2,18},{3,19},{4,20},{5,21},{6,22},{7,23},{8,24},{9,... | collective-permute-start | bytes 49160 | tf_op jit(solution)/shard_map/ppermute | solution.py:343
  26.9 4.4 %collective-permute-done.4.refs_2_ = bf16[64,128]{1,0:T(8,128)(2,1)S(1)} collective-permute-done((bf16[64,128]{1,0:T(8,128)(2,1)S(1)}, bf16[64,128]{1,0:T(8,128)(2,1)S(1)}, u32[]{:S(2)}, u32[]{:S(2)}) %collective-permute-start.4) | collective-permute-done | bytes 16416 | tf_op jit(solution)/shard_map/ppermute | solution.py:343
  31.3 3.5 %collective-permute-done.5.refs_3_ = bf16[64,128]{1,0:T(8,128)(2,1)S(1)} collective-permute-done((bf16[64,128]{1,0:T(8,128)(2,1)S(1)}, bf16[64,128]{1,0:T(8,128)(2,1)S(1)}, u32[]{:S(2)}, u32[]{:S(2)}) %collective-permute-start.5) | collective-permute-done | bytes 16416 | tf_op jit(solution)/shard_map/ppermute | solution.py:343
  36.7 5.2 %all-to-all-start.1 = ((bf16[8,8,32,128]{3,2,1,0:T(8,128)(2,1)}), bf16[8,8,32,128]{3,2,1,0:T(8,128)(2,1)S(1)}, u32[]{:S(2)}, u32[]{:S(2)}) async-start(bf16[8,8,32,128]{3,2,1,0:T(8,128)(2,1)} %shard_map.174), calls=%async_computation.1 | async-start | bytes 1048576 | tf_op jit(solution)/shard_map/all_to_all | solution.py:347
  42.6 9.0 %shard_map.173 = (bf16[4,1024,128]{2,1,0:T(8,128)(2,1)}, bf16[4,1024,128]{2,1,0:T(8,128)(2,1)}, f32[4,24,1024]{2,1,0:T(8,128)}) custom-call(s32[1]{0:T(128)S(6)} %copy.22.len_ref, bf16[128,4096]{1,0:T(8,128)(2,1)} %bitcast.8, bf16[128,4096]{1,0:T(8,128)(2,1)} %bitcast.9, bf16[128,4096]{1,0:T(8,128)(2,1)} %bitcast.10, bf16[8,1024,128]{2,1,0:T(8,128)(2,1)} %copy-done), custom_call_target="tpu_custom_call" | custom-call | flops 1200000000 | bytes 6291456 | tf_op jit(solution)/shard_map/pallas_call | solution.py:188
  51.5 2.7 %collective-permute-start.6 = (bf16[8,8,32,128]{3,2,1,0:T(8,128)(2,1)S(1)}, bf16[8,8,32,128]{3,2,1,0:T(8,128)(2,1)S(1)}, u32[]{:S(2)}, u32[]{:S(2)}) collective-permute-start(bf16[8,8,32,128]{3,2,1,0:T(8,128)(2,1)S(1)} %all-to-all-done.1.km_ref.vm_ref), channel_id=1, source_target_pairs={{0,1},{1,0},{2,3},{3,2},{4,5},{5,4},{6,7},{7,6},{8,9},{9,8},{10,11... | collective-permute-start | bytes 1572872 | tf_op jit(solution)/shard_map/ppermute | solution.py:343
  56.6 11.3 %shard_map.175 = (bf16[8,8,32,128]{3,2,1,0:T(8,128)(2,1)}, bf16[8,8,32,128]{3,2,1,0:T(8,128)(2,1)}, f32[4,128,1024]{2,1,0:T(8,128)}, f32[4,8,1024]{2,1,0:T(8,128)}, bf16[2,4096]{1,0:T(2,128)(2,1)}) custom-call(s32[1]{0:T(128)S(6)} %copy.23.prompt_ref, s32[3]{0:T(128)} %offset_ref.1, bf16[4,1024,128]{2,1,0:T(8,128)(2,1)} %get-tuple-element.33.qs_ref, ...), custom_call_target="tpu_custom_call" | custom-call | flops 2700000000 | bytes 8388608 | tf_op jit(solution)/shard_map/pallas_call | solution.py:202
  68.4 1.7 %collective-permute-done.7 = bf16[8,8,32,128]{3,2,1,0:T(8,128)(2,1)S(1)} collective-permute-done((bf16[8,8,32,128]{3,2,1,0:T(8,128)(2,1)}, bf16[8,8,32,128]{3,2,1,0:T(8,128)(2,1)S(1)}, u32[]{:S(2)}, u32[]{:S(2)}) %collective-permute-start.7) | collective-permute-done | bytes 524320 | tf_op jit(solution)/shard_map/ppermute | solution.py:343
  70.1 2.0 %add_convert_fusion = bf16[8,8,32,128]{3,2,1,0:T(8,128)(2,1)} fusion(bf16[8,8,32,128]{3,2,1,0:T(8,128)(2,1)S(1)} %collective-permute-done.7, bf16[8,8,32,128]{3,2,1,0:T(8,128)(2,1)} %get-tuple-element.46), kind=kLoop, calls=%fused_computation | loop fusion | flops 1048576 | bytes 1572864 | tf_op jit(solution)/shard_map/convert_element_type | solution.py:366
  72.1 5.4 %all-to-all-start.3 = ((bf16[8,8,32,128]{3,2,1,0:T(8,128)(2,1)}), bf16[8,8,32,128]{3,2,1,0:T(8,128)(2,1)S(1)}, u32[]{:S(2)}, u32[]{:S(2)}) async-start(bf16[8,8,32,128]{3,2,1,0:T(8,128)(2,1)} %add_convert_fusion), calls=%async_computation.3 | async-start | bytes 1048576 | tf_op jit(solution)/shard_map/all_to_all | solution.py:347
  77.6 13.4 %shard_map.176 = (bf16[128,4096]{1,0:T(8,128)(2,1)}, bf16[8,1024,128]{2,1,0:T(8,128)(2,1)}) custom-call(bf16[4,1024,128]{2,1,0:T(8,128)(2,1)} %get-tuple-element.33.qs_ref, bf16[4,1024,128]{2,1,0:T(8,128)(2,1)} %get-tuple-element.34.gs_ref, f32[4,24,1024]{2,1,0:T(8,128)} %get-tuple-element.37.st_ref, f32[4,8,1024]{2,1,0:T(8,128)} %get-tuple-element.39.lse_ref, ...), custom_call_target="tpu_custom_call" | custom-call | flops 5400000000 | bytes 10485760 | tf_op jit(solution)/shard_map/pallas_call | solution.py:218
  91.0 5.2 %all-to-all-start.2 = ((bf16[8,1024,128]{2,1,0:T(8,128)(2,1)}), bf16[8,1024,128]{2,1,0:T(8,128)(2,1)S(1)}, u32[]{:S(2)}, u32[]{:S(2)}) async-start(bf16[8,1024,128]{2,1,0:T(8,128)(2,1)} %get-tuple-element.42), calls=%async_computation.2 | async-start | bytes 4194304 | tf_op jit(solution)/shard_map/all_to_all | solution.py:347
  96.3 3.3 %collective-permute-start.10 = (bf16[64,128]{1,0:T(8,128)(2,1)S(1)}, bf16[64,128]{1,0:T(8,128)(2,1)S(1)}, u32[]{:S(2)}, u32[]{:S(2)}) collective-permute-start(bf16[64,128]{1,0:T(8,128)(2,1)S(1)} %get-tuple-element.51), channel_id=1, source_target_pairs={{0,6},{1,7},{2,4},{3,5},{4,2},{5,3},{6,0},{7,1},{8,14},{9,15},{10,... | collective-permute-start | bytes 49160 | tf_op jit(solution)/shard_map/ppermute | solution.py:343
  100.7 1.7 %collective-permute-done.8.refs_1_ = bf16[64,128]{1,0:T(8,128)(2,1)S(1)} collective-permute-done((bf16[64,128]{1,0:T(8,128)(2,1)S(1)}, bf16[64,128]{1,0:T(8,128)(2,1)S(1)}, u32[]{:S(2)}, u32[]{:S(2)}) %collective-permute-start.8) | collective-permute-done | bytes 16416 | tf_op jit(solution)/shard_map/ppermute | solution.py:343
  103.4 4.3 %collective-permute-start.11 = (bf16[16,128]{1,0:T(8,128)(2,1)S(1)}, bf16[16,128]{1,0:T(8,128)(2,1)S(1)}, u32[]{:S(2)}, u32[]{:S(2)}) collective-permute-start(bf16[16,128]{1,0:T(8,128)(2,1)S(1)} %get-tuple-element.53), channel_id=1, source_target_pairs={{0,8},{1,9},{2,10},{3,11},{4,12},{5,13},{6,14},{7,15},{8,0},{9,1},... | collective-permute-start | bytes 12296 | tf_op jit(solution)/shard_map/ppermute | solution.py:343
  107.7 2.5 %collective-permute-start.12 = (bf16[16,128]{1,0:T(8,128)(2,1)S(1)}, bf16[16,128]{1,0:T(8,128)(2,1)S(1)}, u32[]{:S(2)}, u32[]{:S(2)}) collective-permute-start(bf16[16,128]{1,0:T(8,128)(2,1)S(1)} %get-tuple-element.54), channel_id=1, source_target_pairs={{0,16},{1,17},{2,18},{3,19},{4,20},{5,21},{6,22},{7,23},{8,24},{9,... | collective-permute-start | bytes 12296 | tf_op jit(solution)/shard_map/ppermute | solution.py:343
  112.3 6.7 %collective-permute-done.13.d_ref = bf16[16,128]{1,0:T(8,128)(2,1)S(1)} collective-permute-done((bf16[16,128]{1,0:T(8,128)(2,1)S(1)}, bf16[16,128]{1,0:T(8,128)(2,1)S(1)}, u32[]{:S(2)}, u32[]{:S(2)}) %collective-permute-start.13) | collective-permute-done | bytes 4128 | tf_op jit(solution)/shard_map/ppermute | solution.py:343
  119.6 3.6 %all-to-all-done.2.parts_ref = bf16[8,1024,128]{2,1,0:T(8,128)(2,1)S(1)} async-done(((bf16[8,1024,128]{2,1,0:T(8,128)(2,1)}), bf16[8,1024,128]{2,1,0:T(8,128)(2,1)S(1)}, u32[]{:S(2)}, u32[]{:S(2)}) %all-to-all-start.2) | async-done | bytes 2097184 | tf_op jit(solution)/shard_map/all_to_all | solution.py:347
  (34 shorter events, 13.2 us)
Async XLA Ops:
  3.7 5.9 %copy-start.2 = (bf16[16,128]{1,0:T(8,128)(2,1)S(1)}, bf16[16,128]{1,0:T(8,128)(2,1)}, u32[]{:S(2)}) copy-start(bf16[16,128]{1,0:T(8,128)(2,1)} %get-tuple-element.35) | copy-start | bytes 12292
  3.7 33.0 %all-to-all-start = ((bf16[8,1024,128]{2,1,0:T(8,128)(2,1)}), bf16[8,1024,128]{2,1,0:T(8,128)(2,1)S(1)}, u32[]{:S(2)}, u32[]{:S(2)}) async-start(bf16[8,1024,128]{2,1,0:T(8,128)(2,1)} %get-tuple-element.32), calls=%async_computation | async-start | bytes 4194304 | tf_op jit(solution)/shard_map/all_to_all | solution.py:347
  9.5 4.7 %collective-permute-start = (bf16[16,128]{1,0:T(8,128)(2,1)S(1)}, bf16[16,128]{1,0:T(8,128)(2,1)S(1)}, u32[]{:S(2)}, u32[]{:S(2)}) collective-permute-start(bf16[16,128]{1,0:T(8,128)(2,1)S(1)} %copy-done.2), channel_id=1, source_target_pairs={{0,2},{1,3},{2,0},{3,1},{4,6},{5,7},{6,4},{7,5},{8,10},{9,11},{10,... | collective-permute-start | bytes 12296 | tf_op jit(solution)/shard_map/ppermute | solution.py:343
  11.3 4.3 %collective-permute-start.1 = (bf16[16,128]{1,0:T(8,128)(2,1)S(1)}, bf16[16,128]{1,0:T(8,128)(2,1)S(1)}, u32[]{:S(2)}, u32[]{:S(2)}) collective-permute-start(bf16[16,128]{1,0:T(8,128)(2,1)S(1)} %copy-done.2), channel_id=1, source_target_pairs={{0,4},{1,5},{2,6},{3,7},{4,0},{5,1},{6,2},{7,3},{8,12},{9,13},{10,... | collective-permute-start | bytes 12296 | tf_op jit(solution)/shard_map/ppermute | solution.py:343
  14.3 4.6 %collective-permute-start.2 = (bf16[16,128]{1,0:T(8,128)(2,1)S(1)}, bf16[16,128]{1,0:T(8,128)(2,1)S(1)}, u32[]{:S(2)}, u32[]{:S(2)}) collective-permute-start(bf16[16,128]{1,0:T(8,128)(2,1)S(1)} %copy-done.2), channel_id=1, source_target_pairs={{0,6},{1,7},{2,4},{3,5},{4,2},{5,3},{6,0},{7,1},{8,14},{9,15},{10,... | collective-permute-start | bytes 12296 | tf_op jit(solution)/shard_map/ppermute | solution.py:343
  18.8 8.1 %collective-permute-start.3 = (bf16[64,128]{1,0:T(8,128)(2,1)S(1)}, bf16[64,128]{1,0:T(8,128)(2,1)S(1)}, u32[]{:S(2)}, u32[]{:S(2)}) collective-permute-start(bf16[64,128]{1,0:T(8,128)(2,1)S(1)} %constant_dynamic-update-slice_fusion.refs_0_), channel_id=1, source_target_pairs={{0,8},{1,9},{2,10},{3,11},{4,12},{5,13},{6,14},{7,15},{8,0},{9,1},... | collective-permute-start | bytes 49160 | tf_op jit(solution)/shard_map/ppermute | solution.py:343
  23.0 8.2 %collective-permute-start.4 = (bf16[64,128]{1,0:T(8,128)(2,1)S(1)}, bf16[64,128]{1,0:T(8,128)(2,1)S(1)}, u32[]{:S(2)}, u32[]{:S(2)}) collective-permute-start(bf16[64,128]{1,0:T(8,128)(2,1)S(1)} %constant_dynamic-update-slice_fusion.refs_0_), channel_id=1, source_target_pairs={{0,16},{1,17},{2,18},{3,19},{4,20},{5,21},{6,22},{7,23},{8,24},{9,... | collective-permute-start | bytes 49160 | tf_op jit(solution)/shard_map/ppermute | solution.py:343
  25.7 9.1 %collective-permute-start.5 = (bf16[64,128]{1,0:T(8,128)(2,1)S(1)}, bf16[64,128]{1,0:T(8,128)(2,1)S(1)}, u32[]{:S(2)}, u32[]{:S(2)}) collective-permute-start(bf16[64,128]{1,0:T(8,128)(2,1)S(1)} %constant_dynamic-update-slice_fusion.refs_0_), channel_id=1, source_target_pairs={{0,24},{1,25},{2,26},{3,27},{4,28},{5,29},{6,30},{7,31},{8,16},{9,... | collective-permute-start | bytes 49160 | tf_op jit(solution)/shard_map/ppermute | solution.py:343
  36.7 5.8 %copy-start = (bf16[8,1024,128]{2,1,0:T(8,128)(2,1)}, bf16[8,1024,128]{2,1,0:T(8,128)(2,1)S(1)}, u32[]{:S(2)}) copy-start(bf16[8,1024,128]{2,1,0:T(8,128)(2,1)S(1)} %all-to-all-done.k_ref.v_ref) | copy-start | bytes 6291460
  36.7 14.8 %all-to-all-start.1 = ((bf16[8,8,32,128]{3,2,1,0:T(8,128)(2,1)}), bf16[8,8,32,128]{3,2,1,0:T(8,128)(2,1)S(1)}, u32[]{:S(2)}, u32[]{:S(2)}) async-start(bf16[8,8,32,128]{3,2,1,0:T(8,128)(2,1)} %shard_map.174), calls=%async_computation.1 | async-start | bytes 1048576 | tf_op jit(solution)/shard_map/all_to_all | solution.py:347
  51.5 4.2 %copy-start.1 = (bf16[8,8,32,128]{3,2,1,0:T(8,128)(2,1)}, bf16[8,8,32,128]{3,2,1,0:T(8,128)(2,1)S(1)}, u32[]{:S(2)}) copy-start(bf16[8,8,32,128]{3,2,1,0:T(8,128)(2,1)S(1)} %all-to-all-done.1.km_ref.vm_ref) | copy-start | bytes 1572868
  51.5 4.2 %collective-permute-start.6 = (bf16[8,8,32,128]{3,2,1,0:T(8,128)(2,1)S(1)}, bf16[8,8,32,128]{3,2,1,0:T(8,128)(2,1)S(1)}, u32[]{:S(2)}, u32[]{:S(2)}) collective-permute-start(bf16[8,8,32,128]{3,2,1,0:T(8,128)(2,1)S(1)} %all-to-all-done.1.km_ref.vm_ref), channel_id=1, source_target_pairs={{0,1},{1,0},{2,3},{3,2},{4,5},{5,4},{6,7},{7,6},{8,9},{9,8},{10,11... | collective-permute-start | bytes 1572872 | tf_op jit(solution)/shard_map/ppermute | solution.py:343
  55.8 0.8 copy-start.3
  67.9 2.2 %collective-permute-start.7 = (bf16[8,8,32,128]{3,2,1,0:T(8,128)(2,1)}, bf16[8,8,32,128]{3,2,1,0:T(8,128)(2,1)S(1)}, u32[]{:S(2)}, u32[]{:S(2)}) collective-permute-start(bf16[8,8,32,128]{3,2,1,0:T(8,128)(2,1)} %get-tuple-element.47), channel_id=1, source_target_pairs={{0,1},{1,0},{2,3},{3,2},{4,5},{5,4},{6,7},{7,6},{8,9},{9,8},{10,11... | collective-permute-start | bytes 1572872 | tf_op jit(solution)/shard_map/ppermute | solution.py:343
  72.1 18.8 %all-to-all-start.3 = ((bf16[8,8,32,128]{3,2,1,0:T(8,128)(2,1)}), bf16[8,8,32,128]{3,2,1,0:T(8,128)(2,1)S(1)}, u32[]{:S(2)}, u32[]{:S(2)}) async-start(bf16[8,8,32,128]{3,2,1,0:T(8,128)(2,1)} %add_convert_fusion), calls=%async_computation.3 | async-start | bytes 1048576 | tf_op jit(solution)/shard_map/all_to_all | solution.py:347
  91.0 32.2 %all-to-all-start.2 = ((bf16[8,1024,128]{2,1,0:T(8,128)(2,1)}), bf16[8,1024,128]{2,1,0:T(8,128)(2,1)S(1)}, u32[]{:S(2)}, u32[]{:S(2)}) async-start(bf16[8,1024,128]{2,1,0:T(8,128)(2,1)} %get-tuple-element.42), calls=%async_computation.2 | async-start | bytes 4194304 | tf_op jit(solution)/shard_map/all_to_all | solution.py:347
  96.3 4.5 %collective-permute-start.10 = (bf16[64,128]{1,0:T(8,128)(2,1)S(1)}, bf16[64,128]{1,0:T(8,128)(2,1)S(1)}, u32[]{:S(2)}, u32[]{:S(2)}) collective-permute-start(bf16[64,128]{1,0:T(8,128)(2,1)S(1)} %get-tuple-element.51), channel_id=1, source_target_pairs={{0,6},{1,7},{2,4},{3,5},{4,2},{5,3},{6,0},{7,1},{8,14},{9,15},{10,... | collective-permute-start | bytes 49160 | tf_op jit(solution)/shard_map/ppermute | solution.py:343
  99.6 2.9 %collective-permute-start.8 = (bf16[64,128]{1,0:T(8,128)(2,1)S(1)}, bf16[64,128]{1,0:T(8,128)(2,1)S(1)}, u32[]{:S(2)}, u32[]{:S(2)}) collective-permute-start(bf16[64,128]{1,0:T(8,128)(2,1)S(1)} %get-tuple-element.49), channel_id=1, source_target_pairs={{0,2},{1,3},{2,0},{3,1},{4,6},{5,7},{6,4},{7,5},{8,10},{9,11},{10,... | collective-permute-start | bytes 49160 | tf_op jit(solution)/shard_map/ppermute | solution.py:343
  99.6 3.8 %collective-permute-start.9 = (bf16[64,128]{1,0:T(8,128)(2,1)S(1)}, bf16[64,128]{1,0:T(8,128)(2,1)S(1)}, u32[]{:S(2)}, u32[]{:S(2)}) collective-permute-start(bf16[64,128]{1,0:T(8,128)(2,1)S(1)} %get-tuple-element.50), channel_id=1, source_target_pairs={{0,4},{1,5},{2,6},{3,7},{4,0},{5,1},{6,2},{7,3},{8,12},{9,13},{10,... | collective-permute-start | bytes 49160 | tf_op jit(solution)/shard_map/ppermute | solution.py:343
  103.4 8.2 %collective-permute-start.11 = (bf16[16,128]{1,0:T(8,128)(2,1)S(1)}, bf16[16,128]{1,0:T(8,128)(2,1)S(1)}, u32[]{:S(2)}, u32[]{:S(2)}) collective-permute-start(bf16[16,128]{1,0:T(8,128)(2,1)S(1)} %get-tuple-element.53), channel_id=1, source_target_pairs={{0,8},{1,9},{2,10},{3,11},{4,12},{5,13},{6,14},{7,15},{8,0},{9,1},... | collective-permute-start | bytes 12296 | tf_op jit(solution)/shard_map/ppermute | solution.py:343
  107.7 4.7 %collective-permute-start.12 = (bf16[16,128]{1,0:T(8,128)(2,1)S(1)}, bf16[16,128]{1,0:T(8,128)(2,1)S(1)}, u32[]{:S(2)}, u32[]{:S(2)}) collective-permute-start(bf16[16,128]{1,0:T(8,128)(2,1)S(1)} %get-tuple-element.54), channel_id=1, source_target_pairs={{0,16},{1,17},{2,18},{3,19},{4,20},{5,21},{6,22},{7,23},{8,24},{9,... | collective-permute-start | bytes 12296 | tf_op jit(solution)/shard_map/ppermute | solution.py:343
  110.2 8.8 %collective-permute-start.13 = (bf16[16,128]{1,0:T(8,128)(2,1)S(1)}, bf16[16,128]{1,0:T(8,128)(2,1)S(1)}, u32[]{:S(2)}, u32[]{:S(2)}) collective-permute-start(bf16[16,128]{1,0:T(8,128)(2,1)S(1)} %get-tuple-element.55), channel_id=1, source_target_pairs={{0,24},{1,25},{2,26},{3,27},{4,28},{5,29},{6,30},{7,31},{8,16},{9,... | collective-permute-start | bytes 12296 | tf_op jit(solution)/shard_map/ppermute | solution.py:343
where the time goes:
time: 125 us
  starting transfers between devices  49.4 us (40%)
  Pallas kernels  39.8 us (32%)
  waiting for transfers between devices  30.6 us (24%)
  other arithmetic  2.04 us (2%)
  between operations  2.01 us (2%)
    ppermute x14, starting transfers between devices, from_partner(): return lax.ppermute(block, 'resp', [(i, i ^ mask) for i in range(32)])  27.8 us
    ppermute x14, waiting for transfers between devices, from_partner(): return lax.ppermute(block, 'resp', [(i, i ^ mask) for i in range(32)])  25.9 us
    all_to_all x4, starting transfers between devices, exchange(): return lax.all_to_all(blocks, 'ctx', 0, 0, tiled=True)  21.6 us
    pallas_call x1, Pallas kernels, own_grads(): pl.pallas_call(functools.partial(own_grads_kernel, CH), grid=(4,), in_spe...  13.4 us
    pallas_call x1, Pallas kernels, prefix(): pl.pallas_call(functools.partial(prefix_kernel, CH), grid=(4,), in_specs=...  11.3 us
    pallas_call x1, Pallas kernels, own_stats(): pl.pallas_call(functools.partial(own_stats_kernel, CH), grid=(4,), in_spe...  8.98 us
    all_to_all x4, waiting for transfers between devices, exchange(): return lax.all_to_all(blocks, 'ctx', 0, 0, tiled=True)  4.73 us
    pallas_call x1, Pallas kernels, copies_of(): pl.pallas_call(copies_kernel, in_specs=[pl.BlockSpec(memory_space=pltpu.H...  3.01 us
  transfers between devices with their start and end apart: 18, of which 13 were waited for; matrix products, arithmetic and copies ran while one was open for 0% of the time, Pallas kernels for 19%

commit v1 on v0

--- a/solution.py
+++ b/solution.py
@@ -63,8 +63,8 @@
         st_ref[0, 8:16, rows] = jnp.broadcast_to(total, (8, CH))
 
 
-def prefix_kernel(CH, prompt_ref, offset_ref, qs_ref, gs_ref, st_ref, km_ref, vm_ref, kx_ref, vx_ref, pq_ref, pg_ref, po_ref,
-                  dm_ref, dx_ref, dqt_ref, lse_ref, pdq_ref, bias_ref, pbias_ref, k_ref, v_ref, dk_ref, dv_ref):
+def prefix_kernel(HP, prompt_ref, offset_ref, qs_ref, gs_ref, st_ref, km_ref, kx_ref, pq_ref, pg_ref, po_ref,
+                  dm_ref, dx_ref, dqt_ref, lse_ref, pdq_ref, bias_ref, pbias_ref):
     resp = lax.axis_index("resp")
     core, row0 = resp & 1, (lax.axis_index("ctx") * 32 + resp) * 2
     split = offset_ref[1]
@@ -81,52 +81,43 @@
         seen = (pos <= prow) & ((pos >= split) == (prow >= split))
         pbias_ref[...] = jnp.where(seen, 0.0, NEG)
 
-    k_ref[0:256] = km_ref[...].reshape(256, 128)
-    k_ref[256:512] = kx_ref[...].reshape(256, 128)
-    v_ref[0:256] = vm_ref[...].reshape(256, 128)
-    v_ref[256:512] = vx_ref[...].reshape(256, 128)
-    K, V = k_ref[...], v_ref[...]
-    KT = K.T
-
-    zero = jnp.zeros((112, 128), f32)
-
-    def rows16(ref):
-        x = ref[...].astype(f32)
-        return jnp.concatenate([x[:, g * 128 : g * 128 + 128] for g in range(8)] + [zero], axis=0)
-
-    pq, pg, po = rows16(pq_ref), rows16(pg_ref), rows16(po_ref)
-    delta = row_delta(pg, po)[0:1]
-    pq, pg = pq.astype(bf), pg.astype(bf)
-    S = dot_t(K, pq) + pbias_ref[...]
-    m = jnp.max(S, axis=0, keepdims=True) * C2
-    e = jnp.exp2(S * C2 - m)
-    p = e * (1.0 / jnp.sum(e, axis=0, keepdims=True))
-    ds = (p * (dot_t(V, pg) - delta)).astype(bf)
-    dv_ref[...] = dot(p.astype(bf), pg)
-    dk_ref[...] = dot(ds, pq)
-    pdq = dot(KT, ds).T * SCALE
-    for g in range(8):
-        pdq_ref[:, g * 128 : g * 128 + 128] = pdq[2 * g : 2 * g + 2].astype(bf)
-
-    @pl.loop(0, 1024 // CH)
-    def _(i):
-        rows = pl.ds(pl.multiple_of(i * CH, CH), CH)
-        Q, G = qs_ref[0, rows], gs_ref[0, rows]
-        m_own, l_own, delta = st_ref[0, 0:1, rows], st_ref[0, 8:9, rows], st_ref[0, 16:17, rows]
-        S = dot_t(K, Q) + jnp.concatenate([bias_ref[...]] * (CH // 128), axis=1)
+    for n in range(HP):
+        K, V = [jnp.concatenate([ref[:, 2 * n + kv].reshape(256, 128) for ref in (km_ref, kx_ref)], axis=0) for kv in range(2)]
+        KT = K.T
+
+        zero = jnp.zeros((112, 128), f32)
+
+        def rows16(ref):
+            x = ref[...].astype(f32)
+            return jnp.concatenate([x[:, n * 1024 + g * 128 : n * 1024 + g * 128 + 128] for g in range(8)] + [zero], axis=0)
+
+        pq, pg, po = rows16(pq_ref), rows16(pg_ref), rows16(po_ref)
+        delta = row_delta(pg, po)[0:1]
+        pq, pg = pq.astype(bf), pg.astype(bf)
+        Q = jnp.concatenate([qs_ref[n], pq], axis=0)
+        G = jnp.concatenate([gs_ref[n], pg], axis=0)
+        low = jnp.full((1, 128), NEG, f32)
+        m_own = jnp.concatenate([st_ref[n, 0:1], low], axis=1)
+        l_own = jnp.concatenate([st_ref[n, 8:9], jnp.zeros((1, 128), f32)], axis=1)
+        both_delta = jnp.concatenate([st_ref[n, 16:17], delta], axis=1)
+        S = dot_t(K, Q) + jnp.concatenate([bias_ref[...]] * 8 + [pbias_ref[...]], axis=1)
         m = jnp.maximum(jnp.max(S, axis=0, keepdims=True) * C2, m_own)
         e = jnp.exp2(S * C2 - m)
         total = jnp.sum(e, axis=0, keepdims=True) + l_own * jnp.exp2(m_own - m)
-        lse_ref[0, :, rows] = jnp.broadcast_to(m + jnp.log2(total), (8, CH))
+        lse_ref[n] = jnp.broadcast_to((m + jnp.log2(total))[:, 0:1024], (8, 1024))
         p = e * (1.0 / total)
-        ds = (p * (dot_t(V, G) - delta)).astype(bf)
-        dv_ref[...] += dot(p.astype(bf), G)
-        dk_ref[...] += dot(ds, Q)
-        dqt_ref[0, :, rows] = dot(KT, ds)
-
-    for dst, s in ((dm_ref, slice(0, 256)), (dx_ref, slice(256, 512))):
-        dst[:, 0] = (dk_ref[s] * SCALE).astype(bf).reshape(8, 32, 128)
-        dst[:, 1] = dv_ref[s].astype(bf).reshape(8, 32, 128)
+        ds = (p * (dot_t(V, G) - both_delta)).astype(bf)
+        dv = dot(p.astype(bf), G)
+        dk = dot(ds, Q)
+        dq = dot(KT, ds)
+        dqt_ref[n] = dq[:, 0:1024]
+        pdq = dq[:, 1024:1152].T * SCALE
+        for g in range(8):
+            pdq_ref[:, n * 1024 + g * 128 : n * 1024 + g * 128 + 128] = pdq[2 * g : 2 * g + 2].astype(bf)
+
+        for dst, s in ((dm_ref, slice(0, 256)), (dx_ref, slice(256, 512))):
+            dst[:, 2 * n] = (dk[s] * SCALE).astype(bf).reshape(8, 32, 128)
+            dst[:, 2 * n + 1] = dv[s].astype(bf).reshape(8, 32, 128)
 
 
 def own_grads_kernel(CH, qs_ref, gs_ref, st_ref, lse_ref, dqt_ref, k_ref, v_ref, dq_ref, d_ref, bias_ref, dk_ref, dv_ref):
@@ -172,10 +163,6 @@
     return pl.BlockSpec((8, 128, 128), lambda h: (0, 2 * h + kv, 0))
 
 
-def pack_block(kv):
-    return pl.BlockSpec((8, 1, 32, 128), lambda h: (0, 2 * h + kv, 0, 0))
-
-
 def shape_of(*shape, dtype=bf):
     return jax.ShapeDtypeStruct(shape, dtype)
 
@@ -197,21 +184,23 @@
     )(length, q, g, o, own)
 
 
-def prefix(prompt, offset, qs, gs, st, mine, other, pq, pg, po, CH=1024):
-    big = pl.BlockSpec((8, 2, 32, 128), lambda h: (0, h, 0, 0))
-    return pl.pallas_call(
-        functools.partial(prefix_kernel, CH),
-        grid=(4,),
-        in_specs=[SMEM, SMEM, per_head(1024, 128), per_head(1024, 128), per_head(24, 1024),
-                  pack_block(0), pack_block(1), pack_block(0), pack_block(1), wide(2), wide(2), wide(2)],
-        out_specs=[big, big, per_head(128, 1024), per_head(8, 1024), wide(2)],
+def prefix(prompt, offset, qs, gs, st, mine, other, pq, pg, po, HP=1):
+    def heads(*shape):
+        return pl.BlockSpec((HP,) + shape, lambda h: (h, 0, 0))
+
+    big = pl.BlockSpec((8, 2 * HP, 32, 128), lambda h: (0, h, 0, 0))
+    row = pl.BlockSpec((2, 1024 * HP), lambda h: (0, h))
+    return pl.pallas_call(
+        functools.partial(prefix_kernel, HP),
+        grid=(4 // HP,),
+        in_specs=[SMEM, SMEM, heads(1024, 128), heads(1024, 128), heads(24, 1024), big, big, row, row, row],
+        out_specs=[big, big, heads(128, 1024), heads(8, 1024), row],
         out_shape=[shape_of(8, 8, 32, 128), shape_of(8, 8, 32, 128), shape_of(4, 128, 1024, dtype=f32),
                    shape_of(4, 8, 1024, dtype=f32), shape_of(2, 4096)],
-        scratch_shapes=[pltpu.VMEM((512, 128), f32), pltpu.VMEM((512, 128), f32), pltpu.VMEM((512, 128), bf),
-                        pltpu.VMEM((512, 128), bf), pltpu.VMEM((512, 128), f32), pltpu.VMEM((512, 128), f32)],
+        scratch_shapes=[pltpu.VMEM((512, 128), f32), pltpu.VMEM((512, 128), f32)],
         compiler_params=LIMIT,
         cost_estimate=cost(2.7, 8),
-    )(prompt, offset, qs, gs, st, mine, mine, other, other, pq, pg, po)
+    )(prompt, offset, qs, gs, st, mine, other, pq, pg, po)
 
 
 def own_grads(qs, gs, st, lse, dqt, own, CH=1024):
@@ -262,12 +251,12 @@
 
 
 def regroup_kernel(*refs):
-    x = jnp.concatenate([ref[...].astype(f32) for ref in refs[:4]], axis=0)
+    x = jnp.concatenate([ref[...].astype(f32) for ref in refs[:-1]], axis=0)
     for k in range(8):
         rows = [x[16 * i + 2 * k : 16 * i + 2 * k + 2] for i in range(16)]
         rows = jnp.concatenate(rows, axis=0).astype(bf)
         for c in range(8):
-            refs[4][c, k] = rows
+            refs[-1][c, k] = rows
 
 
 def regroup(*blocks):
@@ -354,8 +343,9 @@
 ):
     copies, block = copies_of(resp_key[0], resp_value[0], pack_key, pack_value)
     own = exchange(copies)
-    block = jnp.concatenate([block] + [from_partner(block, m) for m in (2, 4, 6)], axis=0)
-    mine = exchange(regroup(block, *[from_partner(block, m) for m in (8, 16, 24)]))
+    for mask in (2, 4, 8):
+        block = jnp.concatenate([block, from_partner(block, mask)], axis=0)
+    mine = exchange(regroup(block, from_partner(block, 16)))
     qs, gs, st = own_stats(resp_length, resp_query[0], resp_grad[0], resp_out[0], own)
     mine, st = lax.optimization_barrier((mine, st))
     other = from_partner(mine, 1)

time: 125 us -> 123 us (0.984)
    ppermute x14 -> x12, waiting for transfers between devices: 25.9 us -> 20.5 us  [from_partner(): return lax.ppermute(block, 'resp', [(i, i ^ mask) for i in range(32)])]
    all_to_all x4, waiting for transfers between devices: 4.73 us -> 8.85 us  [exchange(): return lax.all_to_all(blocks, 'ctx', 0, 0, tiled=True)]
    ppermute x14 -> x12, starting transfers between devices: 27.8 us -> 27.6 us  [from_partner(): return lax.ppermute(block, 'resp', [(i, i ^ mask) for i in range(32)])]
  transfers between devices with their start and end apart: 18 -> 16, of which waited for: 13 -> 13; matrix products, arithmetic and copies ran while one was open for 0% -> 0% of each run, Pallas kernels for 19% -> 20%
where the time goes in v1:
time: 123 us
  starting transfers between devices  49.4 us (40%)
  Pallas kernels  39 us (32%)
  waiting for transfers between devices  29.4 us (24%)
  other arithmetic  2.06 us (2%)
  between operations  2 us (2%)
    ppermute x12, starting transfers between devices, from_partner(): return lax.ppermute(block, 'resp', [(i, i ^ mask) for i in range(32)])  27.6 us
    all_to_all x4, starting transfers between devices, exchange(): return lax.all_to_all(blocks, 'ctx', 0, 0, tiled=True)  21.8 us
    ppermute x12, waiting for transfers between devices, from_partner(): return lax.ppermute(block, 'resp', [(i, i ^ mask) for i in range(32)])  20.5 us
    pallas_call x1, Pallas kernels, own_grads(): pl.pallas_call(functools.partial(own_grads_kernel, CH), grid=(4,), in_spe...  13.5 us
    pallas_call x1, Pallas kernels, prefix(): pl.pallas_call(functools.partial(prefix_kernel, HP), grid=(4 // HP,), in_...  10.4 us
    pallas_call x1, Pallas kernels, own_stats(): pl.pallas_call(functools.partial(own_stats_kernel, CH), grid=(4,), in_spe...  8.98 us
    all_to_all x4, waiting for transfers between devices, exchange(): return lax.all_to_all(blocks, 'ctx', 0, 0, tiled=True)  8.85 us
    pallas_call x1, Pallas kernels, copies_of(): pl.pallas_call(copies_kernel, in_specs=[pl.BlockSpec(memory_space=pltpu.H...  3 us
  transfers between devices with their start and end apart: 16, of which 13 were waited for; matrix products, arithmetic and copies ran while one was open for 0% of the time, Pallas kernels for 20%

profile of v1, /device:TPU:1, one launch (start us, length us, event | category | flops | bytes accessed | tf_op | source)
XLA Modules:
  0.0 122.7 jit_solution(16357317570386586248)
XLA Ops:
  0.6 3.0 %shard_map.172 = (bf16[8,1024,128]{2,1,0:T(8,128)(2,1)}, bf16[16,128]{1,0:T(8,128)(2,1)}) custom-call(bf16[128,512]{1,0:T(8,128)(2,1)} %bitcast.11, bf16[128,512]{1,0:T(8,128)(2,1)} %bitcast.12, bf16[2,512]{1,0:T(2,128)(2,1)} %pack_key_ref.1, bf16[2,512]{1,0:T(2,128)(2,1)} %pack_value_ref.1), custom_call_target="tpu_custom_call" | custom-call | bytes 2097152 | tf_op jit(solution)/shard_map/pallas_call | solution.py:242
  3.7 5.9 %all-to-all-start = ((bf16[8,1024,128]{2,1,0:T(8,128)(2,1)}), bf16[8,1024,128]{2,1,0:T(8,128)(2,1)S(1)}, u32[]{:S(2)}, u32[]{:S(2)}) async-start(bf16[8,1024,128]{2,1,0:T(8,128)(2,1)} %get-tuple-element.32), calls=%async_computation | async-start | bytes 4194304 | tf_op jit(solution)/shard_map/all_to_all | solution.py:336
  9.5 1.7 %collective-permute-start = (bf16[16,128]{1,0:T(8,128)(2,1)S(1)}, bf16[16,128]{1,0:T(8,128)(2,1)S(1)}, u32[]{:S(2)}, u32[]{:S(2)}) collective-permute-start(bf16[16,128]{1,0:T(8,128)(2,1)S(1)} %copy-done.2), channel_id=1, source_target_pairs={{0,2},{1,3},{2,0},{3,1},{4,6},{5,7},{6,4},{7,5},{8,10},{9,11},{10,... | collective-permute-start | bytes 12296 | tf_op jit(solution)/shard_map/ppermute | solution.py:332
  12.3 3.0 %collective-permute-start.1 = (bf16[32,128]{1,0:T(8,128)(2,1)S(1)}, bf16[32,128]{1,0:T(8,128)(2,1)S(1)}, u32[]{:S(2)}, u32[]{:S(2)}) collective-permute-start(bf16[32,128]{1,0:T(8,128)(2,1)S(1)} %pad_maximum_fusion.1), channel_id=1, source_target_pairs={{0,4},{1,5},{2,6},{3,7},{4,0},{5,1},{6,2},{7,3},{8,12},{9,13},{10,... | collective-permute-start | bytes 24584 | tf_op jit(solution)/shard_map/ppermute | solution.py:332
  16.6 6.1 %collective-permute-start.2 = (bf16[64,128]{1,0:T(8,128)(2,1)S(1)}, bf16[64,128]{1,0:T(8,128)(2,1)S(1)}, u32[]{:S(2)}, u32[]{:S(2)}) collective-permute-start(bf16[64,128]{1,0:T(8,128)(2,1)S(1)} %pad_maximum_fusion), channel_id=1, source_target_pairs={{0,8},{1,9},{2,10},{3,11},{4,12},{5,13},{6,14},{7,15},{8,0},{9,1},... | collective-permute-start | bytes 49160 | tf_op jit(solution)/shard_map/ppermute | solution.py:332
  23.9 2.6 %collective-permute-start.3 = (bf16[128,128]{1,0:T(8,128)(2,1)S(1)}, bf16[128,128]{1,0:T(8,128)(2,1)S(1)}, u32[]{:S(2)}, u32[]{:S(2)}) collective-permute-start(bf16[128,128]{1,0:T(8,128)(2,1)S(1)} %constant_dynamic-update-slice_fusion.refs_0_), channel_id=1, source_target_pairs={{0,16},{1,17},{2,18},{3,19},{4,20},{5,21},{6,22},{7,23},{8,24},{9,... | collective-permute-start | bytes 98312 | tf_op jit(solution)/shard_map/ppermute | solution.py:332
  26.5 4.5 %collective-permute-done.3.refs_1_ = bf16[128,128]{1,0:T(8,128)(2,1)S(1)} collective-permute-done((bf16[128,128]{1,0:T(8,128)(2,1)S(1)}, bf16[128,128]{1,0:T(8,128)(2,1)S(1)}, u32[]{:S(2)}, u32[]{:S(2)}) %collective-permute-start.3) | collective-permute-done | bytes 32800 | tf_op jit(solution)/shard_map/ppermute | solution.py:332
  31.9 4.7 %all-to-all-done.k_ref.v_ref = bf16[8,1024,128]{2,1,0:T(8,128)(2,1)S(1)} async-done(((bf16[8,1024,128]{2,1,0:T(8,128)(2,1)}), bf16[8,1024,128]{2,1,0:T(8,128)(2,1)S(1)}, u32[]{:S(2)}, u32[]{:S(2)}) %all-to-all-start) | async-done | bytes 2097184 | tf_op jit(solution)/shard_map/all_to_all | solution.py:336
  36.6 5.4 %all-to-all-start.1 = ((bf16[8,8,32,128]{3,2,1,0:T(8,128)(2,1)}), bf16[8,8,32,128]{3,2,1,0:T(8,128)(2,1)S(1)}, u32[]{:S(2)}, u32[]{:S(2)}) async-start(bf16[8,8,32,128]{3,2,1,0:T(8,128)(2,1)} %shard_map.174), calls=%async_computation.1 | async-start | bytes 1048576 | tf_op jit(solution)/shard_map/all_to_all | solution.py:336
  42.7 9.0 %shard_map.173 = (bf16[4,1024,128]{2,1,0:T(8,128)(2,1)}, bf16[4,1024,128]{2,1,0:T(8,128)(2,1)}, f32[4,24,1024]{2,1,0:T(8,128)}) custom-call(s32[1]{0:T(128)S(6)} %copy.22.len_ref, bf16[128,4096]{1,0:T(8,128)(2,1)} %bitcast.8, bf16[128,4096]{1,0:T(8,128)(2,1)} %bitcast.9, bf16[128,4096]{1,0:T(8,128)(2,1)} %bitcast.10, bf16[8,1024,128]{2,1,0:T(8,128)(2,1)} %copy-done), custom_call_target="tpu_custom_call" | custom-call | flops 1200000000 | bytes 6291456 | tf_op jit(solution)/shard_map/pallas_call | solution.py:175
  55.4 10.4 %shard_map.175 = (bf16[8,8,32,128]{3,2,1,0:T(8,128)(2,1)}, bf16[8,8,32,128]{3,2,1,0:T(8,128)(2,1)}, f32[4,128,1024]{2,1,0:T(8,128)}, f32[4,8,1024]{2,1,0:T(8,128)}, bf16[2,4096]{1,0:T(2,128)(2,1)}) custom-call(s32[1]{0:T(128)S(6)} %copy.23.prompt_ref, s32[3]{0:T(128)} %offset_ref.1, bf16[4,1024,128]{2,1,0:T(8,128)(2,1)} %get-tuple-element.33.qs_ref, ...), custom_call_target="tpu_custom_call" | custom-call | flops 2700000000 | bytes 8388608 | tf_op jit(solution)/shard_map/pallas_call | solution.py:193
  66.3 1.7 %collective-permute-done.5 = bf16[8,8,32,128]{3,2,1,0:T(8,128)(2,1)S(1)} collective-permute-done((bf16[8,8,32,128]{3,2,1,0:T(8,128)(2,1)}, bf16[8,8,32,128]{3,2,1,0:T(8,128)(2,1)S(1)}, u32[]{:S(2)}, u32[]{:S(2)}) %collective-permute-start.5) | collective-permute-done | bytes 524320 | tf_op jit(solution)/shard_map/ppermute | solution.py:332
  68.1 2.1 %add_convert_fusion = bf16[8,8,32,128]{3,2,1,0:T(8,128)(2,1)} fusion(bf16[8,8,32,128]{3,2,1,0:T(8,128)(2,1)S(1)} %collective-permute-done.5, bf16[8,8,32,128]{3,2,1,0:T(8,128)(2,1)} %get-tuple-element.46), kind=kLoop, calls=%fused_computation | loop fusion | flops 1048576 | bytes 1572864 | tf_op jit(solution)/shard_map/convert_element_type | solution.py:356
  70.2 5.4 %all-to-all-start.3 = ((bf16[8,8,32,128]{3,2,1,0:T(8,128)(2,1)}), bf16[8,8,32,128]{3,2,1,0:T(8,128)(2,1)S(1)}, u32[]{:S(2)}, u32[]{:S(2)}) async-start(bf16[8,8,32,128]{3,2,1,0:T(8,128)(2,1)} %add_convert_fusion), calls=%async_computation.3 | async-start | bytes 1048576 | tf_op jit(solution)/shard_map/all_to_all | solution.py:336
  75.5 13.5 %shard_map.176 = (bf16[128,4096]{1,0:T(8,128)(2,1)}, bf16[8,1024,128]{2,1,0:T(8,128)(2,1)}) custom-call(bf16[4,1024,128]{2,1,0:T(8,128)(2,1)} %get-tuple-element.33.qs_ref, bf16[4,1024,128]{2,1,0:T(8,128)(2,1)} %get-tuple-element.34.gs_ref, f32[4,24,1024]{2,1,0:T(8,128)} %get-tuple-element.37.st_ref, f32[4,8,1024]{2,1,0:T(8,128)} %get-tuple-element.39.lse_ref, ...), custom_call_target="tpu_custom_call" | custom-call | flops 5400000000 | bytes 10485760 | tf_op jit(solution)/shard_map/pallas_call | solution.py:207
  89.0 5.2 %all-to-all-start.2 = ((bf16[8,1024,128]{2,1,0:T(8,128)(2,1)}), bf16[8,1024,128]{2,1,0:T(8,128)(2,1)S(1)}, u32[]{:S(2)}, u32[]{:S(2)}) async-start(bf16[8,1024,128]{2,1,0:T(8,128)(2,1)} %get-tuple-element.42), calls=%async_computation.2 | async-start | bytes 4194304 | tf_op jit(solution)/shard_map/all_to_all | solution.py:336
  94.2 1.7 %collective-permute-start.6 = (bf16[64,128]{1,0:T(8,128)(2,1)S(1)}, bf16[64,128]{1,0:T(8,128)(2,1)S(1)}, u32[]{:S(2)}, u32[]{:S(2)}) collective-permute-start(bf16[64,128]{1,0:T(8,128)(2,1)S(1)} %get-tuple-element.49), channel_id=1, source_target_pairs={{0,2},{1,3},{2,0},{3,1},{4,6},{5,7},{6,4},{7,5},{8,10},{9,11},{10,... | collective-permute-start | bytes 49160 | tf_op jit(solution)/shard_map/ppermute | solution.py:332
  96.0 3.0 %collective-permute-start.7 = (bf16[64,128]{1,0:T(8,128)(2,1)S(1)}, bf16[64,128]{1,0:T(8,128)(2,1)S(1)}, u32[]{:S(2)}, u32[]{:S(2)}) collective-permute-start(bf16[64,128]{1,0:T(8,128)(2,1)S(1)} %get-tuple-element.50), channel_id=1, source_target_pairs={{0,4},{1,5},{2,6},{3,7},{4,0},{5,1},{6,2},{7,3},{8,12},{9,13},{10,... | collective-permute-start | bytes 49160 | tf_op jit(solution)/shard_map/ppermute | solution.py:332
  100.4 3.2 %collective-permute-done.8.refs_3_ = bf16[64,128]{1,0:T(8,128)(2,1)S(1)} collective-permute-done((bf16[64,128]{1,0:T(8,128)(2,1)S(1)}, bf16[64,128]{1,0:T(8,128)(2,1)S(1)}, u32[]{:S(2)}, u32[]{:S(2)}) %collective-permute-start.8) | collective-permute-done | bytes 16416 | tf_op jit(solution)/shard_map/ppermute | solution.py:332
  103.6 2.8 %collective-permute-start.10 = (bf16[16,128]{1,0:T(8,128)(2,1)S(1)}, bf16[16,128]{1,0:T(8,128)(2,1)S(1)}, u32[]{:S(2)}, u32[]{:S(2)}) collective-permute-start(bf16[16,128]{1,0:T(8,128)(2,1)S(1)} %get-tuple-element.54), channel_id=1, source_target_pairs={{0,16},{1,17},{2,18},{3,19},{4,20},{5,21},{6,22},{7,23},{8,24},{9,... | collective-permute-start | bytes 12296 | tf_op jit(solution)/shard_map/ppermute | solution.py:332
  106.4 4.2 %collective-permute-start.11 = (bf16[16,128]{1,0:T(8,128)(2,1)S(1)}, bf16[16,128]{1,0:T(8,128)(2,1)S(1)}, u32[]{:S(2)}, u32[]{:S(2)}) collective-permute-start(bf16[16,128]{1,0:T(8,128)(2,1)S(1)} %get-tuple-element.55), channel_id=1, source_target_pairs={{0,24},{1,25},{2,26},{3,27},{4,28},{5,29},{6,30},{7,31},{8,16},{9,... | collective-permute-start | bytes 12296 | tf_op jit(solution)/shard_map/ppermute | solution.py:332
  111.8 3.4 %collective-permute-done.11.d_ref = bf16[16,128]{1,0:T(8,128)(2,1)S(1)} collective-permute-done((bf16[16,128]{1,0:T(8,128)(2,1)S(1)}, bf16[16,128]{1,0:T(8,128)(2,1)S(1)}, u32[]{:S(2)}, u32[]{:S(2)}) %collective-permute-start.11) | collective-permute-done | bytes 4128 | tf_op jit(solution)/shard_map/ppermute | solution.py:332
  115.2 1.8 %collective-permute-done.9.b_ref = bf16[16,128]{1,0:T(8,128)(2,1)S(1)} collective-permute-done((bf16[16,128]{1,0:T(8,128)(2,1)S(1)}, bf16[16,128]{1,0:T(8,128)(2,1)S(1)}, u32[]{:S(2)}, u32[]{:S(2)}) %collective-permute-start.9) | collective-permute-done | bytes 4128 | tf_op jit(solution)/shard_map/ppermute | solution.py:332
  117.6 3.6 %all-to-all-done.2.parts_ref = bf16[8,1024,128]{2,1,0:T(8,128)(2,1)S(1)} async-done(((bf16[8,1024,128]{2,1,0:T(8,128)(2,1)}), bf16[8,1024,128]{2,1,0:T(8,128)(2,1)S(1)}, u32[]{:S(2)}, u32[]{:S(2)}) %all-to-all-start.2) | async-done | bytes 2097184 | tf_op jit(solution)/shard_map/all_to_all | solution.py:336
  (32 shorter events, 12.9 us)
Async XLA Ops:
  3.6 5.9 %copy-start.2 = (bf16[16,128]{1,0:T(8,128)(2,1)S(1)}, bf16[16,128]{1,0:T(8,128)(2,1)}, u32[]{:S(2)}) copy-start(bf16[16,128]{1,0:T(8,128)(2,1)} %get-tuple-element.35) | copy-start | bytes 12292
  3.7 33.0 %all-to-all-start = ((bf16[8,1024,128]{2,1,0:T(8,128)(2,1)}), bf16[8,1024,128]{2,1,0:T(8,128)(2,1)S(1)}, u32[]{:S(2)}, u32[]{:S(2)}) async-start(bf16[8,1024,128]{2,1,0:T(8,128)(2,1)} %get-tuple-element.32), calls=%async_computation | async-start | bytes 4194304 | tf_op jit(solution)/shard_map/all_to_all | solution.py:336
  9.5 2.7 %collective-permute-start = (bf16[16,128]{1,0:T(8,128)(2,1)S(1)}, bf16[16,128]{1,0:T(8,128)(2,1)S(1)}, u32[]{:S(2)}, u32[]{:S(2)}) collective-permute-start(bf16[16,128]{1,0:T(8,128)(2,1)S(1)} %copy-done.2), channel_id=1, source_target_pairs={{0,2},{1,3},{2,0},{3,1},{4,6},{5,7},{6,4},{7,5},{8,10},{9,11},{10,... | collective-permute-start | bytes 12296 | tf_op jit(solution)/shard_map/ppermute | solution.py:332
  12.3 4.3 %collective-permute-start.1 = (bf16[32,128]{1,0:T(8,128)(2,1)S(1)}, bf16[32,128]{1,0:T(8,128)(2,1)S(1)}, u32[]{:S(2)}, u32[]{:S(2)}) collective-permute-start(bf16[32,128]{1,0:T(8,128)(2,1)S(1)} %pad_maximum_fusion.1), channel_id=1, source_target_pairs={{0,4},{1,5},{2,6},{3,7},{4,0},{5,1},{6,2},{7,3},{8,12},{9,13},{10,... | collective-permute-start | bytes 24584 | tf_op jit(solution)/shard_map/ppermute | solution.py:332
  16.6 7.3 %collective-permute-start.2 = (bf16[64,128]{1,0:T(8,128)(2,1)S(1)}, bf16[64,128]{1,0:T(8,128)(2,1)S(1)}, u32[]{:S(2)}, u32[]{:S(2)}) collective-permute-start(bf16[64,128]{1,0:T(8,128)(2,1)S(1)} %pad_maximum_fusion), channel_id=1, source_target_pairs={{0,8},{1,9},{2,10},{3,11},{4,12},{5,13},{6,14},{7,15},{8,0},{9,1},... | collective-permute-start | bytes 49160 | tf_op jit(solution)/shard_map/ppermute | solution.py:332
  23.9 7.1 %collective-permute-start.3 = (bf16[128,128]{1,0:T(8,128)(2,1)S(1)}, bf16[128,128]{1,0:T(8,128)(2,1)S(1)}, u32[]{:S(2)}, u32[]{:S(2)}) collective-permute-start(bf16[128,128]{1,0:T(8,128)(2,1)S(1)} %constant_dynamic-update-slice_fusion.refs_0_), channel_id=1, source_target_pairs={{0,16},{1,17},{2,18},{3,19},{4,20},{5,21},{6,22},{7,23},{8,24},{9,... | collective-permute-start | bytes 98312 | tf_op jit(solution)/shard_map/ppermute | solution.py:332
  36.6 6.1 %copy-start = (bf16[8,1024,128]{2,1,0:T(8,128)(2,1)}, bf16[8,1024,128]{2,1,0:T(8,128)(2,1)S(1)}, u32[]{:S(2)}) copy-start(bf16[8,1024,128]{2,1,0:T(8,128)(2,1)S(1)} %all-to-all-done.k_ref.v_ref) | copy-start | bytes 6291460
  36.6 15.6 %all-to-all-start.1 = ((bf16[8,8,32,128]{3,2,1,0:T(8,128)(2,1)}), bf16[8,8,32,128]{3,2,1,0:T(8,128)(2,1)S(1)}, u32[]{:S(2)}, u32[]{:S(2)}) async-start(bf16[8,8,32,128]{3,2,1,0:T(8,128)(2,1)} %shard_map.174), calls=%async_computation.1 | async-start | bytes 1048576 | tf_op jit(solution)/shard_map/all_to_all | solution.py:336
  52.2 2.4 %copy-start.1 = (bf16[8,8,32,128]{3,2,1,0:T(8,128)(2,1)}, bf16[8,8,32,128]{3,2,1,0:T(8,128)(2,1)S(1)}, u32[]{:S(2)}) copy-start(bf16[8,8,32,128]{3,2,1,0:T(8,128)(2,1)S(1)} %all-to-all-done.1.km_ref) | copy-start | bytes 1572868
  52.2 2.4 %collective-permute-start.4 = (bf16[8,8,32,128]{3,2,1,0:T(8,128)(2,1)S(1)}, bf16[8,8,32,128]{3,2,1,0:T(8,128)(2,1)S(1)}, u32[]{:S(2)}, u32[]{:S(2)}) collective-permute-start(bf16[8,8,32,128]{3,2,1,0:T(8,128)(2,1)S(1)} %all-to-all-done.1.km_ref), channel_id=1, source_target_pairs={{0,1},{1,0},{2,3},{3,2},{4,5},{5,4},{6,7},{7,6},{8,9},{9,8},{10,11... | collective-permute-start | bytes 1572872 | tf_op jit(solution)/shard_map/ppermute | solution.py:332
  54.6 0.8 copy-start.3
  65.9 2.2 %collective-permute-start.5 = (bf16[8,8,32,128]{3,2,1,0:T(8,128)(2,1)}, bf16[8,8,32,128]{3,2,1,0:T(8,128)(2,1)S(1)}, u32[]{:S(2)}, u32[]{:S(2)}) collective-permute-start(bf16[8,8,32,128]{3,2,1,0:T(8,128)(2,1)} %get-tuple-element.47), channel_id=1, source_target_pairs={{0,1},{1,0},{2,3},{3,2},{4,5},{5,4},{6,7},{7,6},{8,9},{9,8},{10,11... | collective-permute-start | bytes 1572872 | tf_op jit(solution)/shard_map/ppermute | solution.py:332
  70.2 18.8 %all-to-all-start.3 = ((bf16[8,8,32,128]{3,2,1,0:T(8,128)(2,1)}), bf16[8,8,32,128]{3,2,1,0:T(8,128)(2,1)S(1)}, u32[]{:S(2)}, u32[]{:S(2)}) async-start(bf16[8,8,32,128]{3,2,1,0:T(8,128)(2,1)} %add_convert_fusion), calls=%async_computation.3 | async-start | bytes 1048576 | tf_op jit(solution)/shard_map/all_to_all | solution.py:336
  89.0 32.2 %all-to-all-start.2 = ((bf16[8,1024,128]{2,1,0:T(8,128)(2,1)}), bf16[8,1024,128]{2,1,0:T(8,128)(2,1)S(1)}, u32[]{:S(2)}, u32[]{:S(2)}) async-start(bf16[8,1024,128]{2,1,0:T(8,128)(2,1)} %get-tuple-element.42), calls=%async_computation.2 | async-start | bytes 4194304 | tf_op jit(solution)/shard_map/all_to_all | solution.py:336
  94.2 4.7 %collective-permute-start.6 = (bf16[64,128]{1,0:T(8,128)(2,1)S(1)}, bf16[64,128]{1,0:T(8,128)(2,1)S(1)}, u32[]{:S(2)}, u32[]{:S(2)}) collective-permute-start(bf16[64,128]{1,0:T(8,128)(2,1)S(1)} %get-tuple-element.49), channel_id=1, source_target_pairs={{0,2},{1,3},{2,0},{3,1},{4,6},{5,7},{6,4},{7,5},{8,10},{9,11},{10,... | collective-permute-start | bytes 49160 | tf_op jit(solution)/shard_map/ppermute | solution.py:332
  96.0 4.5 %collective-permute-start.7 = (bf16[64,128]{1,0:T(8,128)(2,1)S(1)}, bf16[64,128]{1,0:T(8,128)(2,1)S(1)}, u32[]{:S(2)}, u32[]{:S(2)}) collective-permute-start(bf16[64,128]{1,0:T(8,128)(2,1)S(1)} %get-tuple-element.50), channel_id=1, source_target_pairs={{0,4},{1,5},{2,6},{3,7},{4,0},{5,1},{6,2},{7,3},{8,12},{9,13},{10,... | collective-permute-start | bytes 49160 | tf_op jit(solution)/shard_map/ppermute | solution.py:332
  99.0 4.7 %collective-permute-start.8 = (bf16[64,128]{1,0:T(8,128)(2,1)S(1)}, bf16[64,128]{1,0:T(8,128)(2,1)S(1)}, u32[]{:S(2)}, u32[]{:S(2)}) collective-permute-start(bf16[64,128]{1,0:T(8,128)(2,1)S(1)} %get-tuple-element.51), channel_id=1, source_target_pairs={{0,6},{1,7},{2,4},{3,5},{4,2},{5,3},{6,0},{7,1},{8,14},{9,15},{10,... | collective-permute-start | bytes 49160 | tf_op jit(solution)/shard_map/ppermute | solution.py:332
  103.6 8.2 %collective-permute-start.10 = (bf16[16,128]{1,0:T(8,128)(2,1)S(1)}, bf16[16,128]{1,0:T(8,128)(2,1)S(1)}, u32[]{:S(2)}, u32[]{:S(2)}) collective-permute-start(bf16[16,128]{1,0:T(8,128)(2,1)S(1)} %get-tuple-element.54), channel_id=1, source_target_pairs={{0,16},{1,17},{2,18},{3,19},{4,20},{5,21},{6,22},{7,23},{8,24},{9,... | collective-permute-start | bytes 12296 | tf_op jit(solution)/shard_map/ppermute | solution.py:332
  106.4 8.8 %collective-permute-start.11 = (bf16[16,128]{1,0:T(8,128)(2,1)S(1)}, bf16[16,128]{1,0:T(8,128)(2,1)S(1)}, u32[]{:S(2)}, u32[]{:S(2)}) collective-permute-start(bf16[16,128]{1,0:T(8,128)(2,1)S(1)} %get-tuple-element.55), channel_id=1, source_target_pairs={{0,24},{1,25},{2,26},{3,27},{4,28},{5,29},{6,30},{7,31},{8,16},{9,... | collective-permute-start | bytes 12296 | tf_op jit(solution)/shard_map/ppermute | solution.py:332
  110.6 6.4 %collective-permute-start.9 = (bf16[16,128]{1,0:T(8,128)(2,1)S(1)}, bf16[16,128]{1,0:T(8,128)(2,1)S(1)}, u32[]{:S(2)}, u32[]{:S(2)}) collective-permute-start(bf16[16,128]{1,0:T(8,128)(2,1)S(1)} %get-tuple-element.53), channel_id=1, source_target_pairs={{0,8},{1,9},{2,10},{3,11},{4,12},{5,13},{6,14},{7,15},{8,0},{9,1},... | collective-permute-start | bytes 12296 | tf_op jit(solution)/shard_map/ppermute | solution.py:332

commit v2 on v1

--- a/solution.py
+++ b/solution.py
@@ -37,11 +37,7 @@
     return jnp.where(u <= ctx * 128 + r, 0.0, NEG)
 
 
-def own_stats_kernel(CH, len_ref, q_ref, g_ref, o_ref, k_ref, qs_ref, gs_ref, st_ref, bias_ref):
-    @pl.when(pl.program_id(0) == 0)
-    def _():
-        bias_ref[...] = causal_bias(lax.axis_index("ctx"))
-
+def prepare_kernel(len_ref, q_ref, g_ref, o_ref, qs_ref, gs_ref, delta_ref):
     live = len_ref[0] - lax.axis_index("ctx") * 128
     rr = lax.broadcasted_iota(jnp.int32, (128, 128), 0)
     for g in range(8):
@@ -49,22 +45,24 @@
         qs_ref[0, s] = q_ref[:, s]
         grad = jnp.where(rr < live, g_ref[:, s].astype(f32), 0.0)
         gs_ref[0, s] = grad.astype(bf)
-        st_ref[0, 16:24, s] = row_delta(grad, o_ref[:, s].astype(f32))
+        delta_ref[0, :, s] = row_delta(grad, o_ref[:, s].astype(f32))
+
+
+def own_stats_kernel(qs_ref, k_ref, st_ref, bias_ref):
+    @pl.when(pl.program_id(0) == 0)
+    def _():
+        bias_ref[...] = causal_bias(lax.axis_index("ctx"))
 
     K = k_ref[...].reshape(1024, 128)
-
-    @pl.loop(0, 1024 // CH)
-    def _(i):
-        rows = pl.ds(pl.multiple_of(i * CH, CH), CH)
-        S = dot_t(K, qs_ref[0, rows]) + jnp.concatenate([bias_ref[...]] * (CH // 128), axis=1)
-        m = jnp.max(S, axis=0, keepdims=True) * C2
-        total = jnp.sum(jnp.exp2(S * C2 - m), axis=0, keepdims=True)
-        st_ref[0, 0:8, rows] = jnp.broadcast_to(m, (8, CH))
-        st_ref[0, 8:16, rows] = jnp.broadcast_to(total, (8, CH))
-
-
-def prefix_kernel(HP, prompt_ref, offset_ref, qs_ref, gs_ref, st_ref, km_ref, kx_ref, pq_ref, pg_ref, po_ref,
-                  dm_ref, dx_ref, dqt_ref, lse_ref, pdq_ref, bias_ref, pbias_ref):
+    S = dot_t(K, qs_ref[0]) + jnp.concatenate([bias_ref[...]] * 8, axis=1)
+    m = jnp.max(S, axis=0, keepdims=True) * C2
+    total = jnp.sum(jnp.exp2(S * C2 - m), axis=0, keepdims=True)
+    st_ref[0, 0:8] = jnp.broadcast_to(m, (8, 1024))
+    st_ref[0, 8:16] = jnp.broadcast_to(total, (8, 1024))
+
+
+def prefix_kernel(HP, prompt_ref, offset_ref, qs_ref, gs_ref, st_ref, dl_ref, km_ref, kx_ref, pq_ref, pg_ref, po_ref,
+                  d_ref, dqt_ref, lse_ref, pdq_ref, bias_ref, pbias_ref):
     resp = lax.axis_index("resp")
     core, row0 = resp & 1, (lax.axis_index("ctx") * 32 + resp) * 2
     split = offset_ref[1]
@@ -99,7 +97,7 @@
         low = jnp.full((1, 128), NEG, f32)
         m_own = jnp.concatenate([st_ref[n, 0:1], low], axis=1)
         l_own = jnp.concatenate([st_ref[n, 8:9], jnp.zeros((1, 128), f32)], axis=1)
-        both_delta = jnp.concatenate([st_ref[n, 16:17], delta], axis=1)
+        both_delta = jnp.concatenate([dl_ref[n, 0:1], delta], axis=1)
         S = dot_t(K, Q) + jnp.concatenate([bias_ref[...]] * 8 + [pbias_ref[...]], axis=1)
         m = jnp.maximum(jnp.max(S, axis=0, keepdims=True) * C2, m_own)
         e = jnp.exp2(S * C2 - m)
@@ -115,12 +113,13 @@
         for g in range(8):
             pdq_ref[:, n * 1024 + g * 128 : n * 1024 + g * 128 + 128] = pdq[2 * g : 2 * g + 2].astype(bf)
 
-        for dst, s in ((dm_ref, slice(0, 256)), (dx_ref, slice(256, 512))):
-            dst[:, 2 * n] = (dk[s] * SCALE).astype(bf).reshape(8, 32, 128)
-            dst[:, 2 * n + 1] = dv[s].astype(bf).reshape(8, 32, 128)
-
-
-def own_grads_kernel(CH, qs_ref, gs_ref, st_ref, lse_ref, dqt_ref, k_ref, v_ref, dq_ref, d_ref, bias_ref, dk_ref, dv_ref):
+        for side in range(2):
+            s = slice(256 * side, 256 * side + 256)
+            d_ref[:, side, 2 * n] = (dk[s] * SCALE).astype(bf).reshape(8, 32, 128)
+            d_ref[:, side, 2 * n + 1] = dv[s].astype(bf).reshape(8, 32, 128)
+
+
+def own_grads_kernel(CH, qs_ref, gs_ref, dl_ref, lse_ref, dqt_ref, k_ref, v_ref, dq_ref, d_ref, bias_ref, dk_ref, dv_ref):
     @pl.when(pl.program_id(0) == 0)
     def _():
         bias_ref[...] = causal_bias(lax.axis_index("ctx"))
@@ -136,7 +135,7 @@
         Q, G = qs_ref[0, rows], gs_ref[0, rows]
         S = dot_t(K, Q) + jnp.concatenate([bias_ref[...]] * (CH // 128), axis=1)
         p = jnp.exp2(S * C2 - lse_ref[0, 0:1, rows])
-        ds = (p * (dot_t(V, G) - st_ref[0, 16:17, rows])).astype(bf)
+        ds = (p * (dot_t(V, G) - dl_ref[0, 0:1, rows])).astype(bf)
         dv_ref[...] += dot(p.astype(bf), G)
         dk_ref[...] += dot(ds, Q)
         dq = ((dqt_ref[0, :, rows] + dot(KT, ds)) * SCALE).T
@@ -171,20 +170,32 @@
     return pl.CostEstimate(flops=int(gflops * 1e9), bytes_accessed=int(megabytes * 2**20), transcendentals=0)
 
 
-def own_stats(length, q, g, o, own, CH=1024):
-    return pl.pallas_call(
-        functools.partial(own_stats_kernel, CH),
+def prepare(length, q, g, o):
+    return pl.pallas_call(
+        prepare_kernel,
         grid=(4,),
-        in_specs=[SMEM, wide(128), wide(128), wide(128), own_block(0)],
-        out_specs=[per_head(1024, 128), per_head(1024, 128), per_head(24, 1024)],
-        out_shape=[shape_of(4, 1024, 128), shape_of(4, 1024, 128), shape_of(4, 24, 1024, dtype=f32)],
+        in_specs=[SMEM, wide(128), wide(128), wide(128)],
+        out_specs=[per_head(1024, 128), per_head(1024, 128), per_head(8, 1024)],
+        out_shape=[shape_of(4, 1024, 128), shape_of(4, 1024, 128), shape_of(4, 8, 1024, dtype=f32)],
+        compiler_params=LIMIT,
+        cost_estimate=cost(0.1, 5),
+    )(length, q, g, o)
+
+
+def own_stats(qs, own):
+    return pl.pallas_call(
+        own_stats_kernel,
+        grid=(4,),
+        in_specs=[per_head(1024, 128), own_block(0)],
+        out_specs=per_head(16, 1024),
+        out_shape=shape_of(4, 16, 1024, dtype=f32),
         scratch_shapes=[pltpu.VMEM((1024, 128), f32)],
         compiler_params=LIMIT,
         cost_estimate=cost(1.2, 6),
-    )(length, q, g, o, own)
-
-
-def prefix(prompt, offset, qs, gs, st, mine, other, pq, pg, po, HP=1):
+    )(qs, own)
+
+
+def prefix(prompt, offset, qs, gs, st, delta, mine, other, pq, pg, po, HP=1):
     def heads(*shape):
         return pl.BlockSpec((HP,) + shape, lambda h: (h, 0, 0))
 
@@ -193,28 +204,28 @@
     return pl.pallas_call(
         functools.partial(prefix_kernel, HP),
         grid=(4 // HP,),
-        in_specs=[SMEM, SMEM, heads(1024, 128), heads(1024, 128), heads(24, 1024), big, big, row, row, row],
-        out_specs=[big, big, heads(128, 1024), heads(8, 1024), row],
-        out_shape=[shape_of(8, 8, 32, 128), shape_of(8, 8, 32, 128), shape_of(4, 128, 1024, dtype=f32),
+        in_specs=[SMEM, SMEM, heads(1024, 128), heads(1024, 128), heads(16, 1024), heads(8, 1024), big, big, row, row, row],
+        out_specs=[pl.BlockSpec((8, 2, 2 * HP, 32, 128), lambda h: (0, 0, h, 0, 0)), heads(128, 1024), heads(8, 1024), row],
+        out_shape=[shape_of(8, 2, 8, 32, 128), shape_of(4, 128, 1024, dtype=f32),
                    shape_of(4, 8, 1024, dtype=f32), shape_of(2, 4096)],
         scratch_shapes=[pltpu.VMEM((512, 128), f32), pltpu.VMEM((512, 128), f32)],
         compiler_params=LIMIT,
         cost_estimate=cost(2.7, 8),
-    )(prompt, offset, qs, gs, st, mine, other, pq, pg, po)
-
-
-def own_grads(qs, gs, st, lse, dqt, own, CH=1024):
+    )(prompt, offset, qs, gs, st, delta, mine, other, pq, pg, po)
+
+
+def own_grads(qs, gs, delta, lse, dqt, own, CH=1024):
     return pl.pallas_call(
         functools.partial(own_grads_kernel, CH),
         grid=(4,),
-        in_specs=[per_head(1024, 128), per_head(1024, 128), per_head(24, 1024), per_head(8, 1024), per_head(128, 1024),
+        in_specs=[per_head(1024, 128), per_head(1024, 128), per_head(8, 1024), per_head(8, 1024), per_head(128, 1024),
                   own_block(0), own_block(1)],
         out_specs=[wide(128), pl.BlockSpec((8, 256, 128), lambda h: (0, h, 0))],
         out_shape=[shape_of(128, 4096), shape_of(8, 1024, 128)],
         scratch_shapes=[pltpu.VMEM((1024, 128), f32)] * 3,
         compiler_params=LIMIT,
         cost_estimate=cost(5.4, 10),
-    )(qs, gs, st, lse, dqt, own, own)
+    )(qs, gs, delta, lse, dqt, own, own)
 
 
 def copies_kernel(key_ref, value_ref, pack_key_ref, pack_value_ref, out_ref, pack_ref, block, rows, sems):
@@ -271,14 +282,14 @@
 def ungroup_kernel(parts_ref, *refs):
     total = jnp.sum(parts_ref[...].astype(f32), axis=0)
     for m in range(4):
-        rows = [total[k, 8 * i + 2 * m : 8 * i + 2 * m + 2] for i in range(4) for k in range(8)]
+        rows = [total[s, k, 8 * i + 2 * m : 8 * i + 2 * m + 2] for s in range(2) for i in range(4) for k in range(8)]
         refs[m][...] = jnp.concatenate(rows, axis=0).astype(bf)
 
 
 def ungroup(parts):
     return pl.pallas_call(
         ungroup_kernel,
-        out_shape=[shape_of(64, 128)] * 4,
+        out_shape=[shape_of(128, 128)] * 4,
         compiler_params=SMALL,
         cost_estimate=cost(0, 1),
     )(parts)
@@ -287,26 +298,41 @@
 def quarter_kernel(*refs):
     total = sum(ref[...].astype(f32) for ref in refs[:4])
     for m in range(4):
-        refs[4 + m][...] = total[16 * m : 16 * m + 16].astype(bf)
+        both = [total[i : i + 16] for i in (16 * m, 64 + 16 * m)]
+        refs[4 + m][...] = jnp.concatenate(both, axis=0).astype(bf)
 
 
 def quarter(*blocks):
     return pl.pallas_call(
         quarter_kernel,
-        out_shape=[shape_of(16, 128)] * 4,
+        out_shape=[shape_of(32, 128)] * 4,
         compiler_params=SMALL,
         cost_estimate=cost(0, 0.1),
     )(*blocks)
 
 
-def finish_pack_kernel(a_ref, b_ref, c_ref, d_ref, key_ref, value_ref):
-    rows = sum(ref[...].astype(f32) for ref in (a_ref, b_ref, c_ref, d_ref))
+def sides_kernel(a_ref, b_ref, c_ref, d_ref, mine_ref, other_ref):
+    total = sum(ref[...].astype(f32) for ref in (a_ref, b_ref, c_ref, d_ref))
+    mine_ref[...] = total[0:16].astype(bf)
+    other_ref[...] = total[16:32].astype(bf)
+
+
+def sides(*blocks):
+    return pl.pallas_call(
+        sides_kernel, out_shape=[shape_of(16, 128)] * 2, compiler_params=SMALL, cost_estimate=cost(0, 0.1)
+    )(*blocks)
+
+
+def finish_pack_kernel(a_ref, b_ref, key_ref, value_ref):
+    rows = a_ref[...].astype(f32) + b_ref[...].astype(f32)
     key_ref[...] = jnp.concatenate([rows[4 * h : 4 * h + 2] for h in range(4)], axis=1).astype(bf)
     value_ref[...] = jnp.concatenate([rows[4 * h + 2 : 4 * h + 4] for h in range(4)], axis=1).astype(bf)
 
 
 def finish_pack(*blocks):
-    return pl.pallas_call(finish_pack_kernel, out_shape=[shape_of(2, 512)] * 2, compiler_params=SMALL, cost_estimate=cost(0, 0.1))(*blocks)
+    return pl.pallas_call(
+        finish_pack_kernel, out_shape=[shape_of(2, 512)] * 2, compiler_params=SMALL, cost_estimate=cost(0, 0.1)
+    )(*blocks)
 
 
 def finish_own_kernel(parts_ref, key_ref, value_ref):
@@ -345,20 +371,23 @@
     own = exchange(copies)
     for mask in (2, 4, 8):
         block = jnp.concatenate([block, from_partner(block, mask)], axis=0)
-    mine = exchange(regroup(block, from_partner(block, 16)))
-    qs, gs, st = own_stats(resp_length, resp_query[0], resp_grad[0], resp_out[0], own)
+    block, q, g, o = lax.optimization_barrier((block, resp_query[0], resp_grad[0], resp_out[0]))
+    qs, gs, delta = prepare(resp_length, q, g, o)
+    last, qs = lax.optimization_barrier((from_partner(block, 16), qs))
+    mine = exchange(regroup(block, last))
+    st = own_stats(qs, own)
     mine, st = lax.optimization_barrier((mine, st))
     other = from_partner(mine, 1)
-    dmine, dother, dqt, lse, pdq = prefix(
-        prompt_id, pack_offset, qs, gs, st, mine, other, pack_query, pack_grad, pack_out
+    d, dqt, lse, pdq = prefix(
+        prompt_id, pack_offset, qs, gs, st, delta, mine, other, pack_query, pack_grad, pack_out
     )
-    both = dmine.astype(f32) + from_partner(dother, 1).astype(f32)
-    parts = exchange(both.astype(bf))
-    dq, down = own_grads(qs, gs, st, lse, dqt, own)
+    parts = exchange(d)
+    dq, down = own_grads(qs, gs, delta, lse, dqt, own)
     parts = ungroup(parts)
     own_parts = exchange(down)
     parts = quarter(parts[0], *[from_partner(parts[m], 2 * m) for m in (1, 2, 3)])
-    block_key, block_value = finish_pack(parts[0], *[from_partner(parts[m], 8 * m) for m in (1, 2, 3)])
+    mine, other = sides(parts[0], *[from_partner(parts[m], 8 * m) for m in (1, 2, 3)])
+    block_key, block_value = finish_pack(mine, from_partner(other, 1))
     key, value = finish_own(own_parts)
     return dq[None], key[None], value[None], pdq, block_key, block_value
 

time: 123 us -> 121 us (0.984); the launches traced: 123 us -> 119 us
  waiting for transfers between devices: 29.4 us -> 24.3 us
  Pallas kernels: 39 us -> 42.4 us
  other arithmetic: 2.06 us -> 0.01 us
    ppermute x12, waiting for transfers between devices: 20.5 us -> 15.3 us  [from_partner(): return lax.ppermute(block, 'resp', [(i, i ^ mask) for i in range(32)])]
    pallas_call x3 -> x5, Pallas kernels: 9.11 us -> 12.5 us  [the longest x1 8.06 us: own_stats(): pl.pallas_call(own_stats_kernel, grid=(4,), in_specs=[per_head(1024, 128)...]
    all_to_all x4, starting transfers between devices: 21.8 us -> 18.7 us  [exchange(): return lax.all_to_all(blocks, 'ctx', 0, 0, tiled=True)]
    ppermute x12, starting transfers between devices: 27.6 us -> 30.7 us  [from_partner(): return lax.ppermute(block, 'resp', [(i, i ^ mask) for i in range(32)])]
    convert_element_type x1 -> x0, other arithmetic: 2.06 us -> none  [shards(): parts = exchange(both.astype(bf))]
  transfers between devices with their start and end apart: 16 -> 16, of which waited for: 13 -> 12; matrix products, arithmetic and copies ran while one was open for 0% -> 0% of each run, Pallas kernels for 20% -> 23%
where the time goes in v2:
time: 121 us; the launch traced here: 119 us
  starting transfers between devices  49.3 us (41%)
  Pallas kernels  42.4 us (35%)
  waiting for transfers between devices  24.3 us (20%)
  between operations  2 us (2%)
    ppermute x12, starting transfers between devices, from_partner(): return lax.ppermute(block, 'resp', [(i, i ^ mask) for i in range(32)])  30.7 us
    all_to_all x4, starting transfers between devices, exchange(): return lax.all_to_all(blocks, 'ctx', 0, 0, tiled=True)  18.7 us
    ppermute x12, waiting for transfers between devices, from_partner(): return lax.ppermute(block, 'resp', [(i, i ^ mask) for i in range(32)])  15.3 us
    pallas_call x1, Pallas kernels, own_grads(): pl.pallas_call(functools.partial(own_grads_kernel, CH), grid=(4,), in_spe...  13.4 us
    pallas_call x1, Pallas kernels, prefix(): pl.pallas_call(functools.partial(prefix_kernel, HP), grid=(4 // HP,), in_...  10.5 us
    all_to_all x4, waiting for transfers between devices, exchange(): return lax.all_to_all(blocks, 'ctx', 0, 0, tiled=True)  8.95 us
    pallas_call x1, Pallas kernels, own_stats(): pl.pallas_call(own_stats_kernel, grid=(4,), in_specs=[per_head(1024, 128)...  8.06 us
    pallas_call x1, Pallas kernels, prepare(): pl.pallas_call(prepare_kernel, grid=(4,), in_specs=[SMEM, wide(128), wide...  4.19 us
  transfers between devices with their start and end apart: 16, of which 12 were waited for; matrix products, arithmetic and copies ran while one was open for 0% of the time, Pallas kernels for 23%

profile of v2, /device:TPU:1, one launch (start us, length us, event | category | flops | bytes accessed | tf_op | source)
XLA Modules:
  0.0 118.9 jit_solution(9738008599827478925)
XLA Ops:
  0.6 3.0 %shard_map.172 = (bf16[8,1024,128]{2,1,0:T(8,128)(2,1)}, bf16[16,128]{1,0:T(8,128)(2,1)}) custom-call(bf16[128,512]{1,0:T(8,128)(2,1)} %bitcast.11, bf16[128,512]{1,0:T(8,128)(2,1)} %bitcast.12, bf16[2,512]{1,0:T(2,128)(2,1)} %pack_key_ref.1, bf16[2,512]{1,0:T(2,128)(2,1)} %pack_value_ref.1), custom_call_target="tpu_custom_call" | custom-call | bytes 2097152 | tf_op jit(solution)/shard_map/pallas_call | solution.py:253
  3.7 5.9 %all-to-all-start.1 = ((bf16[8,1024,128]{2,1,0:T(8,128)(2,1)}), bf16[8,1024,128]{2,1,0:T(8,128)(2,1)S(1)}, u32[]{:S(2)}, u32[]{:S(2)}) async-start(bf16[8,1024,128]{2,1,0:T(8,128)(2,1)} %get-tuple-element.49), calls=%async_computation.1 | async-start | bytes 4194304 | tf_op jit(solution)/shard_map/all_to_all | solution.py:362
  9.5 1.7 %collective-permute-start = (bf16[16,128]{1,0:T(8,128)(2,1)S(1)}, bf16[16,128]{1,0:T(8,128)(2,1)S(1)}, u32[]{:S(2)}, u32[]{:S(2)}) collective-permute-start(bf16[16,128]{1,0:T(8,128)(2,1)S(1)} %copy-done.2), channel_id=1, source_target_pairs={{0,2},{1,3},{2,0},{3,1},{4,6},{5,7},{6,4},{7,5},{8,10},{9,11},{10,... | collective-permute-start | bytes 12296 | tf_op jit(solution)/shard_map/ppermute | solution.py:358
  12.3 3.0 %collective-permute-start.1 = (bf16[32,128]{1,0:T(8,128)(2,1)S(1)}, bf16[32,128]{1,0:T(8,128)(2,1)S(1)}, u32[]{:S(2)}, u32[]{:S(2)}) collective-permute-start(bf16[32,128]{1,0:T(8,128)(2,1)S(1)} %pad_maximum_fusion.2), channel_id=1, source_target_pairs={{0,4},{1,5},{2,6},{3,7},{4,0},{5,1},{6,2},{7,3},{8,12},{9,13},{10,... | collective-permute-start | bytes 24584 | tf_op jit(solution)/shard_map/ppermute | solution.py:358
  16.6 6.1 %collective-permute-start.2 = (bf16[64,128]{1,0:T(8,128)(2,1)S(1)}, bf16[64,128]{1,0:T(8,128)(2,1)S(1)}, u32[]{:S(2)}, u32[]{:S(2)}) collective-permute-start(bf16[64,128]{1,0:T(8,128)(2,1)S(1)} %pad_maximum_fusion.1), channel_id=1, source_target_pairs={{0,8},{1,9},{2,10},{3,11},{4,12},{5,13},{6,14},{7,15},{8,0},{9,1},... | collective-permute-start | bytes 49160 | tf_op jit(solution)/shard_map/ppermute | solution.py:358
  23.9 2.6 %collective-permute-start.3 = (bf16[128,128]{1,0:T(8,128)(2,1)S(1)}, bf16[128,128]{1,0:T(8,128)(2,1)S(1)}, u32[]{:S(2)}, u32[]{:S(2)}) collective-permute-start(bf16[128,128]{1,0:T(8,128)(2,1)S(1)} %pad_maximum_fusion.refs_0_), channel_id=1, source_target_pairs={{0,16},{1,17},{2,18},{3,19},{4,20},{5,21},{6,22},{7,23},{8,24},{9,... | collective-permute-start | bytes 98312 | tf_op jit(solution)/shard_map/ppermute | solution.py:358
  27.2 4.2 %shard_map.173 = (bf16[4,1024,128]{2,1,0:T(8,128)(2,1)}, bf16[4,1024,128]{2,1,0:T(8,128)(2,1)}, f32[4,8,1024]{2,1,0:T(8,128)}) custom-call(s32[1]{0:T(128)S(6)} %copy.19.len_ref, bf16[128,4096]{1,0:T(8,128)(2,1)} %bitcast.8, bf16[128,4096]{1,0:T(8,128)(2,1)} %bitcast.9, bf16[128,4096]{1,0:T(8,128)(2,1)} %bitcast.10), custom_call_target="tpu_custom_call" | custom-call | flops 100000000 | bytes 5242880 | tf_op jit(solution)/shard_map/pallas_call | solution.py:174
  32.2 4.4 %all-to-all-done.1.k_ref.v_ref = bf16[8,1024,128]{2,1,0:T(8,128)(2,1)S(1)} async-done(((bf16[8,1024,128]{2,1,0:T(8,128)(2,1)}), bf16[8,1024,128]{2,1,0:T(8,128)(2,1)S(1)}, u32[]{:S(2)}, u32[]{:S(2)}) %all-to-all-start.1) | async-done | bytes 2097184 | tf_op jit(solution)/shard_map/all_to_all | solution.py:362
  36.6 5.4 %all-to-all-start = ((bf16[8,8,32,128]{3,2,1,0:T(8,128)(2,1)}), bf16[8,8,32,128]{3,2,1,0:T(8,128)(2,1)S(1)}, u32[]{:S(2)}, u32[]{:S(2)}) async-start(bf16[8,8,32,128]{3,2,1,0:T(8,128)(2,1)} %shard_map.174), calls=%async_computation | async-start | bytes 1048576 | tf_op jit(solution)/shard_map/all_to_all | solution.py:362
  42.1 8.1 %shard_map.175.st_ref = f32[4,16,1024]{2,1,0:T(8,128)} custom-call(bf16[4,1024,128]{2,1,0:T(8,128)(2,1)} %get-tuple-element.45.qs_ref, bf16[8,1024,128]{2,1,0:T(8,128)(2,1)} %copy-done), custom_call_target="tpu_custom_call" | custom-call | flops 1200000000 | bytes 6291456 | tf_op jit(solution)/shard_map/pallas_call | solution.py:186
  50.1 2.1 %all-to-all-done.km_ref = bf16[8,8,32,128]{3,2,1,0:T(8,128)(2,1)S(1)} async-done(((bf16[8,8,32,128]{3,2,1,0:T(8,128)(2,1)}), bf16[8,8,32,128]{3,2,1,0:T(8,128)(2,1)S(1)}, u32[]{:S(2)}, u32[]{:S(2)}) %all-to-all-start) | async-done | bytes 524320 | tf_op jit(solution)/shard_map/all_to_all | solution.py:362
  55.5 10.5 %shard_map.176 = (bf16[8,2,8,32,128]{4,3,2,1,0:T(8,128)(2,1)}, f32[4,128,1024]{2,1,0:T(8,128)}, f32[4,8,1024]{2,1,0:T(8,128)}, bf16[2,4096]{1,0:T(2,128)(2,1)}) custom-call(s32[1]{0:T(128)S(6)} %copy.20.prompt_ref, s32[3]{0:T(128)} %offset_ref.1, bf16[4,1024,128]{2,1,0:T(8,128)(2,1)} %get-tuple-element.45.qs_ref, ...), custom_call_target="tpu_custom_call" | custom-call | flops 2700000000 | bytes 8388608 | tf_op jit(solution)/shard_map/pallas_call | solution.py:204
  65.9 3.8 %all-to-all-start.3 = ((bf16[8,2,8,32,128]{4,3,2,1,0:T(8,128)(2,1)}), bf16[8,2,8,32,128]{4,3,2,1,0:T(8,128)(2,1)S(1)}, u32[]{:S(2)}, u32[]{:S(2)}) async-start(bf16[8,2,8,32,128]{4,3,2,1,0:T(8,128)(2,1)} %get-tuple-element.59), calls=%async_computation.3 | async-start | bytes 2097152 | tf_op jit(solution)/shard_map/all_to_all | solution.py:362
  69.7 13.4 %shard_map.177 = (bf16[128,4096]{1,0:T(8,128)(2,1)}, bf16[8,1024,128]{2,1,0:T(8,128)(2,1)}) custom-call(bf16[4,1024,128]{2,1,0:T(8,128)(2,1)} %get-tuple-element.45.qs_ref, bf16[4,1024,128]{2,1,0:T(8,128)(2,1)} %get-tuple-element.46.gs_ref, f32[4,8,1024]{2,1,0:T(8,128)} %get-tuple-element.47.dl_ref, f32[4,8,1024]{2,1,0:T(8,128)} %get-tuple-element.52.lse_ref, ...), custom_call_target="tpu_custom_call" | custom-call | flops 5400000000 | bytes 10485760 | tf_op jit(solution)/shard_map/pallas_call | solution.py:218
  83.1 2.4 %all-to-all-done.3.parts_ref = bf16[8,2,8,32,128]{4,3,2,1,0:T(8,128)(2,1)S(1)} async-done(((bf16[8,2,8,32,128]{4,3,2,1,0:T(8,128)(2,1)}), bf16[8,2,8,32,128]{4,3,2,1,0:T(8,128)(2,1)S(1)}, u32[]{:S(2)}, u32[]{:S(2)}) %all-to-all-start.3) | async-done | bytes 1048608 | tf_op jit(solution)/shard_map/all_to_all | solution.py:362
  85.5 3.6 %all-to-all-start.2 = ((bf16[8,1024,128]{2,1,0:T(8,128)(2,1)}), bf16[8,1024,128]{2,1,0:T(8,128)(2,1)S(1)}, u32[]{:S(2)}, u32[]{:S(2)}) async-start(bf16[8,1024,128]{2,1,0:T(8,128)(2,1)} %get-tuple-element.55), calls=%async_computation.2 | async-start | bytes 4194304 | tf_op jit(solution)/shard_map/all_to_all | solution.py:362
  89.4 1.7 %collective-permute-start.5 = (bf16[128,128]{1,0:T(8,128)(2,1)S(1)}, bf16[128,128]{1,0:T(8,128)(2,1)S(1)}, u32[]{:S(2)}, u32[]{:S(2)}) collective-permute-start(bf16[128,128]{1,0:T(8,128)(2,1)S(1)} %get-tuple-element.61), channel_id=1, source_target_pairs={{0,2},{1,3},{2,0},{3,1},{4,6},{5,7},{6,4},{7,5},{8,10},{9,11},{10,... | collective-permute-start | bytes 98312 | tf_op jit(solution)/shard_map/ppermute | solution.py:358
  91.1 3.0 %collective-permute-start.6 = (bf16[128,128]{1,0:T(8,128)(2,1)S(1)}, bf16[128,128]{1,0:T(8,128)(2,1)S(1)}, u32[]{:S(2)}, u32[]{:S(2)}) collective-permute-start(bf16[128,128]{1,0:T(8,128)(2,1)S(1)} %get-tuple-element.62), channel_id=1, source_target_pairs={{0,4},{1,5},{2,6},{3,7},{4,0},{5,1},{6,2},{7,3},{8,12},{9,13},{10,... | collective-permute-start | bytes 98312 | tf_op jit(solution)/shard_map/ppermute | solution.py:358
  94.1 1.9 %collective-permute-done.6.refs_2_ = bf16[128,128]{1,0:T(8,128)(2,1)S(1)} collective-permute-done((bf16[128,128]{1,0:T(8,128)(2,1)S(1)}, bf16[128,128]{1,0:T(8,128)(2,1)S(1)}, u32[]{:S(2)}, u32[]{:S(2)}) %collective-permute-start.6) | collective-permute-done | bytes 32800 | tf_op jit(solution)/shard_map/ppermute | solution.py:358
  96.1 2.9 %collective-permute-done.7.refs_3_ = bf16[128,128]{1,0:T(8,128)(2,1)S(1)} collective-permute-done((bf16[128,128]{1,0:T(8,128)(2,1)S(1)}, bf16[128,128]{1,0:T(8,128)(2,1)S(1)}, u32[]{:S(2)}, u32[]{:S(2)}) %collective-permute-start.7) | collective-permute-done | bytes 32800 | tf_op jit(solution)/shard_map/ppermute | solution.py:358
  99.0 7.0 %collective-permute-start.10 = (bf16[32,128]{1,0:T(8,128)(2,1)S(1)}, bf16[32,128]{1,0:T(8,128)(2,1)S(1)}, u32[]{:S(2)}, u32[]{:S(2)}) collective-permute-start(bf16[32,128]{1,0:T(8,128)(2,1)S(1)} %get-tuple-element.67), channel_id=1, source_target_pairs={{0,24},{1,25},{2,26},{3,27},{4,28},{5,29},{6,30},{7,31},{8,16},{9,... | collective-permute-start | bytes 24584 | tf_op jit(solution)/shard_map/ppermute | solution.py:358
  107.1 2.4 %collective-permute-done.10.d_ref = bf16[32,128]{1,0:T(8,128)(2,1)S(1)} collective-permute-done((bf16[32,128]{1,0:T(8,128)(2,1)S(1)}, bf16[32,128]{1,0:T(8,128)(2,1)S(1)}, u32[]{:S(2)}, u32[]{:S(2)}) %collective-permute-start.10) | collective-permute-done | bytes 8224 | tf_op jit(solution)/shard_map/ppermute | solution.py:358
  109.5 2.8 %collective-permute-done.8.b_ref = bf16[32,128]{1,0:T(8,128)(2,1)S(1)} collective-permute-done((bf16[32,128]{1,0:T(8,128)(2,1)S(1)}, bf16[32,128]{1,0:T(8,128)(2,1)S(1)}, u32[]{:S(2)}, u32[]{:S(2)}) %collective-permute-start.8) | collective-permute-done | bytes 8224 | tf_op jit(solution)/shard_map/ppermute | solution.py:358
  112.4 3.5 %collective-permute-start.11 = (bf16[16,128]{1,0:T(8,128)(2,1)S(1)}, bf16[16,128]{1,0:T(8,128)(2,1)S(1)}, u32[]{:S(2)}, u32[]{:S(2)}) collective-permute-start(bf16[16,128]{1,0:T(8,128)(2,1)S(1)} %get-tuple-element.69), channel_id=1, source_target_pairs={{0,1},{1,0},{2,3},{3,2},{4,5},{5,4},{6,7},{7,6},{8,9},{9,8},{10,11... | collective-permute-start | bytes 12296 | tf_op jit(solution)/shard_map/ppermute | solution.py:358
  (30 shorter events, 11.4 us)
Async XLA Ops:
  3.7 5.9 %copy-start.2 = (bf16[16,128]{1,0:T(8,128)(2,1)S(1)}, bf16[16,128]{1,0:T(8,128)(2,1)}, u32[]{:S(2)}) copy-start(bf16[16,128]{1,0:T(8,128)(2,1)} %get-tuple-element.39) | copy-start | bytes 12292
  3.7 33.0 %all-to-all-start.1 = ((bf16[8,1024,128]{2,1,0:T(8,128)(2,1)}), bf16[8,1024,128]{2,1,0:T(8,128)(2,1)S(1)}, u32[]{:S(2)}, u32[]{:S(2)}) async-start(bf16[8,1024,128]{2,1,0:T(8,128)(2,1)} %get-tuple-element.49), calls=%async_computation.1 | async-start | bytes 4194304 | tf_op jit(solution)/shard_map/all_to_all | solution.py:362
  9.5 2.7 %collective-permute-start = (bf16[16,128]{1,0:T(8,128)(2,1)S(1)}, bf16[16,128]{1,0:T(8,128)(2,1)S(1)}, u32[]{:S(2)}, u32[]{:S(2)}) collective-permute-start(bf16[16,128]{1,0:T(8,128)(2,1)S(1)} %copy-done.2), channel_id=1, source_target_pairs={{0,2},{1,3},{2,0},{3,1},{4,6},{5,7},{6,4},{7,5},{8,10},{9,11},{10,... | collective-permute-start | bytes 12296 | tf_op jit(solution)/shard_map/ppermute | solution.py:358
  12.3 4.3 %collective-permute-start.1 = (bf16[32,128]{1,0:T(8,128)(2,1)S(1)}, bf16[32,128]{1,0:T(8,128)(2,1)S(1)}, u32[]{:S(2)}, u32[]{:S(2)}) collective-permute-start(bf16[32,128]{1,0:T(8,128)(2,1)S(1)} %pad_maximum_fusion.2), channel_id=1, source_target_pairs={{0,4},{1,5},{2,6},{3,7},{4,0},{5,1},{6,2},{7,3},{8,12},{9,13},{10,... | collective-permute-start | bytes 24584 | tf_op jit(solution)/shard_map/ppermute | solution.py:358
  16.6 7.3 %collective-permute-start.2 = (bf16[64,128]{1,0:T(8,128)(2,1)S(1)}, bf16[64,128]{1,0:T(8,128)(2,1)S(1)}, u32[]{:S(2)}, u32[]{:S(2)}) collective-permute-start(bf16[64,128]{1,0:T(8,128)(2,1)S(1)} %pad_maximum_fusion.1), channel_id=1, source_target_pairs={{0,8},{1,9},{2,10},{3,11},{4,12},{5,13},{6,14},{7,15},{8,0},{9,1},... | collective-permute-start | bytes 49160 | tf_op jit(solution)/shard_map/ppermute | solution.py:358
  23.9 7.5 %collective-permute-start.3 = (bf16[128,128]{1,0:T(8,128)(2,1)S(1)}, bf16[128,128]{1,0:T(8,128)(2,1)S(1)}, u32[]{:S(2)}, u32[]{:S(2)}) collective-permute-start(bf16[128,128]{1,0:T(8,128)(2,1)S(1)} %pad_maximum_fusion.refs_0_), channel_id=1, source_target_pairs={{0,16},{1,17},{2,18},{3,19},{4,20},{5,21},{6,22},{7,23},{8,24},{9,... | collective-permute-start | bytes 98312 | tf_op jit(solution)/shard_map/ppermute | solution.py:358
  36.6 5.4 %copy-start = (bf16[8,1024,128]{2,1,0:T(8,128)(2,1)}, bf16[8,1024,128]{2,1,0:T(8,128)(2,1)S(1)}, u32[]{:S(2)}) copy-start(bf16[8,1024,128]{2,1,0:T(8,128)(2,1)S(1)} %all-to-all-done.1.k_ref.v_ref) | copy-start | bytes 6291460
  36.6 15.6 %all-to-all-start = ((bf16[8,8,32,128]{3,2,1,0:T(8,128)(2,1)}), bf16[8,8,32,128]{3,2,1,0:T(8,128)(2,1)S(1)}, u32[]{:S(2)}, u32[]{:S(2)}) async-start(bf16[8,8,32,128]{3,2,1,0:T(8,128)(2,1)} %shard_map.174), calls=%async_computation | async-start | bytes 1048576 | tf_op jit(solution)/shard_map/all_to_all | solution.py:362
  52.2 2.4 %copy-start.1 = (bf16[8,8,32,128]{3,2,1,0:T(8,128)(2,1)}, bf16[8,8,32,128]{3,2,1,0:T(8,128)(2,1)S(1)}, u32[]{:S(2)}) copy-start(bf16[8,8,32,128]{3,2,1,0:T(8,128)(2,1)S(1)} %all-to-all-done.km_ref) | copy-start | bytes 1572868
  52.3 2.4 %collective-permute-start.4 = (bf16[8,8,32,128]{3,2,1,0:T(8,128)(2,1)S(1)}, bf16[8,8,32,128]{3,2,1,0:T(8,128)(2,1)S(1)}, u32[]{:S(2)}, u32[]{:S(2)}) collective-permute-start(bf16[8,8,32,128]{3,2,1,0:T(8,128)(2,1)S(1)} %all-to-all-done.km_ref), channel_id=1, source_target_pairs={{0,1},{1,0},{2,3},{3,2},{4,5},{5,4},{6,7},{7,6},{8,9},{9,8},{10,11... | collective-permute-start | bytes 1572872 | tf_op jit(solution)/shard_map/ppermute | solution.py:358
  54.6 0.8 copy-start.3
  65.9 19.6 %all-to-all-start.3 = ((bf16[8,2,8,32,128]{4,3,2,1,0:T(8,128)(2,1)}), bf16[8,2,8,32,128]{4,3,2,1,0:T(8,128)(2,1)S(1)}, u32[]{:S(2)}, u32[]{:S(2)}) async-start(bf16[8,2,8,32,128]{4,3,2,1,0:T(8,128)(2,1)} %get-tuple-element.59), calls=%async_computation.3 | async-start | bytes 2097152 | tf_op jit(solution)/shard_map/all_to_all | solution.py:362
  85.5 31.7 %all-to-all-start.2 = ((bf16[8,1024,128]{2,1,0:T(8,128)(2,1)}), bf16[8,1024,128]{2,1,0:T(8,128)(2,1)S(1)}, u32[]{:S(2)}, u32[]{:S(2)}) async-start(bf16[8,1024,128]{2,1,0:T(8,128)(2,1)} %get-tuple-element.55), calls=%async_computation.2 | async-start | bytes 4194304 | tf_op jit(solution)/shard_map/all_to_all | solution.py:362
  89.4 4.7 %collective-permute-start.5 = (bf16[128,128]{1,0:T(8,128)(2,1)S(1)}, bf16[128,128]{1,0:T(8,128)(2,1)S(1)}, u32[]{:S(2)}, u32[]{:S(2)}) collective-permute-start(bf16[128,128]{1,0:T(8,128)(2,1)S(1)} %get-tuple-element.61), channel_id=1, source_target_pairs={{0,2},{1,3},{2,0},{3,1},{4,6},{5,7},{6,4},{7,5},{8,10},{9,11},{10,... | collective-permute-start | bytes 98312 | tf_op jit(solution)/shard_map/ppermute | solution.py:358
  91.1 4.9 %collective-permute-start.6 = (bf16[128,128]{1,0:T(8,128)(2,1)S(1)}, bf16[128,128]{1,0:T(8,128)(2,1)S(1)}, u32[]{:S(2)}, u32[]{:S(2)}) collective-permute-start(bf16[128,128]{1,0:T(8,128)(2,1)S(1)} %get-tuple-element.62), channel_id=1, source_target_pairs={{0,4},{1,5},{2,6},{3,7},{4,0},{5,1},{6,2},{7,3},{8,12},{9,13},{10,... | collective-permute-start | bytes 98312 | tf_op jit(solution)/shard_map/ppermute | solution.py:358
  94.1 4.9 %collective-permute-start.7 = (bf16[128,128]{1,0:T(8,128)(2,1)S(1)}, bf16[128,128]{1,0:T(8,128)(2,1)S(1)}, u32[]{:S(2)}, u32[]{:S(2)}) collective-permute-start(bf16[128,128]{1,0:T(8,128)(2,1)S(1)} %get-tuple-element.63), channel_id=1, source_target_pairs={{0,6},{1,7},{2,4},{3,5},{4,2},{5,3},{6,0},{7,1},{8,14},{9,15},{10,... | collective-permute-start | bytes 98312 | tf_op jit(solution)/shard_map/ppermute | solution.py:358
  99.0 10.5 %collective-permute-start.10 = (bf16[32,128]{1,0:T(8,128)(2,1)S(1)}, bf16[32,128]{1,0:T(8,128)(2,1)S(1)}, u32[]{:S(2)}, u32[]{:S(2)}) collective-permute-start(bf16[32,128]{1,0:T(8,128)(2,1)S(1)} %get-tuple-element.67), channel_id=1, source_target_pairs={{0,24},{1,25},{2,26},{3,27},{4,28},{5,29},{6,30},{7,31},{8,16},{9,... | collective-permute-start | bytes 24584 | tf_op jit(solution)/shard_map/ppermute | solution.py:358
  105.9 6.4 %collective-permute-start.8 = (bf16[32,128]{1,0:T(8,128)(2,1)S(1)}, bf16[32,128]{1,0:T(8,128)(2,1)S(1)}, u32[]{:S(2)}, u32[]{:S(2)}) collective-permute-start(bf16[32,128]{1,0:T(8,128)(2,1)S(1)} %get-tuple-element.65), channel_id=1, source_target_pairs={{0,8},{1,9},{2,10},{3,11},{4,12},{5,13},{6,14},{7,15},{8,0},{9,1},... | collective-permute-start | bytes 24584 | tf_op jit(solution)/shard_map/ppermute | solution.py:358
  106.9 5.5 %collective-permute-start.9 = (bf16[32,128]{1,0:T(8,128)(2,1)S(1)}, bf16[32,128]{1,0:T(8,128)(2,1)S(1)}, u32[]{:S(2)}, u32[]{:S(2)}) collective-permute-start(bf16[32,128]{1,0:T(8,128)(2,1)S(1)} %get-tuple-element.66), channel_id=1, source_target_pairs={{0,16},{1,17},{2,18},{3,19},{4,20},{5,21},{6,22},{7,23},{8,24},{9,... | collective-permute-start | bytes 24584 | tf_op jit(solution)/shard_map/ppermute | solution.py:358
  112.4 4.3 %collective-permute-start.11 = (bf16[16,128]{1,0:T(8,128)(2,1)S(1)}, bf16[16,128]{1,0:T(8,128)(2,1)S(1)}, u32[]{:S(2)}, u32[]{:S(2)}) collective-permute-start(bf16[16,128]{1,0:T(8,128)(2,1)S(1)} %get-tuple-element.69), channel_id=1, source_target_pairs={{0,1},{1,0},{2,3},{3,2},{4,5},{5,4},{6,7},{7,6},{8,9},{9,8},{10,11... | collective-permute-start | bytes 12296 | tf_op jit(solution)/shard_map/ppermute | solution.py:358

commit v3 on v2

--- a/solution.py
+++ b/solution.py
@@ -279,35 +279,47 @@
     )(*blocks)
 
 
-def ungroup_kernel(parts_ref, *refs):
+def ungroup_kernel(parts_ref, keep_ref, away_ref):
     total = jnp.sum(parts_ref[...].astype(f32), axis=0)
-    for m in range(4):
-        rows = [total[s, k, 8 * i + 2 * m : 8 * i + 2 * m + 2] for s in range(2) for i in range(4) for k in range(8)]
-        refs[m][...] = jnp.concatenate(rows, axis=0).astype(bf)
+    for b, ref in enumerate((keep_ref, away_ref)):
+        rows = [
+            total[s, k, 8 * i + 4 * c + 2 * b : 8 * i + 4 * c + 2 * b + 2]
+            for c in range(2) for s in range(2) for i in range(4) for k in range(8)
+        ]
+        ref[...] = jnp.concatenate(rows, axis=0).astype(bf)
 
 
 def ungroup(parts):
     return pl.pallas_call(
         ungroup_kernel,
-        out_shape=[shape_of(128, 128)] * 4,
+        out_shape=[shape_of(256, 128)] * 2,
         compiler_params=SMALL,
         cost_estimate=cost(0, 1),
     )(parts)
 
 
-def quarter_kernel(*refs):
-    total = sum(ref[...].astype(f32) for ref in refs[:4])
+def halve_kernel(a_ref, b_ref, keep_ref, away_ref):
+    total = a_ref[...].astype(f32) + b_ref[...].astype(f32)
+    keep_ref[...] = total[0:128].astype(bf)
+    away_ref[...] = total[128:256].astype(bf)
+
+
+def halve(*blocks):
+    return pl.pallas_call(
+        halve_kernel, out_shape=[shape_of(128, 128)] * 2, compiler_params=SMALL, cost_estimate=cost(0, 0.1)
+    )(*blocks)
+
+
+def quarter_kernel(a_ref, b_ref, *refs):
+    total = a_ref[...].astype(f32) + b_ref[...].astype(f32)
     for m in range(4):
         both = [total[i : i + 16] for i in (16 * m, 64 + 16 * m)]
-        refs[4 + m][...] = jnp.concatenate(both, axis=0).astype(bf)
+        refs[m][...] = jnp.concatenate(both, axis=0).astype(bf)
 
 
 def quarter(*blocks):
     return pl.pallas_call(
-        quarter_kernel,
-        out_shape=[shape_of(32, 128)] * 4,
-        compiler_params=SMALL,
-        cost_estimate=cost(0, 0.1),
+        quarter_kernel, out_shape=[shape_of(32, 128)] * 4, compiler_params=SMALL, cost_estimate=cost(0, 0.1)
     )(*blocks)
 
 
@@ -383,12 +395,14 @@
     )
     parts = exchange(d)
     dq, down = own_grads(qs, gs, delta, lse, dqt, own)
-    parts = ungroup(parts)
+    keep, away = ungroup(parts)
     own_parts = exchange(down)
-    parts = quarter(parts[0], *[from_partner(parts[m], 2 * m) for m in (1, 2, 3)])
+    keep, away = halve(keep, from_partner(away, 2))
+    parts = quarter(keep, from_partner(away, 4))
     mine, other = sides(parts[0], *[from_partner(parts[m], 8 * m) for m in (1, 2, 3)])
+    key, value = finish_own(own_parts)
+    mine, key = lax.optimization_barrier((mine, key))
     block_key, block_value = finish_pack(mine, from_partner(other, 1))
-    key, value = finish_own(own_parts)
     return dq[None], key[None], value[None], pdq, block_key, block_value
 
 

time: 121 us -> 123 us (1.017)
  starting transfers between devices: 49.3 us -> 51.3 us
    ppermute x12 -> x11, starting transfers between devices: 30.7 us -> 32.6 us  [from_partner(): return lax.ppermute(block, 'resp', [(i, i ^ mask) for i in range(32)])]
    ppermute x12 -> x11, waiting for transfers between devices: 15.3 us -> 16.5 us  [from_partner(): return lax.ppermute(block, 'resp', [(i, i ^ mask) for i in range(32)])]
  transfers between devices with their start and end apart: 16 -> 15, of which waited for: 12 -> 11; matrix products, arithmetic and copies ran while one was open for 0% -> 0% of each run, Pallas kernels for 23% -> 23%
where the time goes in v3:
time: 123 us; the launch traced here: 122 us
  starting transfers between devices  51.3 us (42%)
  Pallas kernels  42.4 us (34%)
  waiting for transfers between devices  25.4 us (21%)
  between operations  2 us (2%)
    ppermute x11, starting transfers between devices, from_partner(): return lax.ppermute(block, 'resp', [(i, i ^ mask) for i in range(32)])  32.6 us
    all_to_all x4, starting transfers between devices, exchange(): return lax.all_to_all(blocks, 'ctx', 0, 0, tiled=True)  18.7 us
    ppermute x11, waiting for transfers between devices, from_partner(): return lax.ppermute(block, 'resp', [(i, i ^ mask) for i in range(32)])  16.5 us
    pallas_call x1, Pallas kernels, own_grads(): pl.pallas_call(functools.partial(own_grads_kernel, CH), grid=(4,), in_spe...  13.4 us
    pallas_call x1, Pallas kernels, prefix(): pl.pallas_call(functools.partial(prefix_kernel, HP), grid=(4 // HP,), in_...  10.5 us
    all_to_all x4, waiting for transfers between devices, exchange(): return lax.all_to_all(blocks, 'ctx', 0, 0, tiled=True)  8.95 us
    pallas_call x1, Pallas kernels, own_stats(): pl.pallas_call(own_stats_kernel, grid=(4,), in_specs=[per_head(1024, 128)...  8.06 us
    pallas_call x1, Pallas kernels, prepare(): pl.pallas_call(prepare_kernel, grid=(4,), in_specs=[SMEM, wide(128), wide...  4.19 us
  transfers between devices with their start and end apart: 15, of which 11 were waited for; matrix products, arithmetic and copies ran while one was open for 0% of the time, Pallas kernels for 23%

profile of v3, /device:TPU:1, one launch (start us, length us, event | category | flops | bytes accessed | tf_op | source)
XLA Modules:
  0.0 122.0 jit_solution(16796914219052240970)
XLA Ops:
  0.6 3.0 %shard_map.172 = (bf16[8,1024,128]{2,1,0:T(8,128)(2,1)}, bf16[16,128]{1,0:T(8,128)(2,1)}) custom-call(bf16[128,512]{1,0:T(8,128)(2,1)} %bitcast.11, bf16[128,512]{1,0:T(8,128)(2,1)} %bitcast.12, bf16[2,512]{1,0:T(2,128)(2,1)} %pack_key_ref.1, bf16[2,512]{1,0:T(2,128)(2,1)} %pack_value_ref.1), custom_call_target="tpu_custom_call" | custom-call | bytes 2097152 | tf_op jit(solution)/shard_map/pallas_call | solution.py:253
  3.7 5.9 %all-to-all-start.1 = ((bf16[8,1024,128]{2,1,0:T(8,128)(2,1)}), bf16[8,1024,128]{2,1,0:T(8,128)(2,1)S(1)}, u32[]{:S(2)}, u32[]{:S(2)}) async-start(bf16[8,1024,128]{2,1,0:T(8,128)(2,1)} %get-tuple-element.51), calls=%async_computation.1 | async-start | bytes 4194304 | tf_op jit(solution)/shard_map/all_to_all | solution.py:374
  9.5 1.7 %collective-permute-start = (bf16[16,128]{1,0:T(8,128)(2,1)S(1)}, bf16[16,128]{1,0:T(8,128)(2,1)S(1)}, u32[]{:S(2)}, u32[]{:S(2)}) collective-permute-start(bf16[16,128]{1,0:T(8,128)(2,1)S(1)} %copy-done.2), channel_id=1, source_target_pairs={{0,2},{1,3},{2,0},{3,1},{4,6},{5,7},{6,4},{7,5},{8,10},{9,11},{10,... | collective-permute-start | bytes 12296 | tf_op jit(solution)/shard_map/ppermute | solution.py:370
  12.3 3.0 %collective-permute-start.1 = (bf16[32,128]{1,0:T(8,128)(2,1)S(1)}, bf16[32,128]{1,0:T(8,128)(2,1)S(1)}, u32[]{:S(2)}, u32[]{:S(2)}) collective-permute-start(bf16[32,128]{1,0:T(8,128)(2,1)S(1)} %pad_maximum_fusion.2), channel_id=1, source_target_pairs={{0,4},{1,5},{2,6},{3,7},{4,0},{5,1},{6,2},{7,3},{8,12},{9,13},{10,... | collective-permute-start | bytes 24584 | tf_op jit(solution)/shard_map/ppermute | solution.py:370
  16.6 6.1 %collective-permute-start.2 = (bf16[64,128]{1,0:T(8,128)(2,1)S(1)}, bf16[64,128]{1,0:T(8,128)(2,1)S(1)}, u32[]{:S(2)}, u32[]{:S(2)}) collective-permute-start(bf16[64,128]{1,0:T(8,128)(2,1)S(1)} %pad_maximum_fusion.1), channel_id=1, source_target_pairs={{0,8},{1,9},{2,10},{3,11},{4,12},{5,13},{6,14},{7,15},{8,0},{9,1},... | collective-permute-start | bytes 49160 | tf_op jit(solution)/shard_map/ppermute | solution.py:370
  23.9 2.6 %collective-permute-start.3 = (bf16[128,128]{1,0:T(8,128)(2,1)S(1)}, bf16[128,128]{1,0:T(8,128)(2,1)S(1)}, u32[]{:S(2)}, u32[]{:S(2)}) collective-permute-start(bf16[128,128]{1,0:T(8,128)(2,1)S(1)} %pad_maximum_fusion.refs_0_), channel_id=1, source_target_pairs={{0,16},{1,17},{2,18},{3,19},{4,20},{5,21},{6,22},{7,23},{8,24},{9,... | collective-permute-start | bytes 98312 | tf_op jit(solution)/shard_map/ppermute | solution.py:370
  27.2 4.2 %shard_map.173 = (bf16[4,1024,128]{2,1,0:T(8,128)(2,1)}, bf16[4,1024,128]{2,1,0:T(8,128)(2,1)}, f32[4,8,1024]{2,1,0:T(8,128)}) custom-call(s32[1]{0:T(128)S(6)} %copy.19.len_ref, bf16[128,4096]{1,0:T(8,128)(2,1)} %bitcast.8, bf16[128,4096]{1,0:T(8,128)(2,1)} %bitcast.9, bf16[128,4096]{1,0:T(8,128)(2,1)} %bitcast.10), custom_call_target="tpu_custom_call" | custom-call | flops 100000000 | bytes 5242880 | tf_op jit(solution)/shard_map/pallas_call | solution.py:174
  32.2 4.4 %all-to-all-done.1.k_ref.v_ref = bf16[8,1024,128]{2,1,0:T(8,128)(2,1)S(1)} async-done(((bf16[8,1024,128]{2,1,0:T(8,128)(2,1)}), bf16[8,1024,128]{2,1,0:T(8,128)(2,1)S(1)}, u32[]{:S(2)}, u32[]{:S(2)}) %all-to-all-start.1) | async-done | bytes 2097184 | tf_op jit(solution)/shard_map/all_to_all | solution.py:374
  36.6 5.4 %all-to-all-start = ((bf16[8,8,32,128]{3,2,1,0:T(8,128)(2,1)}), bf16[8,8,32,128]{3,2,1,0:T(8,128)(2,1)S(1)}, u32[]{:S(2)}, u32[]{:S(2)}) async-start(bf16[8,8,32,128]{3,2,1,0:T(8,128)(2,1)} %shard_map.174), calls=%async_computation | async-start | bytes 1048576 | tf_op jit(solution)/shard_map/all_to_all | solution.py:374
  42.1 8.1 %shard_map.175.st_ref = f32[4,16,1024]{2,1,0:T(8,128)} custom-call(bf16[4,1024,128]{2,1,0:T(8,128)(2,1)} %get-tuple-element.47.qs_ref, bf16[8,1024,128]{2,1,0:T(8,128)(2,1)} %copy-done), custom_call_target="tpu_custom_call" | custom-call | flops 1200000000 | bytes 6291456 | tf_op jit(solution)/shard_map/pallas_call | solution.py:186
  50.1 2.1 %all-to-all-done.km_ref = bf16[8,8,32,128]{3,2,1,0:T(8,128)(2,1)S(1)} async-done(((bf16[8,8,32,128]{3,2,1,0:T(8,128)(2,1)}), bf16[8,8,32,128]{3,2,1,0:T(8,128)(2,1)S(1)}, u32[]{:S(2)}, u32[]{:S(2)}) %all-to-all-start) | async-done | bytes 524320 | tf_op jit(solution)/shard_map/all_to_all | solution.py:374
  55.5 10.5 %shard_map.176 = (bf16[8,2,8,32,128]{4,3,2,1,0:T(8,128)(2,1)}, f32[4,128,1024]{2,1,0:T(8,128)}, f32[4,8,1024]{2,1,0:T(8,128)}, bf16[2,4096]{1,0:T(2,128)(2,1)}) custom-call(s32[1]{0:T(128)S(6)} %copy.20.prompt_ref, s32[3]{0:T(128)} %offset_ref.1, bf16[4,1024,128]{2,1,0:T(8,128)(2,1)} %get-tuple-element.47.qs_ref, ...), custom_call_target="tpu_custom_call" | custom-call | flops 2700000000 | bytes 8388608 | tf_op jit(solution)/shard_map/pallas_call | solution.py:204
  65.9 3.8 %all-to-all-start.2 = ((bf16[8,2,8,32,128]{4,3,2,1,0:T(8,128)(2,1)}), bf16[8,2,8,32,128]{4,3,2,1,0:T(8,128)(2,1)S(1)}, u32[]{:S(2)}, u32[]{:S(2)}) async-start(bf16[8,2,8,32,128]{4,3,2,1,0:T(8,128)(2,1)} %get-tuple-element.57), calls=%async_computation.2 | async-start | bytes 2097152 | tf_op jit(solution)/shard_map/all_to_all | solution.py:374
  69.7 13.4 %shard_map.177 = (bf16[128,4096]{1,0:T(8,128)(2,1)}, bf16[8,1024,128]{2,1,0:T(8,128)(2,1)}) custom-call(bf16[4,1024,128]{2,1,0:T(8,128)(2,1)} %get-tuple-element.47.qs_ref, bf16[4,1024,128]{2,1,0:T(8,128)(2,1)} %get-tuple-element.48.gs_ref, f32[4,8,1024]{2,1,0:T(8,128)} %get-tuple-element.49.dl_ref, f32[4,8,1024]{2,1,0:T(8,128)} %get-tuple-element.54.lse_ref, ...), custom_call_target="tpu_custom_call" | custom-call | flops 5400000000 | bytes 10485760 | tf_op jit(solution)/shard_map/pallas_call | solution.py:218
  83.1 2.4 %all-to-all-done.2.parts_ref = bf16[8,2,8,32,128]{4,3,2,1,0:T(8,128)(2,1)S(1)} async-done(((bf16[8,2,8,32,128]{4,3,2,1,0:T(8,128)(2,1)}), bf16[8,2,8,32,128]{4,3,2,1,0:T(8,128)(2,1)S(1)}, u32[]{:S(2)}, u32[]{:S(2)}) %all-to-all-start.2) | async-done | bytes 1048608 | tf_op jit(solution)/shard_map/all_to_all | solution.py:374
  85.5 3.6 %all-to-all-start.3 = ((bf16[8,1024,128]{2,1,0:T(8,128)(2,1)}), bf16[8,1024,128]{2,1,0:T(8,128)(2,1)S(1)}, u32[]{:S(2)}, u32[]{:S(2)}) async-start(bf16[8,1024,128]{2,1,0:T(8,128)(2,1)} %get-tuple-element.67), calls=%async_computation.3 | async-start | bytes 4194304 | tf_op jit(solution)/shard_map/all_to_all | solution.py:374
  89.4 1.7 %collective-permute-start.5 = (bf16[256,128]{1,0:T(8,128)(2,1)S(1)}, bf16[256,128]{1,0:T(8,128)(2,1)S(1)}, u32[]{:S(2)}, u32[]{:S(2)}) collective-permute-start(bf16[256,128]{1,0:T(8,128)(2,1)S(1)} %get-tuple-element.59), channel_id=1, source_target_pairs={{0,2},{1,3},{2,0},{3,1},{4,6},{5,7},{6,4},{7,5},{8,10},{9,11},{10,... | collective-permute-start | bytes 196616 | tf_op jit(solution)/shard_map/ppermute | solution.py:370
  91.1 1.7 %collective-permute-done.5.b_ref = bf16[256,128]{1,0:T(8,128)(2,1)S(1)} collective-permute-done((bf16[256,128]{1,0:T(8,128)(2,1)S(1)}, bf16[256,128]{1,0:T(8,128)(2,1)S(1)}, u32[]{:S(2)}, u32[]{:S(2)}) %collective-permute-start.5) | collective-permute-done | bytes 65568 | tf_op jit(solution)/shard_map/ppermute | solution.py:370
  92.8 3.1 %collective-permute-start.6 = (bf16[128,128]{1,0:T(8,128)(2,1)S(1)}, bf16[128,128]{1,0:T(8,128)(2,1)S(1)}, u32[]{:S(2)}, u32[]{:S(2)}) collective-permute-start(bf16[128,128]{1,0:T(8,128)(2,1)S(1)} %get-tuple-element.61), channel_id=1, source_target_pairs={{0,4},{1,5},{2,6},{3,7},{4,0},{5,1},{6,2},{7,3},{8,12},{9,13},{10,... | collective-permute-start | bytes 98312 | tf_op jit(solution)/shard_map/ppermute | solution.py:370
  97.5 6.2 %collective-permute-start.7 = (bf16[32,128]{1,0:T(8,128)(2,1)S(1)}, bf16[32,128]{1,0:T(8,128)(2,1)S(1)}, u32[]{:S(2)}, u32[]{:S(2)}) collective-permute-start(bf16[32,128]{1,0:T(8,128)(2,1)S(1)} %get-tuple-element.63), channel_id=1, source_target_pairs={{0,8},{1,9},{2,10},{3,11},{4,12},{5,13},{6,14},{7,15},{8,0},{9,1},... | collective-permute-start | bytes 24584 | tf_op jit(solution)/shard_map/ppermute | solution.py:370
  103.7 2.7 %collective-permute-start.8 = (bf16[32,128]{1,0:T(8,128)(2,1)S(1)}, bf16[32,128]{1,0:T(8,128)(2,1)S(1)}, u32[]{:S(2)}, u32[]{:S(2)}) collective-permute-start(bf16[32,128]{1,0:T(8,128)(2,1)S(1)} %get-tuple-element.64), channel_id=1, source_target_pairs={{0,16},{1,17},{2,18},{3,19},{4,20},{5,21},{6,22},{7,23},{8,24},{9,... | collective-permute-start | bytes 24584 | tf_op jit(solution)/shard_map/ppermute | solution.py:370
  106.5 2.0 %collective-permute-done.8.c_ref = bf16[32,128]{1,0:T(8,128)(2,1)S(1)} collective-permute-done((bf16[32,128]{1,0:T(8,128)(2,1)S(1)}, bf16[32,128]{1,0:T(8,128)(2,1)S(1)}, u32[]{:S(2)}, u32[]{:S(2)}) %collective-permute-start.8) | collective-permute-done | bytes 8224 | tf_op jit(solution)/shard_map/ppermute | solution.py:370
  108.5 6.8 %collective-permute-done.9.d_ref = bf16[32,128]{1,0:T(8,128)(2,1)S(1)} collective-permute-done((bf16[32,128]{1,0:T(8,128)(2,1)S(1)}, bf16[32,128]{1,0:T(8,128)(2,1)S(1)}, u32[]{:S(2)}, u32[]{:S(2)}) %collective-permute-start.9) | collective-permute-done | bytes 8224 | tf_op jit(solution)/shard_map/ppermute | solution.py:370
  115.3 4.6 %collective-permute-start.10 = (bf16[16,128]{1,0:T(8,128)(2,1)S(1)}, bf16[16,128]{1,0:T(8,128)(2,1)S(1)}, u32[]{:S(2)}, u32[]{:S(2)}) collective-permute-start(bf16[16,128]{1,0:T(8,128)(2,1)S(1)} %get-tuple-element.73), channel_id=1, source_target_pairs={{0,1},{1,0},{2,3},{3,2},{4,5},{5,4},{6,7},{7,6},{8,9},{9,8},{10,11... | collective-permute-start | bytes 12296 | tf_op jit(solution)/shard_map/ppermute | solution.py:370
  (29 shorter events, 11.1 us)
Async XLA Ops:
  3.7 5.9 %copy-start.2 = (bf16[16,128]{1,0:T(8,128)(2,1)S(1)}, bf16[16,128]{1,0:T(8,128)(2,1)}, u32[]{:S(2)}) copy-start(bf16[16,128]{1,0:T(8,128)(2,1)} %get-tuple-element.41) | copy-start | bytes 12292
  3.7 33.0 %all-to-all-start.1 = ((bf16[8,1024,128]{2,1,0:T(8,128)(2,1)}), bf16[8,1024,128]{2,1,0:T(8,128)(2,1)S(1)}, u32[]{:S(2)}, u32[]{:S(2)}) async-start(bf16[8,1024,128]{2,1,0:T(8,128)(2,1)} %get-tuple-element.51), calls=%async_computation.1 | async-start | bytes 4194304 | tf_op jit(solution)/shard_map/all_to_all | solution.py:374
  9.5 2.7 %collective-permute-start = (bf16[16,128]{1,0:T(8,128)(2,1)S(1)}, bf16[16,128]{1,0:T(8,128)(2,1)S(1)}, u32[]{:S(2)}, u32[]{:S(2)}) collective-permute-start(bf16[16,128]{1,0:T(8,128)(2,1)S(1)} %copy-done.2), channel_id=1, source_target_pairs={{0,2},{1,3},{2,0},{3,1},{4,6},{5,7},{6,4},{7,5},{8,10},{9,11},{10,... | collective-permute-start | bytes 12296 | tf_op jit(solution)/shard_map/ppermute | solution.py:370
  12.3 4.3 %collective-permute-start.1 = (bf16[32,128]{1,0:T(8,128)(2,1)S(1)}, bf16[32,128]{1,0:T(8,128)(2,1)S(1)}, u32[]{:S(2)}, u32[]{:S(2)}) collective-permute-start(bf16[32,128]{1,0:T(8,128)(2,1)S(1)} %pad_maximum_fusion.2), channel_id=1, source_target_pairs={{0,4},{1,5},{2,6},{3,7},{4,0},{5,1},{6,2},{7,3},{8,12},{9,13},{10,... | collective-permute-start | bytes 24584 | tf_op jit(solution)/shard_map/ppermute | solution.py:370
  16.6 7.3 %collective-permute-start.2 = (bf16[64,128]{1,0:T(8,128)(2,1)S(1)}, bf16[64,128]{1,0:T(8,128)(2,1)S(1)}, u32[]{:S(2)}, u32[]{:S(2)}) collective-permute-start(bf16[64,128]{1,0:T(8,128)(2,1)S(1)} %pad_maximum_fusion.1), channel_id=1, source_target_pairs={{0,8},{1,9},{2,10},{3,11},{4,12},{5,13},{6,14},{7,15},{8,0},{9,1},... | collective-permute-start | bytes 49160 | tf_op jit(solution)/shard_map/ppermute | solution.py:370
  23.9 7.5 %collective-permute-start.3 = (bf16[128,128]{1,0:T(8,128)(2,1)S(1)}, bf16[128,128]{1,0:T(8,128)(2,1)S(1)}, u32[]{:S(2)}, u32[]{:S(2)}) collective-permute-start(bf16[128,128]{1,0:T(8,128)(2,1)S(1)} %pad_maximum_fusion.refs_0_), channel_id=1, source_target_pairs={{0,16},{1,17},{2,18},{3,19},{4,20},{5,21},{6,22},{7,23},{8,24},{9,... | collective-permute-start | bytes 98312 | tf_op jit(solution)/shard_map/ppermute | solution.py:370
  36.6 5.4 %copy-start = (bf16[8,1024,128]{2,1,0:T(8,128)(2,1)}, bf16[8,1024,128]{2,1,0:T(8,128)(2,1)S(1)}, u32[]{:S(2)}) copy-start(bf16[8,1024,128]{2,1,0:T(8,128)(2,1)S(1)} %all-to-all-done.1.k_ref.v_ref) | copy-start | bytes 6291460
  36.6 15.6 %all-to-all-start = ((bf16[8,8,32,128]{3,2,1,0:T(8,128)(2,1)}), bf16[8,8,32,128]{3,2,1,0:T(8,128)(2,1)S(1)}, u32[]{:S(2)}, u32[]{:S(2)}) async-start(bf16[8,8,32,128]{3,2,1,0:T(8,128)(2,1)} %shard_map.174), calls=%async_computation | async-start | bytes 1048576 | tf_op jit(solution)/shard_map/all_to_all | solution.py:374
  52.2 2.4 %copy-start.1 = (bf16[8,8,32,128]{3,2,1,0:T(8,128)(2,1)}, bf16[8,8,32,128]{3,2,1,0:T(8,128)(2,1)S(1)}, u32[]{:S(2)}) copy-start(bf16[8,8,32,128]{3,2,1,0:T(8,128)(2,1)S(1)} %all-to-all-done.km_ref) | copy-start | bytes 1572868
  52.3 2.4 %collective-permute-start.4 = (bf16[8,8,32,128]{3,2,1,0:T(8,128)(2,1)S(1)}, bf16[8,8,32,128]{3,2,1,0:T(8,128)(2,1)S(1)}, u32[]{:S(2)}, u32[]{:S(2)}) collective-permute-start(bf16[8,8,32,128]{3,2,1,0:T(8,128)(2,1)S(1)} %all-to-all-done.km_ref), channel_id=1, source_target_pairs={{0,1},{1,0},{2,3},{3,2},{4,5},{5,4},{6,7},{7,6},{8,9},{9,8},{10,11... | collective-permute-start | bytes 1572872 | tf_op jit(solution)/shard_map/ppermute | solution.py:370
  54.6 0.8 copy-start.3
  65.9 19.6 %all-to-all-start.2 = ((bf16[8,2,8,32,128]{4,3,2,1,0:T(8,128)(2,1)}), bf16[8,2,8,32,128]{4,3,2,1,0:T(8,128)(2,1)S(1)}, u32[]{:S(2)}, u32[]{:S(2)}) async-start(bf16[8,2,8,32,128]{4,3,2,1,0:T(8,128)(2,1)} %get-tuple-element.57), calls=%async_computation.2 | async-start | bytes 2097152 | tf_op jit(solution)/shard_map/all_to_all | solution.py:374
  85.5 34.3 %all-to-all-start.3 = ((bf16[8,1024,128]{2,1,0:T(8,128)(2,1)}), bf16[8,1024,128]{2,1,0:T(8,128)(2,1)S(1)}, u32[]{:S(2)}, u32[]{:S(2)}) async-start(bf16[8,1024,128]{2,1,0:T(8,128)(2,1)} %get-tuple-element.67), calls=%async_computation.3 | async-start | bytes 4194304 | tf_op jit(solution)/shard_map/all_to_all | solution.py:374
  89.4 3.4 %collective-permute-start.5 = (bf16[256,128]{1,0:T(8,128)(2,1)S(1)}, bf16[256,128]{1,0:T(8,128)(2,1)S(1)}, u32[]{:S(2)}, u32[]{:S(2)}) collective-permute-start(bf16[256,128]{1,0:T(8,128)(2,1)S(1)} %get-tuple-element.59), channel_id=1, source_target_pairs={{0,2},{1,3},{2,0},{3,1},{4,6},{5,7},{6,4},{7,5},{8,10},{9,11},{10,... | collective-permute-start | bytes 196616 | tf_op jit(solution)/shard_map/ppermute | solution.py:370
  92.8 4.7 %collective-permute-start.6 = (bf16[128,128]{1,0:T(8,128)(2,1)S(1)}, bf16[128,128]{1,0:T(8,128)(2,1)S(1)}, u32[]{:S(2)}, u32[]{:S(2)}) collective-permute-start(bf16[128,128]{1,0:T(8,128)(2,1)S(1)} %get-tuple-element.61), channel_id=1, source_target_pairs={{0,4},{1,5},{2,6},{3,7},{4,0},{5,1},{6,2},{7,3},{8,12},{9,13},{10,... | collective-permute-start | bytes 98312 | tf_op jit(solution)/shard_map/ppermute | solution.py:370
  97.5 9.0 %collective-permute-start.7 = (bf16[32,128]{1,0:T(8,128)(2,1)S(1)}, bf16[32,128]{1,0:T(8,128)(2,1)S(1)}, u32[]{:S(2)}, u32[]{:S(2)}) collective-permute-start(bf16[32,128]{1,0:T(8,128)(2,1)S(1)} %get-tuple-element.63), channel_id=1, source_target_pairs={{0,8},{1,9},{2,10},{3,11},{4,12},{5,13},{6,14},{7,15},{8,0},{9,1},... | collective-permute-start | bytes 24584 | tf_op jit(solution)/shard_map/ppermute | solution.py:370
  103.7 4.8 %collective-permute-start.8 = (bf16[32,128]{1,0:T(8,128)(2,1)S(1)}, bf16[32,128]{1,0:T(8,128)(2,1)S(1)}, u32[]{:S(2)}, u32[]{:S(2)}) collective-permute-start(bf16[32,128]{1,0:T(8,128)(2,1)S(1)} %get-tuple-element.64), channel_id=1, source_target_pairs={{0,16},{1,17},{2,18},{3,19},{4,20},{5,21},{6,22},{7,23},{8,24},{9,... | collective-permute-start | bytes 24584 | tf_op jit(solution)/shard_map/ppermute | solution.py:370
  106.4 8.9 %collective-permute-start.9 = (bf16[32,128]{1,0:T(8,128)(2,1)S(1)}, bf16[32,128]{1,0:T(8,128)(2,1)S(1)}, u32[]{:S(2)}, u32[]{:S(2)}) collective-permute-start(bf16[32,128]{1,0:T(8,128)(2,1)S(1)} %get-tuple-element.65), channel_id=1, source_target_pairs={{0,24},{1,25},{2,26},{3,27},{4,28},{5,29},{6,30},{7,31},{8,16},{9,... | collective-permute-start | bytes 24584 | tf_op jit(solution)/shard_map/ppermute | solution.py:370
  115.3 6.1 %collective-permute-start.10 = (bf16[16,128]{1,0:T(8,128)(2,1)S(1)}, bf16[16,128]{1,0:T(8,128)(2,1)S(1)}, u32[]{:S(2)}, u32[]{:S(2)}) collective-permute-start(bf16[16,128]{1,0:T(8,128)(2,1)S(1)} %get-tuple-element.73), channel_id=1, source_target_pairs={{0,1},{1,0},{2,3},{3,2},{4,5},{5,4},{6,7},{7,6},{8,9},{9,8},{10,11... | collective-permute-start | bytes 12296 | tf_op jit(solution)/shard_map/ppermute | solution.py:370

commit v4 on v2

--- a/solution.py
+++ b/solution.py
@@ -387,8 +387,9 @@
     own_parts = exchange(down)
     parts = quarter(parts[0], *[from_partner(parts[m], 2 * m) for m in (1, 2, 3)])
     mine, other = sides(parts[0], *[from_partner(parts[m], 8 * m) for m in (1, 2, 3)])
+    key, value = finish_own(own_parts)
+    mine, key = lax.optimization_barrier((mine, key))
     block_key, block_value = finish_pack(mine, from_partner(other, 1))
-    key, value = finish_own(own_parts)
     return dq[None], key[None], value[None], pdq, block_key, block_value
 
 

time: 121 us -> 120 us (level)
  transfers between devices with their start and end apart: 16 -> 16, of which waited for: 12 -> 12; matrix products, arithmetic and copies ran while one was open for 0% -> 0% of each run, Pallas kernels for 23% -> 24%
where the time goes in v4:
time: 120 us; the launch traced here: 118 us
  starting transfers between devices  49.3 us (41%)
  Pallas kernels  42.4 us (35%)
  waiting for transfers between devices  23.9 us (20%)
  between operations  2 us (2%)
    ppermute x12, starting transfers between devices, from_partner(): return lax.ppermute(block, 'resp', [(i, i ^ mask) for i in range(32)])  30.7 us
    all_to_all x4, starting transfers between devices, exchange(): return lax.all_to_all(blocks, 'ctx', 0, 0, tiled=True)  18.7 us
    ppermute x12, waiting for transfers between devices, from_partner(): return lax.ppermute(block, 'resp', [(i, i ^ mask) for i in range(32)])  14.5 us
    pallas_call x1, Pallas kernels, own_grads(): pl.pallas_call(functools.partial(own_grads_kernel, CH), grid=(4,), in_spe...  13.4 us
    pallas_call x1, Pallas kernels, prefix(): pl.pallas_call(functools.partial(prefix_kernel, HP), grid=(4 // HP,), in_...  10.5 us
    all_to_all x4, waiting for transfers between devices, exchange(): return lax.all_to_all(blocks, 'ctx', 0, 0, tiled=True)  9.37 us
    pallas_call x1, Pallas kernels, own_stats(): pl.pallas_call(own_stats_kernel, grid=(4,), in_specs=[per_head(1024, 128)...  8.06 us
    pallas_call x1, Pallas kernels, prepare(): pl.pallas_call(prepare_kernel, grid=(4,), in_specs=[SMEM, wide(128), wide...  4.19 us
  transfers between devices with their start and end apart: 16, of which 12 were waited for; matrix products, arithmetic and copies ran while one was open for 0% of the time, Pallas kernels for 24%

profile of v4, /device:TPU:1, one launch (start us, length us, event | category | flops | bytes accessed | tf_op | source)
XLA Modules:
  0.0 118.5 jit_solution(17349683633042118040)
XLA Ops:
  0.6 3.0 %shard_map.172 = (bf16[8,1024,128]{2,1,0:T(8,128)(2,1)}, bf16[16,128]{1,0:T(8,128)(2,1)}) custom-call(bf16[128,512]{1,0:T(8,128)(2,1)} %bitcast.11, bf16[128,512]{1,0:T(8,128)(2,1)} %bitcast.12, bf16[2,512]{1,0:T(2,128)(2,1)} %pack_key_ref.1, bf16[2,512]{1,0:T(2,128)(2,1)} %pack_value_ref.1), custom_call_target="tpu_custom_call" | custom-call | bytes 2097152 | tf_op jit(solution)/shard_map/pallas_call | solution.py:253
  3.7 5.9 %all-to-all-start.1 = ((bf16[8,1024,128]{2,1,0:T(8,128)(2,1)}), bf16[8,1024,128]{2,1,0:T(8,128)(2,1)S(1)}, u32[]{:S(2)}, u32[]{:S(2)}) async-start(bf16[8,1024,128]{2,1,0:T(8,128)(2,1)} %get-tuple-element.51), calls=%async_computation.1 | async-start | bytes 4194304 | tf_op jit(solution)/shard_map/all_to_all | solution.py:362
  9.5 1.7 %collective-permute-start = (bf16[16,128]{1,0:T(8,128)(2,1)S(1)}, bf16[16,128]{1,0:T(8,128)(2,1)S(1)}, u32[]{:S(2)}, u32[]{:S(2)}) collective-permute-start(bf16[16,128]{1,0:T(8,128)(2,1)S(1)} %copy-done.2), channel_id=1, source_target_pairs={{0,2},{1,3},{2,0},{3,1},{4,6},{5,7},{6,4},{7,5},{8,10},{9,11},{10,... | collective-permute-start | bytes 12296 | tf_op jit(solution)/shard_map/ppermute | solution.py:358
  12.3 3.0 %collective-permute-start.1 = (bf16[32,128]{1,0:T(8,128)(2,1)S(1)}, bf16[32,128]{1,0:T(8,128)(2,1)S(1)}, u32[]{:S(2)}, u32[]{:S(2)}) collective-permute-start(bf16[32,128]{1,0:T(8,128)(2,1)S(1)} %pad_maximum_fusion.2), channel_id=1, source_target_pairs={{0,4},{1,5},{2,6},{3,7},{4,0},{5,1},{6,2},{7,3},{8,12},{9,13},{10,... | collective-permute-start | bytes 24584 | tf_op jit(solution)/shard_map/ppermute | solution.py:358
  16.6 6.1 %collective-permute-start.2 = (bf16[64,128]{1,0:T(8,128)(2,1)S(1)}, bf16[64,128]{1,0:T(8,128)(2,1)S(1)}, u32[]{:S(2)}, u32[]{:S(2)}) collective-permute-start(bf16[64,128]{1,0:T(8,128)(2,1)S(1)} %pad_maximum_fusion.1), channel_id=1, source_target_pairs={{0,8},{1,9},{2,10},{3,11},{4,12},{5,13},{6,14},{7,15},{8,0},{9,1},... | collective-permute-start | bytes 49160 | tf_op jit(solution)/shard_map/ppermute | solution.py:358
  23.9 2.6 %collective-permute-start.3 = (bf16[128,128]{1,0:T(8,128)(2,1)S(1)}, bf16[128,128]{1,0:T(8,128)(2,1)S(1)}, u32[]{:S(2)}, u32[]{:S(2)}) collective-permute-start(bf16[128,128]{1,0:T(8,128)(2,1)S(1)} %pad_maximum_fusion.refs_0_), channel_id=1, source_target_pairs={{0,16},{1,17},{2,18},{3,19},{4,20},{5,21},{6,22},{7,23},{8,24},{9,... | collective-permute-start | bytes 98312 | tf_op jit(solution)/shard_map/ppermute | solution.py:358
  27.2 4.2 %shard_map.173 = (bf16[4,1024,128]{2,1,0:T(8,128)(2,1)}, bf16[4,1024,128]{2,1,0:T(8,128)(2,1)}, f32[4,8,1024]{2,1,0:T(8,128)}) custom-call(s32[1]{0:T(128)S(6)} %copy.19.len_ref, bf16[128,4096]{1,0:T(8,128)(2,1)} %bitcast.8, bf16[128,4096]{1,0:T(8,128)(2,1)} %bitcast.9, bf16[128,4096]{1,0:T(8,128)(2,1)} %bitcast.10), custom_call_target="tpu_custom_call" | custom-call | flops 100000000 | bytes 5242880 | tf_op jit(solution)/shard_map/pallas_call | solution.py:174
  32.2 4.4 %all-to-all-done.1.k_ref.v_ref = bf16[8,1024,128]{2,1,0:T(8,128)(2,1)S(1)} async-done(((bf16[8,1024,128]{2,1,0:T(8,128)(2,1)}), bf16[8,1024,128]{2,1,0:T(8,128)(2,1)S(1)}, u32[]{:S(2)}, u32[]{:S(2)}) %all-to-all-start.1) | async-done | bytes 2097184 | tf_op jit(solution)/shard_map/all_to_all | solution.py:362
  36.6 5.4 %all-to-all-start = ((bf16[8,8,32,128]{3,2,1,0:T(8,128)(2,1)}), bf16[8,8,32,128]{3,2,1,0:T(8,128)(2,1)S(1)}, u32[]{:S(2)}, u32[]{:S(2)}) async-start(bf16[8,8,32,128]{3,2,1,0:T(8,128)(2,1)} %shard_map.174), calls=%async_computation | async-start | bytes 1048576 | tf_op jit(solution)/shard_map/all_to_all | solution.py:362
  42.1 8.1 %shard_map.175.st_ref = f32[4,16,1024]{2,1,0:T(8,128)} custom-call(bf16[4,1024,128]{2,1,0:T(8,128)(2,1)} %get-tuple-element.47.qs_ref, bf16[8,1024,128]{2,1,0:T(8,128)(2,1)} %copy-done), custom_call_target="tpu_custom_call" | custom-call | flops 1200000000 | bytes 6291456 | tf_op jit(solution)/shard_map/pallas_call | solution.py:186
  50.1 2.1 %all-to-all-done.km_ref = bf16[8,8,32,128]{3,2,1,0:T(8,128)(2,1)S(1)} async-done(((bf16[8,8,32,128]{3,2,1,0:T(8,128)(2,1)}), bf16[8,8,32,128]{3,2,1,0:T(8,128)(2,1)S(1)}, u32[]{:S(2)}, u32[]{:S(2)}) %all-to-all-start) | async-done | bytes 524320 | tf_op jit(solution)/shard_map/all_to_all | solution.py:362
  55.5 10.5 %shard_map.176 = (bf16[8,2,8,32,128]{4,3,2,1,0:T(8,128)(2,1)}, f32[4,128,1024]{2,1,0:T(8,128)}, f32[4,8,1024]{2,1,0:T(8,128)}, bf16[2,4096]{1,0:T(2,128)(2,1)}) custom-call(s32[1]{0:T(128)S(6)} %copy.20.prompt_ref, s32[3]{0:T(128)} %offset_ref.1, bf16[4,1024,128]{2,1,0:T(8,128)(2,1)} %get-tuple-element.47.qs_ref, ...), custom_call_target="tpu_custom_call" | custom-call | flops 2700000000 | bytes 8388608 | tf_op jit(solution)/shard_map/pallas_call | solution.py:204
  65.9 3.8 %all-to-all-start.2 = ((bf16[8,2,8,32,128]{4,3,2,1,0:T(8,128)(2,1)}), bf16[8,2,8,32,128]{4,3,2,1,0:T(8,128)(2,1)S(1)}, u32[]{:S(2)}, u32[]{:S(2)}) async-start(bf16[8,2,8,32,128]{4,3,2,1,0:T(8,128)(2,1)} %get-tuple-element.57), calls=%async_computation.2 | async-start | bytes 2097152 | tf_op jit(solution)/shard_map/all_to_all | solution.py:362
  69.7 13.4 %shard_map.177 = (bf16[128,4096]{1,0:T(8,128)(2,1)}, bf16[8,1024,128]{2,1,0:T(8,128)(2,1)}) custom-call(bf16[4,1024,128]{2,1,0:T(8,128)(2,1)} %get-tuple-element.47.qs_ref, bf16[4,1024,128]{2,1,0:T(8,128)(2,1)} %get-tuple-element.48.gs_ref, f32[4,8,1024]{2,1,0:T(8,128)} %get-tuple-element.49.dl_ref, f32[4,8,1024]{2,1,0:T(8,128)} %get-tuple-element.54.lse_ref, ...), custom_call_target="tpu_custom_call" | custom-call | flops 5400000000 | bytes 10485760 | tf_op jit(solution)/shard_map/pallas_call | solution.py:218
  83.1 2.4 %all-to-all-done.2.parts_ref = bf16[8,2,8,32,128]{4,3,2,1,0:T(8,128)(2,1)S(1)} async-done(((bf16[8,2,8,32,128]{4,3,2,1,0:T(8,128)(2,1)}), bf16[8,2,8,32,128]{4,3,2,1,0:T(8,128)(2,1)S(1)}, u32[]{:S(2)}, u32[]{:S(2)}) %all-to-all-start.2) | async-done | bytes 1048608 | tf_op jit(solution)/shard_map/all_to_all | solution.py:362
  85.5 3.6 %all-to-all-start.3 = ((bf16[8,1024,128]{2,1,0:T(8,128)(2,1)}), bf16[8,1024,128]{2,1,0:T(8,128)(2,1)S(1)}, u32[]{:S(2)}, u32[]{:S(2)}) async-start(bf16[8,1024,128]{2,1,0:T(8,128)(2,1)} %get-tuple-element.67), calls=%async_computation.3 | async-start | bytes 4194304 | tf_op jit(solution)/shard_map/all_to_all | solution.py:362
  89.4 1.7 %collective-permute-start.5 = (bf16[128,128]{1,0:T(8,128)(2,1)S(1)}, bf16[128,128]{1,0:T(8,128)(2,1)S(1)}, u32[]{:S(2)}, u32[]{:S(2)}) collective-permute-start(bf16[128,128]{1,0:T(8,128)(2,1)S(1)} %get-tuple-element.59), channel_id=1, source_target_pairs={{0,2},{1,3},{2,0},{3,1},{4,6},{5,7},{6,4},{7,5},{8,10},{9,11},{10,... | collective-permute-start | bytes 98312 | tf_op jit(solution)/shard_map/ppermute | solution.py:358
  91.1 3.0 %collective-permute-start.6 = (bf16[128,128]{1,0:T(8,128)(2,1)S(1)}, bf16[128,128]{1,0:T(8,128)(2,1)S(1)}, u32[]{:S(2)}, u32[]{:S(2)}) collective-permute-start(bf16[128,128]{1,0:T(8,128)(2,1)S(1)} %get-tuple-element.60), channel_id=1, source_target_pairs={{0,4},{1,5},{2,6},{3,7},{4,0},{5,1},{6,2},{7,3},{8,12},{9,13},{10,... | collective-permute-start | bytes 98312 | tf_op jit(solution)/shard_map/ppermute | solution.py:358
  94.1 1.9 %collective-permute-done.6.refs_2_ = bf16[128,128]{1,0:T(8,128)(2,1)S(1)} collective-permute-done((bf16[128,128]{1,0:T(8,128)(2,1)S(1)}, bf16[128,128]{1,0:T(8,128)(2,1)S(1)}, u32[]{:S(2)}, u32[]{:S(2)}) %collective-permute-start.6) | collective-permute-done | bytes 32800 | tf_op jit(solution)/shard_map/ppermute | solution.py:358
  96.1 2.9 %collective-permute-done.7.refs_3_ = bf16[128,128]{1,0:T(8,128)(2,1)S(1)} collective-permute-done((bf16[128,128]{1,0:T(8,128)(2,1)S(1)}, bf16[128,128]{1,0:T(8,128)(2,1)S(1)}, u32[]{:S(2)}, u32[]{:S(2)}) %collective-permute-start.7) | collective-permute-done | bytes 32800 | tf_op jit(solution)/shard_map/ppermute | solution.py:358
  99.0 7.0 %collective-permute-start.10 = (bf16[32,128]{1,0:T(8,128)(2,1)S(1)}, bf16[32,128]{1,0:T(8,128)(2,1)S(1)}, u32[]{:S(2)}, u32[]{:S(2)}) collective-permute-start(bf16[32,128]{1,0:T(8,128)(2,1)S(1)} %get-tuple-element.65), channel_id=1, source_target_pairs={{0,24},{1,25},{2,26},{3,27},{4,28},{5,29},{6,30},{7,31},{8,16},{9,... | collective-permute-start | bytes 24584 | tf_op jit(solution)/shard_map/ppermute | solution.py:358
  107.1 2.4 %collective-permute-done.10.d_ref = bf16[32,128]{1,0:T(8,128)(2,1)S(1)} collective-permute-done((bf16[32,128]{1,0:T(8,128)(2,1)S(1)}, bf16[32,128]{1,0:T(8,128)(2,1)S(1)}, u32[]{:S(2)}, u32[]{:S(2)}) %collective-permute-start.10) | collective-permute-done | bytes 8224 | tf_op jit(solution)/shard_map/ppermute | solution.py:358
  109.5 2.8 %collective-permute-done.8.b_ref = bf16[32,128]{1,0:T(8,128)(2,1)S(1)} collective-permute-done((bf16[32,128]{1,0:T(8,128)(2,1)S(1)}, bf16[32,128]{1,0:T(8,128)(2,1)S(1)}, u32[]{:S(2)}, u32[]{:S(2)}) %collective-permute-start.8) | collective-permute-done | bytes 8224 | tf_op jit(solution)/shard_map/ppermute | solution.py:358
  112.4 3.5 %collective-permute-start.11 = (bf16[16,128]{1,0:T(8,128)(2,1)S(1)}, bf16[16,128]{1,0:T(8,128)(2,1)S(1)}, u32[]{:S(2)}, u32[]{:S(2)}) collective-permute-start(bf16[16,128]{1,0:T(8,128)(2,1)S(1)} %get-tuple-element.73), channel_id=1, source_target_pairs={{0,1},{1,0},{2,3},{3,2},{4,5},{5,4},{6,7},{7,6},{8,9},{9,8},{10,11... | collective-permute-start | bytes 12296 | tf_op jit(solution)/shard_map/ppermute | solution.py:358
  (30 shorter events, 11.0 us)
Async XLA Ops:
  3.7 5.9 %copy-start.2 = (bf16[16,128]{1,0:T(8,128)(2,1)S(1)}, bf16[16,128]{1,0:T(8,128)(2,1)}, u32[]{:S(2)}) copy-start(bf16[16,128]{1,0:T(8,128)(2,1)} %get-tuple-element.41) | copy-start | bytes 12292
  3.7 33.0 %all-to-all-start.1 = ((bf16[8,1024,128]{2,1,0:T(8,128)(2,1)}), bf16[8,1024,128]{2,1,0:T(8,128)(2,1)S(1)}, u32[]{:S(2)}, u32[]{:S(2)}) async-start(bf16[8,1024,128]{2,1,0:T(8,128)(2,1)} %get-tuple-element.51), calls=%async_computation.1 | async-start | bytes 4194304 | tf_op jit(solution)/shard_map/all_to_all | solution.py:362
  9.5 2.7 %collective-permute-start = (bf16[16,128]{1,0:T(8,128)(2,1)S(1)}, bf16[16,128]{1,0:T(8,128)(2,1)S(1)}, u32[]{:S(2)}, u32[]{:S(2)}) collective-permute-start(bf16[16,128]{1,0:T(8,128)(2,1)S(1)} %copy-done.2), channel_id=1, source_target_pairs={{0,2},{1,3},{2,0},{3,1},{4,6},{5,7},{6,4},{7,5},{8,10},{9,11},{10,... | collective-permute-start | bytes 12296 | tf_op jit(solution)/shard_map/ppermute | solution.py:358
  12.3 4.3 %collective-permute-start.1 = (bf16[32,128]{1,0:T(8,128)(2,1)S(1)}, bf16[32,128]{1,0:T(8,128)(2,1)S(1)}, u32[]{:S(2)}, u32[]{:S(2)}) collective-permute-start(bf16[32,128]{1,0:T(8,128)(2,1)S(1)} %pad_maximum_fusion.2), channel_id=1, source_target_pairs={{0,4},{1,5},{2,6},{3,7},{4,0},{5,1},{6,2},{7,3},{8,12},{9,13},{10,... | collective-permute-start | bytes 24584 | tf_op jit(solution)/shard_map/ppermute | solution.py:358
  16.6 7.3 %collective-permute-start.2 = (bf16[64,128]{1,0:T(8,128)(2,1)S(1)}, bf16[64,128]{1,0:T(8,128)(2,1)S(1)}, u32[]{:S(2)}, u32[]{:S(2)}) collective-permute-start(bf16[64,128]{1,0:T(8,128)(2,1)S(1)} %pad_maximum_fusion.1), channel_id=1, source_target_pairs={{0,8},{1,9},{2,10},{3,11},{4,12},{5,13},{6,14},{7,15},{8,0},{9,1},... | collective-permute-start | bytes 49160 | tf_op jit(solution)/shard_map/ppermute | solution.py:358
  23.9 7.5 %collective-permute-start.3 = (bf16[128,128]{1,0:T(8,128)(2,1)S(1)}, bf16[128,128]{1,0:T(8,128)(2,1)S(1)}, u32[]{:S(2)}, u32[]{:S(2)}) collective-permute-start(bf16[128,128]{1,0:T(8,128)(2,1)S(1)} %pad_maximum_fusion.refs_0_), channel_id=1, source_target_pairs={{0,16},{1,17},{2,18},{3,19},{4,20},{5,21},{6,22},{7,23},{8,24},{9,... | collective-permute-start | bytes 98312 | tf_op jit(solution)/shard_map/ppermute | solution.py:358
  36.6 5.4 %copy-start = (bf16[8,1024,128]{2,1,0:T(8,128)(2,1)}, bf16[8,1024,128]{2,1,0:T(8,128)(2,1)S(1)}, u32[]{:S(2)}) copy-start(bf16[8,1024,128]{2,1,0:T(8,128)(2,1)S(1)} %all-to-all-done.1.k_ref.v_ref) | copy-start | bytes 6291460
  36.6 15.6 %all-to-all-start = ((bf16[8,8,32,128]{3,2,1,0:T(8,128)(2,1)}), bf16[8,8,32,128]{3,2,1,0:T(8,128)(2,1)S(1)}, u32[]{:S(2)}, u32[]{:S(2)}) async-start(bf16[8,8,32,128]{3,2,1,0:T(8,128)(2,1)} %shard_map.174), calls=%async_computation | async-start | bytes 1048576 | tf_op jit(solution)/shard_map/all_to_all | solution.py:362
  52.2 2.4 %copy-start.1 = (bf16[8,8,32,128]{3,2,1,0:T(8,128)(2,1)}, bf16[8,8,32,128]{3,2,1,0:T(8,128)(2,1)S(1)}, u32[]{:S(2)}) copy-start(bf16[8,8,32,128]{3,2,1,0:T(8,128)(2,1)S(1)} %all-to-all-done.km_ref) | copy-start | bytes 1572868
  52.3 2.4 %collective-permute-start.4 = (bf16[8,8,32,128]{3,2,1,0:T(8,128)(2,1)S(1)}, bf16[8,8,32,128]{3,2,1,0:T(8,128)(2,1)S(1)}, u32[]{:S(2)}, u32[]{:S(2)}) collective-permute-start(bf16[8,8,32,128]{3,2,1,0:T(8,128)(2,1)S(1)} %all-to-all-done.km_ref), channel_id=1, source_target_pairs={{0,1},{1,0},{2,3},{3,2},{4,5},{5,4},{6,7},{7,6},{8,9},{9,8},{10,11... | collective-permute-start | bytes 1572872 | tf_op jit(solution)/shard_map/ppermute | solution.py:358
  54.6 0.8 copy-start.3
  65.9 19.6 %all-to-all-start.2 = ((bf16[8,2,8,32,128]{4,3,2,1,0:T(8,128)(2,1)}), bf16[8,2,8,32,128]{4,3,2,1,0:T(8,128)(2,1)S(1)}, u32[]{:S(2)}, u32[]{:S(2)}) async-start(bf16[8,2,8,32,128]{4,3,2,1,0:T(8,128)(2,1)} %get-tuple-element.57), calls=%async_computation.2 | async-start | bytes 2097152 | tf_op jit(solution)/shard_map/all_to_all | solution.py:362
  85.5 30.7 %all-to-all-start.3 = ((bf16[8,1024,128]{2,1,0:T(8,128)(2,1)}), bf16[8,1024,128]{2,1,0:T(8,128)(2,1)S(1)}, u32[]{:S(2)}, u32[]{:S(2)}) async-start(bf16[8,1024,128]{2,1,0:T(8,128)(2,1)} %get-tuple-element.67), calls=%async_computation.3 | async-start | bytes 4194304 | tf_op jit(solution)/shard_map/all_to_all | solution.py:362
  89.4 4.7 %collective-permute-start.5 = (bf16[128,128]{1,0:T(8,128)(2,1)S(1)}, bf16[128,128]{1,0:T(8,128)(2,1)S(1)}, u32[]{:S(2)}, u32[]{:S(2)}) collective-permute-start(bf16[128,128]{1,0:T(8,128)(2,1)S(1)} %get-tuple-element.59), channel_id=1, source_target_pairs={{0,2},{1,3},{2,0},{3,1},{4,6},{5,7},{6,4},{7,5},{8,10},{9,11},{10,... | collective-permute-start | bytes 98312 | tf_op jit(solution)/shard_map/ppermute | solution.py:358
  91.1 4.9 %collective-permute-start.6 = (bf16[128,128]{1,0:T(8,128)(2,1)S(1)}, bf16[128,128]{1,0:T(8,128)(2,1)S(1)}, u32[]{:S(2)}, u32[]{:S(2)}) collective-permute-start(bf16[128,128]{1,0:T(8,128)(2,1)S(1)} %get-tuple-element.60), channel_id=1, source_target_pairs={{0,4},{1,5},{2,6},{3,7},{4,0},{5,1},{6,2},{7,3},{8,12},{9,13},{10,... | collective-permute-start | bytes 98312 | tf_op jit(solution)/shard_map/ppermute | solution.py:358
  94.1 4.9 %collective-permute-start.7 = (bf16[128,128]{1,0:T(8,128)(2,1)S(1)}, bf16[128,128]{1,0:T(8,128)(2,1)S(1)}, u32[]{:S(2)}, u32[]{:S(2)}) collective-permute-start(bf16[128,128]{1,0:T(8,128)(2,1)S(1)} %get-tuple-element.61), channel_id=1, source_target_pairs={{0,6},{1,7},{2,4},{3,5},{4,2},{5,3},{6,0},{7,1},{8,14},{9,15},{10,... | collective-permute-start | bytes 98312 | tf_op jit(solution)/shard_map/ppermute | solution.py:358
  99.0 10.5 %collective-permute-start.10 = (bf16[32,128]{1,0:T(8,128)(2,1)S(1)}, bf16[32,128]{1,0:T(8,128)(2,1)S(1)}, u32[]{:S(2)}, u32[]{:S(2)}) collective-permute-start(bf16[32,128]{1,0:T(8,128)(2,1)S(1)} %get-tuple-element.65), channel_id=1, source_target_pairs={{0,24},{1,25},{2,26},{3,27},{4,28},{5,29},{6,30},{7,31},{8,16},{9,... | collective-permute-start | bytes 24584 | tf_op jit(solution)/shard_map/ppermute | solution.py:358
  105.9 6.4 %collective-permute-start.8 = (bf16[32,128]{1,0:T(8,128)(2,1)S(1)}, bf16[32,128]{1,0:T(8,128)(2,1)S(1)}, u32[]{:S(2)}, u32[]{:S(2)}) collective-permute-start(bf16[32,128]{1,0:T(8,128)(2,1)S(1)} %get-tuple-element.63), channel_id=1, source_target_pairs={{0,8},{1,9},{2,10},{3,11},{4,12},{5,13},{6,14},{7,15},{8,0},{9,1},... | collective-permute-start | bytes 24584 | tf_op jit(solution)/shard_map/ppermute | solution.py:358
  106.9 5.5 %collective-permute-start.9 = (bf16[32,128]{1,0:T(8,128)(2,1)S(1)}, bf16[32,128]{1,0:T(8,128)(2,1)S(1)}, u32[]{:S(2)}, u32[]{:S(2)}) collective-permute-start(bf16[32,128]{1,0:T(8,128)(2,1)S(1)} %get-tuple-element.64), channel_id=1, source_target_pairs={{0,16},{1,17},{2,18},{3,19},{4,20},{5,21},{6,22},{7,23},{8,24},{9,... | collective-permute-start | bytes 24584 | tf_op jit(solution)/shard_map/ppermute | solution.py:358
  112.4 5.5 %collective-permute-start.11 = (bf16[16,128]{1,0:T(8,128)(2,1)S(1)}, bf16[16,128]{1,0:T(8,128)(2,1)S(1)}, u32[]{:S(2)}, u32[]{:S(2)}) collective-permute-start(bf16[16,128]{1,0:T(8,128)(2,1)S(1)} %get-tuple-element.73), channel_id=1, source_target_pairs={{0,1},{1,0},{2,3},{3,2},{4,5},{5,4},{6,7},{7,6},{8,9},{9,8},{10,11... | collective-permute-start | bytes 12296 | tf_op jit(solution)/shard_map/ppermute | solution.py:358

commit v5 on v4

--- a/solution.py
+++ b/solution.py
@@ -264,7 +264,8 @@
 def regroup_kernel(*refs):
     x = jnp.concatenate([ref[...].astype(f32) for ref in refs[:-1]], axis=0)
     for k in range(8):
-        rows = [x[16 * i + 2 * k : 16 * i + 2 * k + 2] for i in range(16)]
+        blocks = [(i >> 3) | ((i & 7) << 1) for i in range(16)]
+        rows = [x[16 * i + 2 * k : 16 * i + 2 * k + 2] for i in blocks]
         rows = jnp.concatenate(rows, axis=0).astype(bf)
         for c in range(8):
             refs[-1][c, k] = rows
@@ -369,11 +370,11 @@
 ):
     copies, block = copies_of(resp_key[0], resp_value[0], pack_key, pack_value)
     own = exchange(copies)
-    for mask in (2, 4, 8):
+    for mask in (16, 2, 4):
         block = jnp.concatenate([block, from_partner(block, mask)], axis=0)
     block, q, g, o = lax.optimization_barrier((block, resp_query[0], resp_grad[0], resp_out[0]))
     qs, gs, delta = prepare(resp_length, q, g, o)
-    last, qs = lax.optimization_barrier((from_partner(block, 16), qs))
+    last, qs = lax.optimization_barrier((from_partner(block, 8), qs))
     mine = exchange(regroup(block, last))
     st = own_stats(qs, own)
     mine, st = lax.optimization_barrier((mine, st))

time: 120 us -> 139 us (1.16)
  starting transfers between devices: 49.3 us -> 68.3 us
    all_to_all x4, starting transfers between devices: 18.7 us -> 35.9 us  [exchange(): return lax.all_to_all(blocks, 'ctx', 0, 0, tiled=True)]
    ppermute x12, waiting for transfers between devices: 14.5 us -> 16.6 us  [from_partner(): return lax.ppermute(block, 'resp', [(i, i ^ mask) for i in range(32)])]
    all_to_all x4, waiting for transfers between devices: 9.37 us -> 7.42 us  [exchange(): return lax.all_to_all(blocks, 'ctx', 0, 0, tiled=True)]
    ppermute x12, starting transfers between devices: 30.7 us -> 32.4 us  [from_partner(): return lax.ppermute(block, 'resp', [(i, i ^ mask) for i in range(32)])]
  transfers between devices with their start and end apart: 16 -> 16, of which waited for: 12 -> 11; matrix products, arithmetic and copies ran while one was open for 0% -> 0% of each run, Pallas kernels for 24% -> 21%
where the time goes in v5:
time: 139 us; the launch traced here: 138 us
  starting transfers between devices  68.3 us (49%)
  Pallas kernels  42.4 us (31%)
  waiting for transfers between devices  24.1 us (17%)
  between operations  2 us (1%)
    all_to_all x4, starting transfers between devices, exchange(): return lax.all_to_all(blocks, 'ctx', 0, 0, tiled=True)  35.9 us
    ppermute x12, starting transfers between devices, from_partner(): return lax.ppermute(block, 'resp', [(i, i ^ mask) for i in range(32)])  32.4 us
    ppermute x12, waiting for transfers between devices, from_partner(): return lax.ppermute(block, 'resp', [(i, i ^ mask) for i in range(32)])  16.6 us
    pallas_call x1, Pallas kernels, own_grads(): pl.pallas_call(functools.partial(own_grads_kernel, CH), grid=(4,), in_spe...  13.4 us
    pallas_call x1, Pallas kernels, prefix(): pl.pallas_call(functools.partial(prefix_kernel, HP), grid=(4 // HP,), in_...  10.5 us
    pallas_call x1, Pallas kernels, own_stats(): pl.pallas_call(own_stats_kernel, grid=(4,), in_specs=[per_head(1024, 128)...  8.06 us
    all_to_all x4, waiting for transfers between devices, exchange(): return lax.all_to_all(blocks, 'ctx', 0, 0, tiled=True)  7.42 us
    pallas_call x1, Pallas kernels, prepare(): pl.pallas_call(prepare_kernel, grid=(4,), in_specs=[SMEM, wide(128), wide...  4.19 us
  transfers between devices with their start and end apart: 16, of which 11 were waited for; matrix products, arithmetic and copies ran while one was open for 0% of the time, Pallas kernels for 21%

profile of v5, /device:TPU:1, one launch (start us, length us, event | category | flops | bytes accessed | tf_op | source)
XLA Modules:
  0.0 137.6 jit_solution(1226231265306060666)
XLA Ops:
  0.6 3.0 %shard_map.172 = (bf16[8,1024,128]{2,1,0:T(8,128)(2,1)}, bf16[16,128]{1,0:T(8,128)(2,1)}) custom-call(bf16[128,512]{1,0:T(8,128)(2,1)} %bitcast.11, bf16[128,512]{1,0:T(8,128)(2,1)} %bitcast.12, bf16[2,512]{1,0:T(2,128)(2,1)} %pack_key_ref.1, bf16[2,512]{1,0:T(2,128)(2,1)} %pack_value_ref.1), custom_call_target="tpu_custom_call" | custom-call | bytes 2097152 | tf_op jit(solution)/shard_map/pallas_call | solution.py:253
  3.7 5.9 %all-to-all-start.1 = ((bf16[8,1024,128]{2,1,0:T(8,128)(2,1)}), bf16[8,1024,128]{2,1,0:T(8,128)(2,1)S(1)}, u32[]{:S(2)}, u32[]{:S(2)}) async-start(bf16[8,1024,128]{2,1,0:T(8,128)(2,1)} %get-tuple-element.51), calls=%async_computation.1 | async-start | bytes 4194304 | tf_op jit(solution)/shard_map/all_to_all | solution.py:363
  9.5 2.7 %collective-permute-start = (bf16[16,128]{1,0:T(8,128)(2,1)S(1)}, bf16[16,128]{1,0:T(8,128)(2,1)S(1)}, u32[]{:S(2)}, u32[]{:S(2)}) collective-permute-start(bf16[16,128]{1,0:T(8,128)(2,1)S(1)} %copy-done.2), channel_id=1, source_target_pairs={{0,16},{1,17},{2,18},{3,19},{4,20},{5,21},{6,22},{7,23},{8,24},{9,... | collective-permute-start | bytes 12296 | tf_op jit(solution)/shard_map/ppermute | solution.py:359
  12.3 5.9 %collective-permute-done = bf16[16,128]{1,0:T(8,128)(2,1)S(1)} collective-permute-done((bf16[16,128]{1,0:T(8,128)(2,1)S(1)}, bf16[16,128]{1,0:T(8,128)(2,1)S(1)}, u32[]{:S(2)}, u32[]{:S(2)}) %collective-permute-start) | collective-permute-done | bytes 4128 | tf_op jit(solution)/shard_map/ppermute | solution.py:359
  18.2 1.6 %collective-permute-start.1 = (bf16[32,128]{1,0:T(8,128)(2,1)S(1)}, bf16[32,128]{1,0:T(8,128)(2,1)S(1)}, u32[]{:S(2)}, u32[]{:S(2)}) collective-permute-start(bf16[32,128]{1,0:T(8,128)(2,1)S(1)} %pad_maximum_fusion.2), channel_id=1, source_target_pairs={{0,2},{1,3},{2,0},{3,1},{4,6},{5,7},{6,4},{7,5},{8,10},{9,11},{10,... | collective-permute-start | bytes 24584 | tf_op jit(solution)/shard_map/ppermute | solution.py:359
  21.1 3.0 %collective-permute-start.2 = (bf16[64,128]{1,0:T(8,128)(2,1)S(1)}, bf16[64,128]{1,0:T(8,128)(2,1)S(1)}, u32[]{:S(2)}, u32[]{:S(2)}) collective-permute-start(bf16[64,128]{1,0:T(8,128)(2,1)S(1)} %pad_maximum_fusion.1), channel_id=1, source_target_pairs={{0,4},{1,5},{2,6},{3,7},{4,0},{5,1},{6,2},{7,3},{8,12},{9,13},{10,... | collective-permute-start | bytes 49160 | tf_op jit(solution)/shard_map/ppermute | solution.py:359
  25.6 6.1 %collective-permute-start.3 = (bf16[128,128]{1,0:T(8,128)(2,1)S(1)}, bf16[128,128]{1,0:T(8,128)(2,1)S(1)}, u32[]{:S(2)}, u32[]{:S(2)}) collective-permute-start(bf16[128,128]{1,0:T(8,128)(2,1)S(1)} %pad_maximum_fusion.refs_0_), channel_id=1, source_target_pairs={{0,8},{1,9},{2,10},{3,11},{4,12},{5,13},{6,14},{7,15},{8,0},{9,1},... | collective-permute-start | bytes 98312 | tf_op jit(solution)/shard_map/ppermute | solution.py:359
  32.3 4.2 %shard_map.173 = (bf16[4,1024,128]{2,1,0:T(8,128)(2,1)}, bf16[4,1024,128]{2,1,0:T(8,128)(2,1)}, f32[4,8,1024]{2,1,0:T(8,128)}) custom-call(s32[1]{0:T(128)S(6)} %copy.19.len_ref, bf16[128,4096]{1,0:T(8,128)(2,1)} %bitcast.8, bf16[128,4096]{1,0:T(8,128)(2,1)} %bitcast.9, bf16[128,4096]{1,0:T(8,128)(2,1)} %bitcast.10), custom_call_target="tpu_custom_call" | custom-call | flops 100000000 | bytes 5242880 | tf_op jit(solution)/shard_map/pallas_call | solution.py:174
  37.4 21.6 %all-to-all-start = ((bf16[8,8,32,128]{3,2,1,0:T(8,128)(2,1)}), bf16[8,8,32,128]{3,2,1,0:T(8,128)(2,1)S(1)}, u32[]{:S(2)}, u32[]{:S(2)}) async-start(bf16[8,8,32,128]{3,2,1,0:T(8,128)(2,1)} %shard_map.174), calls=%async_computation | async-start | bytes 1048576 | tf_op jit(solution)/shard_map/all_to_all | solution.py:363
  58.9 8.1 %shard_map.175.st_ref = f32[4,16,1024]{2,1,0:T(8,128)} custom-call(bf16[4,1024,128]{2,1,0:T(8,128)(2,1)} %get-tuple-element.47.qs_ref, bf16[8,1024,128]{2,1,0:T(8,128)(2,1)} %copy-done), custom_call_target="tpu_custom_call" | custom-call | flops 1200000000 | bytes 6291456 | tf_op jit(solution)/shard_map/pallas_call | solution.py:186
  67.0 4.3 %collective-permute-start.4 = (bf16[8,8,32,128]{3,2,1,0:T(8,128)(2,1)S(1)}, bf16[8,8,32,128]{3,2,1,0:T(8,128)(2,1)S(1)}, u32[]{:S(2)}, u32[]{:S(2)}) collective-permute-start(bf16[8,8,32,128]{3,2,1,0:T(8,128)(2,1)S(1)} %all-to-all-done.km_ref), channel_id=1, source_target_pairs={{0,1},{1,0},{2,3},{3,2},{4,5},{5,4},{6,7},{7,6},{8,9},{9,8},{10,11... | collective-permute-start | bytes 1572872 | tf_op jit(solution)/shard_map/ppermute | solution.py:359
  73.6 10.5 %shard_map.176 = (bf16[8,2,8,32,128]{4,3,2,1,0:T(8,128)(2,1)}, f32[4,128,1024]{2,1,0:T(8,128)}, f32[4,8,1024]{2,1,0:T(8,128)}, bf16[2,4096]{1,0:T(2,128)(2,1)}) custom-call(s32[1]{0:T(128)S(6)} %copy.20.prompt_ref, s32[3]{0:T(128)} %offset_ref.1, bf16[4,1024,128]{2,1,0:T(8,128)(2,1)} %get-tuple-element.47.qs_ref, ...), custom_call_target="tpu_custom_call" | custom-call | flops 2700000000 | bytes 8388608 | tf_op jit(solution)/shard_map/pallas_call | solution.py:204
  84.1 4.9 %all-to-all-start.2 = ((bf16[8,2,8,32,128]{4,3,2,1,0:T(8,128)(2,1)}), bf16[8,2,8,32,128]{4,3,2,1,0:T(8,128)(2,1)S(1)}, u32[]{:S(2)}, u32[]{:S(2)}) async-start(bf16[8,2,8,32,128]{4,3,2,1,0:T(8,128)(2,1)} %get-tuple-element.57), calls=%async_computation.2 | async-start | bytes 2097152 | tf_op jit(solution)/shard_map/all_to_all | solution.py:363
  89.0 13.4 %shard_map.177 = (bf16[128,4096]{1,0:T(8,128)(2,1)}, bf16[8,1024,128]{2,1,0:T(8,128)(2,1)}) custom-call(bf16[4,1024,128]{2,1,0:T(8,128)(2,1)} %get-tuple-element.47.qs_ref, bf16[4,1024,128]{2,1,0:T(8,128)(2,1)} %get-tuple-element.48.gs_ref, f32[4,8,1024]{2,1,0:T(8,128)} %get-tuple-element.49.dl_ref, f32[4,8,1024]{2,1,0:T(8,128)} %get-tuple-element.54.lse_ref, ...), custom_call_target="tpu_custom_call" | custom-call | flops 5400000000 | bytes 10485760 | tf_op jit(solution)/shard_map/pallas_call | solution.py:218
  102.4 2.4 %all-to-all-done.2.parts_ref = bf16[8,2,8,32,128]{4,3,2,1,0:T(8,128)(2,1)S(1)} async-done(((bf16[8,2,8,32,128]{4,3,2,1,0:T(8,128)(2,1)}), bf16[8,2,8,32,128]{4,3,2,1,0:T(8,128)(2,1)S(1)}, u32[]{:S(2)}, u32[]{:S(2)}) %all-to-all-start.2) | async-done | bytes 1048608 | tf_op jit(solution)/shard_map/all_to_all | solution.py:363
  104.8 3.6 %all-to-all-start.3 = ((bf16[8,1024,128]{2,1,0:T(8,128)(2,1)}), bf16[8,1024,128]{2,1,0:T(8,128)(2,1)S(1)}, u32[]{:S(2)}, u32[]{:S(2)}) async-start(bf16[8,1024,128]{2,1,0:T(8,128)(2,1)} %get-tuple-element.67), calls=%async_computation.3 | async-start | bytes 4194304 | tf_op jit(solution)/shard_map/all_to_all | solution.py:363
  110.8 1.5 %collective-permute-start.7 = (bf16[128,128]{1,0:T(8,128)(2,1)S(1)}, bf16[128,128]{1,0:T(8,128)(2,1)S(1)}, u32[]{:S(2)}, u32[]{:S(2)}) collective-permute-start(bf16[128,128]{1,0:T(8,128)(2,1)S(1)} %get-tuple-element.61), channel_id=1, source_target_pairs={{0,6},{1,7},{2,4},{3,5},{4,2},{5,3},{6,0},{7,1},{8,14},{9,15},{10,... | collective-permute-start | bytes 98312 | tf_op jit(solution)/shard_map/ppermute | solution.py:359
  113.1 2.6 %collective-permute-done.7.refs_3_ = bf16[128,128]{1,0:T(8,128)(2,1)S(1)} collective-permute-done((bf16[128,128]{1,0:T(8,128)(2,1)S(1)}, bf16[128,128]{1,0:T(8,128)(2,1)S(1)}, u32[]{:S(2)}, u32[]{:S(2)}) %collective-permute-start.7) | collective-permute-done | bytes 32800 | tf_op jit(solution)/shard_map/ppermute | solution.py:359
  115.8 4.1 %collective-permute-start.10 = (bf16[32,128]{1,0:T(8,128)(2,1)S(1)}, bf16[32,128]{1,0:T(8,128)(2,1)S(1)}, u32[]{:S(2)}, u32[]{:S(2)}) collective-permute-start(bf16[32,128]{1,0:T(8,128)(2,1)S(1)} %get-tuple-element.65), channel_id=1, source_target_pairs={{0,24},{1,25},{2,26},{3,27},{4,28},{5,29},{6,30},{7,31},{8,16},{9,... | collective-permute-start | bytes 24584 | tf_op jit(solution)/shard_map/ppermute | solution.py:359
  119.9 2.7 %collective-permute-start.8 = (bf16[32,128]{1,0:T(8,128)(2,1)S(1)}, bf16[32,128]{1,0:T(8,128)(2,1)S(1)}, u32[]{:S(2)}, u32[]{:S(2)}) collective-permute-start(bf16[32,128]{1,0:T(8,128)(2,1)S(1)} %get-tuple-element.63), channel_id=1, source_target_pairs={{0,8},{1,9},{2,10},{3,11},{4,12},{5,13},{6,14},{7,15},{8,0},{9,1},... | collective-permute-start | bytes 24584 | tf_op jit(solution)/shard_map/ppermute | solution.py:359
  123.9 2.5 %collective-permute-done.10.d_ref = bf16[32,128]{1,0:T(8,128)(2,1)S(1)} collective-permute-done((bf16[32,128]{1,0:T(8,128)(2,1)S(1)}, bf16[32,128]{1,0:T(8,128)(2,1)S(1)}, u32[]{:S(2)}, u32[]{:S(2)}) %collective-permute-start.10) | collective-permute-done | bytes 8224 | tf_op jit(solution)/shard_map/ppermute | solution.py:359
  127.5 2.9 %collective-permute-start.11 = (bf16[16,128]{1,0:T(8,128)(2,1)S(1)}, bf16[16,128]{1,0:T(8,128)(2,1)S(1)}, u32[]{:S(2)}, u32[]{:S(2)}) collective-permute-start(bf16[16,128]{1,0:T(8,128)(2,1)S(1)} %get-tuple-element.73), channel_id=1, source_target_pairs={{0,1},{1,0},{2,3},{3,2},{4,5},{5,4},{6,7},{7,6},{8,9},{9,8},{10,11... | collective-permute-start | bytes 12296 | tf_op jit(solution)/shard_map/ppermute | solution.py:359
  130.4 5.0 %all-to-all-done.3.parts_ref = bf16[8,1024,128]{2,1,0:T(8,128)(2,1)S(1)} async-done(((bf16[8,1024,128]{2,1,0:T(8,128)(2,1)}), bf16[8,1024,128]{2,1,0:T(8,128)(2,1)S(1)}, u32[]{:S(2)}, u32[]{:S(2)}) %all-to-all-start.3) | async-done | bytes 2097184 | tf_op jit(solution)/shard_map/all_to_all | solution.py:363
  135.4 1.6 %shard_map.181 = (bf16[128,512]{1,0:T(8,128)(2,1)}, bf16[128,512]{1,0:T(8,128)(2,1)}) custom-call(bf16[8,1024,128]{2,1,0:T(8,128)(2,1)S(1)} %all-to-all-done.3.parts_ref), custom_call_target="tpu_custom_call" | custom-call | bytes 3145728 | tf_op jit(solution)/shard_map/pallas_call | solution.py:347
  (30 shorter events, 11.6 us)
Async XLA Ops:
  3.7 5.9 %copy-start.2 = (bf16[16,128]{1,0:T(8,128)(2,1)S(1)}, bf16[16,128]{1,0:T(8,128)(2,1)}, u32[]{:S(2)}) copy-start(bf16[16,128]{1,0:T(8,128)(2,1)} %get-tuple-element.41) | copy-start | bytes 12292
  3.7 33.7 %all-to-all-start.1 = ((bf16[8,1024,128]{2,1,0:T(8,128)(2,1)}), bf16[8,1024,128]{2,1,0:T(8,128)(2,1)S(1)}, u32[]{:S(2)}, u32[]{:S(2)}) async-start(bf16[8,1024,128]{2,1,0:T(8,128)(2,1)} %get-tuple-element.51), calls=%async_computation.1 | async-start | bytes 4194304 | tf_op jit(solution)/shard_map/all_to_all | solution.py:363
  9.5 8.6 %collective-permute-start = (bf16[16,128]{1,0:T(8,128)(2,1)S(1)}, bf16[16,128]{1,0:T(8,128)(2,1)S(1)}, u32[]{:S(2)}, u32[]{:S(2)}) collective-permute-start(bf16[16,128]{1,0:T(8,128)(2,1)S(1)} %copy-done.2), channel_id=1, source_target_pairs={{0,16},{1,17},{2,18},{3,19},{4,20},{5,21},{6,22},{7,23},{8,24},{9,... | collective-permute-start | bytes 12296 | tf_op jit(solution)/shard_map/ppermute | solution.py:359
  18.2 3.0 %collective-permute-start.1 = (bf16[32,128]{1,0:T(8,128)(2,1)S(1)}, bf16[32,128]{1,0:T(8,128)(2,1)S(1)}, u32[]{:S(2)}, u32[]{:S(2)}) collective-permute-start(bf16[32,128]{1,0:T(8,128)(2,1)S(1)} %pad_maximum_fusion.2), channel_id=1, source_target_pairs={{0,2},{1,3},{2,0},{3,1},{4,6},{5,7},{6,4},{7,5},{8,10},{9,11},{10,... | collective-permute-start | bytes 24584 | tf_op jit(solution)/shard_map/ppermute | solution.py:359
  21.1 4.4 %collective-permute-start.2 = (bf16[64,128]{1,0:T(8,128)(2,1)S(1)}, bf16[64,128]{1,0:T(8,128)(2,1)S(1)}, u32[]{:S(2)}, u32[]{:S(2)}) collective-permute-start(bf16[64,128]{1,0:T(8,128)(2,1)S(1)} %pad_maximum_fusion.1), channel_id=1, source_target_pairs={{0,4},{1,5},{2,6},{3,7},{4,0},{5,1},{6,2},{7,3},{8,12},{9,13},{10,... | collective-permute-start | bytes 49160 | tf_op jit(solution)/shard_map/ppermute | solution.py:359
  25.6 10.9 %collective-permute-start.3 = (bf16[128,128]{1,0:T(8,128)(2,1)S(1)}, bf16[128,128]{1,0:T(8,128)(2,1)S(1)}, u32[]{:S(2)}, u32[]{:S(2)}) collective-permute-start(bf16[128,128]{1,0:T(8,128)(2,1)S(1)} %pad_maximum_fusion.refs_0_), channel_id=1, source_target_pairs={{0,8},{1,9},{2,10},{3,11},{4,12},{5,13},{6,14},{7,15},{8,0},{9,1},... | collective-permute-start | bytes 98312 | tf_op jit(solution)/shard_map/ppermute | solution.py:359
  37.4 21.6 %copy-start = (bf16[8,1024,128]{2,1,0:T(8,128)(2,1)}, bf16[8,1024,128]{2,1,0:T(8,128)(2,1)S(1)}, u32[]{:S(2)}) copy-start(bf16[8,1024,128]{2,1,0:T(8,128)(2,1)S(1)} %all-to-all-done.1.k_ref.v_ref) | copy-start | bytes 6291460
  37.4 29.6 %all-to-all-start = ((bf16[8,8,32,128]{3,2,1,0:T(8,128)(2,1)}), bf16[8,8,32,128]{3,2,1,0:T(8,128)(2,1)S(1)}, u32[]{:S(2)}, u32[]{:S(2)}) async-start(bf16[8,8,32,128]{3,2,1,0:T(8,128)(2,1)} %shard_map.174), calls=%async_computation | async-start | bytes 1048576 | tf_op jit(solution)/shard_map/all_to_all | solution.py:363
  67.0 5.8 %copy-start.1 = (bf16[8,8,32,128]{3,2,1,0:T(8,128)(2,1)}, bf16[8,8,32,128]{3,2,1,0:T(8,128)(2,1)S(1)}, u32[]{:S(2)}) copy-start(bf16[8,8,32,128]{3,2,1,0:T(8,128)(2,1)S(1)} %all-to-all-done.km_ref) | copy-start | bytes 1572868
  67.0 5.8 %collective-permute-start.4 = (bf16[8,8,32,128]{3,2,1,0:T(8,128)(2,1)S(1)}, bf16[8,8,32,128]{3,2,1,0:T(8,128)(2,1)S(1)}, u32[]{:S(2)}, u32[]{:S(2)}) collective-permute-start(bf16[8,8,32,128]{3,2,1,0:T(8,128)(2,1)S(1)} %all-to-all-done.km_ref), channel_id=1, source_target_pairs={{0,1},{1,0},{2,3},{3,2},{4,5},{5,4},{6,7},{7,6},{8,9},{9,8},{10,11... | collective-permute-start | bytes 1572872 | tf_op jit(solution)/shard_map/ppermute | solution.py:359
  72.8 0.8 copy-start.3
  84.1 20.7 %all-to-all-start.2 = ((bf16[8,2,8,32,128]{4,3,2,1,0:T(8,128)(2,1)}), bf16[8,2,8,32,128]{4,3,2,1,0:T(8,128)(2,1)S(1)}, u32[]{:S(2)}, u32[]{:S(2)}) async-start(bf16[8,2,8,32,128]{4,3,2,1,0:T(8,128)(2,1)} %get-tuple-element.57), calls=%async_computation.2 | async-start | bytes 2097152 | tf_op jit(solution)/shard_map/all_to_all | solution.py:363
  104.8 30.6 %all-to-all-start.3 = ((bf16[8,1024,128]{2,1,0:T(8,128)(2,1)}), bf16[8,1024,128]{2,1,0:T(8,128)(2,1)S(1)}, u32[]{:S(2)}, u32[]{:S(2)}) async-start(bf16[8,1024,128]{2,1,0:T(8,128)(2,1)} %get-tuple-element.67), calls=%async_computation.3 | async-start | bytes 4194304 | tf_op jit(solution)/shard_map/all_to_all | solution.py:363
  108.6 3.6 %collective-permute-start.5 = (bf16[128,128]{1,0:T(8,128)(2,1)S(1)}, bf16[128,128]{1,0:T(8,128)(2,1)S(1)}, u32[]{:S(2)}, u32[]{:S(2)}) collective-permute-start(bf16[128,128]{1,0:T(8,128)(2,1)S(1)} %get-tuple-element.59), channel_id=1, source_target_pairs={{0,2},{1,3},{2,0},{3,1},{4,6},{5,7},{6,4},{7,5},{8,10},{9,11},{10,... | collective-permute-start | bytes 98312 | tf_op jit(solution)/shard_map/ppermute | solution.py:359
  109.5 3.7 %collective-permute-start.6 = (bf16[128,128]{1,0:T(8,128)(2,1)S(1)}, bf16[128,128]{1,0:T(8,128)(2,1)S(1)}, u32[]{:S(2)}, u32[]{:S(2)}) collective-permute-start(bf16[128,128]{1,0:T(8,128)(2,1)S(1)} %get-tuple-element.60), channel_id=1, source_target_pairs={{0,4},{1,5},{2,6},{3,7},{4,0},{5,1},{6,2},{7,3},{8,12},{9,13},{10,... | collective-permute-start | bytes 98312 | tf_op jit(solution)/shard_map/ppermute | solution.py:359
  110.8 5.0 %collective-permute-start.7 = (bf16[128,128]{1,0:T(8,128)(2,1)S(1)}, bf16[128,128]{1,0:T(8,128)(2,1)S(1)}, u32[]{:S(2)}, u32[]{:S(2)}) collective-permute-start(bf16[128,128]{1,0:T(8,128)(2,1)S(1)} %get-tuple-element.61), channel_id=1, source_target_pairs={{0,6},{1,7},{2,4},{3,5},{4,2},{5,3},{6,0},{7,1},{8,14},{9,15},{10,... | collective-permute-start | bytes 98312 | tf_op jit(solution)/shard_map/ppermute | solution.py:359
  115.8 10.7 %collective-permute-start.10 = (bf16[32,128]{1,0:T(8,128)(2,1)S(1)}, bf16[32,128]{1,0:T(8,128)(2,1)S(1)}, u32[]{:S(2)}, u32[]{:S(2)}) collective-permute-start(bf16[32,128]{1,0:T(8,128)(2,1)S(1)} %get-tuple-element.65), channel_id=1, source_target_pairs={{0,24},{1,25},{2,26},{3,27},{4,28},{5,29},{6,30},{7,31},{8,16},{9,... | collective-permute-start | bytes 24584 | tf_op jit(solution)/shard_map/ppermute | solution.py:359
  119.9 6.7 %collective-permute-start.8 = (bf16[32,128]{1,0:T(8,128)(2,1)S(1)}, bf16[32,128]{1,0:T(8,128)(2,1)S(1)}, u32[]{:S(2)}, u32[]{:S(2)}) collective-permute-start(bf16[32,128]{1,0:T(8,128)(2,1)S(1)} %get-tuple-element.63), channel_id=1, source_target_pairs={{0,8},{1,9},{2,10},{3,11},{4,12},{5,13},{6,14},{7,15},{8,0},{9,1},... | collective-permute-start | bytes 24584 | tf_op jit(solution)/shard_map/ppermute | solution.py:359
  122.5 5.0 %collective-permute-start.9 = (bf16[32,128]{1,0:T(8,128)(2,1)S(1)}, bf16[32,128]{1,0:T(8,128)(2,1)S(1)}, u32[]{:S(2)}, u32[]{:S(2)}) collective-permute-start(bf16[32,128]{1,0:T(8,128)(2,1)S(1)} %get-tuple-element.64), channel_id=1, source_target_pairs={{0,16},{1,17},{2,18},{3,19},{4,20},{5,21},{6,22},{7,23},{8,24},{9,... | collective-permute-start | bytes 24584 | tf_op jit(solution)/shard_map/ppermute | solution.py:359
  127.5 9.5 %collective-permute-start.11 = (bf16[16,128]{1,0:T(8,128)(2,1)S(1)}, bf16[16,128]{1,0:T(8,128)(2,1)S(1)}, u32[]{:S(2)}, u32[]{:S(2)}) collective-permute-start(bf16[16,128]{1,0:T(8,128)(2,1)S(1)} %get-tuple-element.73), channel_id=1, source_target_pairs={{0,1},{1,0},{2,3},{3,2},{4,5},{5,4},{6,7},{7,6},{8,9},{9,8},{10,11... | collective-permute-start | bytes 12296 | tf_op jit(solution)/shard_map/ppermute | solution.py:359
